TPU v7x, 32 devices: a whole 2x2x4 slice. The times are simulated.
32 devices in a mesh: chan: 8 (over y, x, core), tm: 4 (over z).
Axes of the slice: x: 2, y: 2, z: 4, core: 2. Of those that a mesh axis runs over, the one named last changes fastest.
Arguments:
- spectra: bfloat16 [256, 2, 250, 2048], P('tm', None, None, 'chan'), may hold values from -6 to 6
- src_blocks: int32 [2], replicated, may hold values from 0 to 31
- valid: int32 [256], P('tm'), may hold values 0 or 1
Outputs:
- stacked: bfloat16 [128, 101, 2048], P('tm', None, 'chan')
All inputs are finite; a program needn't handle non-finite values. No bound on the sum of `valid` on one device may be relied on, other than what follows from the above.
Results may differ from a plain program's by a relative error of at most 0.013.
Values may be sent and summed in bfloat16 or wider, within the bound.
A program may use at most 192 MiB of HBM per device.

v0:
```python
import jax
import jax.numpy as jnp
from jax import lax
from jax.sharding import PartitionSpec as P

LAGS = 101
SRC_BLK = 64


def from_root(x, axis, root):
    mine = lax.axis_index(axis) == root
    return lax.psum(jnp.where(mine, x, jnp.zeros_like(x)), axis)


def lag_table(bin_count, lag_count, segment_total):
    bins_idx = jnp.arange(bin_count, dtype=jnp.int32) + 1
    lag_steps = jnp.arange(lag_count, dtype=jnp.int32) - (lag_count - 1) // 2
    phase_int = lag_steps[:, None] * bins_idx[None, :] % (2 * bin_count)
    phase = phase_int.astype(jnp.float32) * (2.0 * jnp.pi / (2.0 * bin_count))
    scale = 1.0 / jnp.sqrt(jnp.float32(segment_total * bin_count))
    return jnp.stack([jnp.cos(phase) * scale, -jnp.sin(phase) * scale]).astype(jnp.bfloat16)


def cross_spectra(source, spectra):
    rotated = jnp.concatenate([spectra[:, 1:2], -spectra[:, 0:1]], axis=1)
    real_part = jnp.einsum("scfk,scfr->fkr", source, spectra, preferred_element_type=jnp.float32)
    imag_part = jnp.einsum("scfk,scfr->fkr", source, rotated, preferred_element_type=jnp.float32)
    return jnp.stack([real_part, imag_part]).astype(jnp.bfloat16)


def to_lags(table, cross):
    return jnp.einsum("plf,pfkr->klr", table, cross, preferred_element_type=jnp.float32)


def fetch_block(window, owner):
    return from_root(window, "chan", owner)


def body(spectra, src_blocks, valid):
    seg_count, _, bin_count, chan_width = spectra.shape
    tm_count = lax.axis_size("tm")
    chan_index = lax.axis_index("chan")
    keep_mask = valid.astype(jnp.bfloat16)[:, None, None, None]
    starts = src_blocks * SRC_BLK
    owners = starts // chan_width
    windows = []
    for block in range(2):
        offset = jnp.clip(starts[block] - chan_index * chan_width, 0, chan_width - SRC_BLK)
        windows.append(lax.dynamic_slice_in_dim(spectra, offset, SRC_BLK, 3))
    sources = [fetch_block(windows[block], owners[block]) for block in range(2)]
    table = lag_table(bin_count, LAGS, seg_count * tm_count)
    pieces = [
        to_lags(table, cross_spectra(sources[block] * keep_mask, spectra)) for block in range(2)
    ]
    partial_value = jnp.concatenate(pieces, axis=0)
    row_count = partial_value.shape[0] // tm_count
    total = lax.psum(partial_value.astype(jnp.bfloat16), "tm").astype(jnp.float32)
    own_rows = lax.dynamic_slice_in_dim(total, lax.axis_index("tm") * row_count, row_count, 0)
    return own_rows.astype(jnp.bfloat16)


def solution(mesh):
    placed = (P("tm", None, None, "chan"), P(), P("tm"))
    return jax.shard_map(
        body, mesh=mesh, in_specs=placed, out_specs=P("tm", None, "chan"), check_vma=False
    )
```

profile of v0, /device:TPU:8, one launch (start us, length us, event | category | flops | bytes accessed | tf_op | source)
XLA Modules:
  0.0 601.2 jit_solution(1878756861856491891)
XLA Ops:
  6.5 0.0 all-reduce.6.cloned.1.call-start
  6.5 0.7 and_select_fusion
  7.2 0.6 fusion.30
  9.1 24.8 %constant_dynamic-slice_fusion.1 = (bf16[64,2,250,64]{3,1,2,0:T(2,128)(2,1)}, bf16[64,2,250,64]{3,1,2,0:T(2,128)(2,1)}) fusion(bf16[64,2,250,256]{3,1,2,0:T(2,128)(2,1)} %param.3, s32[]{:T(128)S(6)} %min.7, s32[]{:T(128)S(6)} %min.8), kind=kLoop, calls=%fused_computation.46 | loop fusion | bytes 16384008 | tf_op jit(solution)/shard_map/dynamic_slice | solution.py:49
  33.9 17.2 %copy.35 = bf16[64,2,250,64]{2,3,1,0:T(8,128)(2,1)} copy(bf16[64,2,250,64]{3,1,2,0:T(2,128)(2,1)} %get-tuple-element.9) | data formatting | bytes 8192000
  51.8 17.3 %copy.36 = bf16[64,2,250,64]{2,3,1,0:T(8,128)(2,1)} copy(bf16[64,2,250,64]{3,1,2,0:T(2,128)(2,1)} %get-tuple-element.10) | data formatting | bytes 8192000
  69.6 0.0 copy-start
  69.6 2.4 broadcast_select_fusion.1
  72.0 1.3 copy-done
  73.3 2.3 broadcast_select_fusion
  75.6 0.0 all-reduce.6.cloned.1.call-update
  75.6 0.0 copy-start.1
  75.6 0.2 all-reduce.4.cloned.1.call-start
  75.9 11.3 %copy.17 = bf16[64,2,250,256]{3,0,1,2:T(8,128)(2,1)S(1)} copy(bf16[64,2,250,256]{3,1,2,0:T(2,128)(2,1)} %param.3) | data formatting | bytes 32768000 | tf_op args[0]
  87.2 0.0 copy-done.1
  87.3 0.5 multiply_convert_fusion.1
  87.8 6.0 %fusion.29 = (bf16[64,1,250,256]{3,0,1,2:T(8,128)(2,1)}, bf16[64,1,250,256]{3,0,1,2:T(8,128)(2,1)}) fusion(bf16[64,2,250,256]{3,0,1,2:T(8,128)(2,1)S(1)} %copy.17), kind=kLoop, calls=%fused_computation.55 | loop fusion | flops 4096000 | bytes 32768000 | tf_op jit(solution)/shard_map/slice | solution.py:25
  93.8 111.0 %all-reduce.6.cloned.1.call-done = (bf16[64,2,250,64]{2,3,1,0:T(8,128)(2,1)}, bf16[64,2,250,64]{2,3,1,0:T(8,128)(2,1)}) async-done(((bf16[64,2,250,64]{2,3,1,0:T(8,128)(2,1)}, bf16[64,2,250,64]{2,3,1,0:T(8,128)(2,1)}), (bf16[64,2,250,64]{2,3,1,0:T(8,128)(2,1)}, bf16[64,2,250,64]{2,3,1,0:T(8,128)(2,1)})) %all-reduce.6.cloned.1.call-update) | async-done | bytes 8192016 | tf_op jit(solution)/shard_map/psum | solution.py:12
  204.8 5.9 broadcast_multiply_fusion.1
  210.7 14.3 %copy.16 = bf16[64,2,250,64]{0,3,1,2:T(8,128)(2,1)} copy(bf16[64,2,250,64]{2,3,1,0:T(8,128)(2,1)} %get-tuple-element.13) | data formatting | bytes 8192000 | tf_op jit(solution)/shard_map/mul | solution.py:53
  225.0 13.0 %fusion.8 = bf16[1,250,64,256]{3,2,1,0:T(8,128)(2,1)} fusion(bf16[64,2,250,64]{0,3,1,2:T(8,128)(2,1)} %copy.16, bf16[64,2,250,256]{3,1,2,0:T(2,128)(2,1)} %param.3), kind=kOutput, calls=%fused_computation.19 | convolution fusion | flops 1052672000 | bytes 28672000 | tf_op jit(solution)/shard_map/scfk,scfr->fkr/dot_general | solution.py:26
  238.0 14.3 %copy.24 = bf16[64,2,250,64]{0,3,1,2:T(8,128)(2,1)} copy(bf16[64,2,250,64]{2,3,1,0:T(8,128)(2,1)} %get-tuple-element.14) | data formatting | bytes 8192000 | tf_op jit(solution)/shard_map/mul | solution.py:53
  252.3 12.3 %fusion.6 = bf16[1,250,64,256]{3,2,1,0:T(8,128)(2,1)} fusion(bf16[64,2,250,64]{0,3,1,2:T(8,128)(2,1)} %copy.16, bf16[64,1,250,256]{3,0,1,2:T(8,128)(2,1)} %get-tuple-element.8, bf16[64,1,250,256]{3,0,1,2:T(8,128)(2,1)} %get-tuple-element.7), kind=kOutput, calls=%fused_computation.13 | convolution fusion | flops 1060864000 | bytes 28672000 | tf_op jit(solution)/shard_map/scfk,scfr->fkr/dot_general | solution.py:27
  264.6 12.4 %fusion.7 = bf16[1,250,64,256]{3,2,1,0:T(8,128)(2,1)} fusion(bf16[64,2,250,64]{0,3,1,2:T(8,128)(2,1)} %copy.24, bf16[64,1,250,256]{3,0,1,2:T(8,128)(2,1)} %get-tuple-element.8, bf16[64,1,250,256]{3,0,1,2:T(8,128)(2,1)} %get-tuple-element.7), kind=kOutput, calls=%fused_computation.14 | convolution fusion | flops 1060864000 | bytes 28672000 | tf_op jit(solution)/shard_map/scfk,scfr->fkr/dot_general | solution.py:27
  277.0 13.4 %fusion.9 = bf16[1,250,64,256]{3,2,1,0:T(8,128)(2,1)} fusion(bf16[64,2,250,64]{0,3,1,2:T(8,128)(2,1)} %copy.24, bf16[64,2,250,256]{3,1,2,0:T(2,128)(2,1)} %param.3), kind=kOutput, calls=%fused_computation.20 | convolution fusion | flops 1052672000 | bytes 28672000 | tf_op jit(solution)/shard_map/scfk,scfr->fkr/dot_general | solution.py:26
  290.4 0.0 slice-start
  290.4 14.0 %pad_maximum_fusion.1 = bf16[2,250,64,256]{3,2,1,0:T(8,128)(2,1)} fusion(bf16[1,250,64,256]{3,2,1,0:T(8,128)(2,1)} %fusion.6, bf16[1,250,64,256]{3,2,1,0:T(8,128)(2,1)} %fusion.8), kind=kLoop, calls=%fused_computation.5 | loop fusion | flops 8192000 | bytes 32768000 | tf_op jit(solution)/shard_map/stack | solution.py:28
  304.4 0.0 slice-start.1
  304.4 17.9 %fusion.12 = bf16[64,256,101]{1,2,0:T(8,128)(2,1)} fusion(bf16[2,250,64,256]{3,2,1,0:T(8,128)(2,1)} %pad_maximum_fusion.1, bf16[1,101,250]{2,1,0:T(8,128)(2,1)S(1)} %get-tuple-element.12, bf16[1,101,250]{2,1,0:T(8,128)(2,1)S(1)} %get-tuple-element.11), kind=kOutput, calls=%fused_computation.26 | convolution fusion | flops 1654834560 | bytes 19794568 | tf_op jit(solution)/shard_map/plf,pfkr->klr/dot_general | solution.py:32
  322.3 2.7 copy.55
  325.0 0.0 slice-done
  325.0 0.0 slice-done.1
  325.1 10.8 %pad_maximum_fusion.2 = bf16[2,250,64,256]{3,2,1,0:T(8,128)(2,1)} fusion(bf16[1,250,64,256]{3,2,1,0:T(8,128)(2,1)} %fusion.7, bf16[1,250,64,256]{3,2,1,0:T(8,128)(2,1)S(1)} %bitcast.53), kind=kLoop, calls=%fused_computation.6 | loop fusion | flops 8192000 | bytes 32768000 | tf_op jit(solution)/shard_map/stack | solution.py:28
  335.9 17.6 %fusion.15 = bf16[64,256,101]{1,2,0:T(8,128)(2,1)} fusion(bf16[2,250,64,256]{3,2,1,0:T(8,128)(2,1)} %pad_maximum_fusion.2, bf16[1,101,250]{2,1,0:T(8,128)(2,1)S(1)} %get-tuple-element.12, bf16[1,101,250]{2,1,0:T(8,128)(2,1)S(1)} %get-tuple-element.11), kind=kOutput, calls=%fused_computation.27 | convolution fusion | flops 1654834560 | bytes 19794568 | tf_op jit(solution)/shard_map/plf,pfkr->klr/dot_general | solution.py:32
  353.5 2.7 copy.56
  356.2 3.6 pad_maximum_fusion.9
  359.8 0.0 all-reduce.4.cloned.1.call-update
  359.9 231.5 %all-reduce.4.cloned.1.call-done = bf16[128,101,256]{2,0,1:T(8,128)(2,1)} async-done(((bf16[128,101,256]{2,0,1:T(8,128)(2,1)}), bf16[128,101,256]{2,0,1:T(8,128)(2,1)}) %all-reduce.4.cloned.1.call-update) | async-done | bytes 6619152 | tf_op jit(solution)/shard_map/psum | solution.py:57
  591.4 2.7 convert_convert_fusion
  (4 shorter events, 0.0 us)
Async XLA Ops:
  6.5 198.3 %all-reduce.6.cloned.1.call-start = ((), (), s32[]{:S(2)}) async-start(), calls=%async_computation.1 | async-start | bytes 16777216 | tf_op jit(solution)/shard_map/psum | solution.py:12
  69.6 3.7 copy-start
  75.6 11.6 %copy-start.1 = (s32[64]{0:T(128)S(1)}, s32[64]{0:T(128)}, u32[]{:S(2)}) copy-start(s32[64]{0:T(128)} %param.5) | copy-start | bytes 772
  75.6 515.8 %all-reduce.4.cloned.1.call-start = ((), (), s32[]{:S(2)}) async-start(), calls=%async_computation | async-start | bytes 13238272 | tf_op jit(solution)/shard_map/psum | solution.py:57
  290.4 34.7 %slice-start = ((s8[8192000]{0:T(1024)(128)(4,1)}), s8[4194304]{0:T(1024)(128)(4,1)S(1)}, s32[]{:S(2)}) async-start(s8[8192000]{0:T(1024)(128)(4,1)} %bitcast.52), calls=%async_computation.2 | async-start | bytes 8388608
  304.4 20.6 %slice-start.1 = ((s8[8192000]{0:T(1024)(128)(4,1)}), s8[3997696]{0:T(1024)(128)(4,1)S(1)}, s32[]{:S(2)}) async-start(s8[8192000]{0:T(1024)(128)(4,1)} %bitcast.52), calls=%async_computation.3 | async-start | bytes 7995392
Sparse Core Ops, SparseCore 0:
  75.7 129.0 all-reduce.5
  360.0 231.3 all-reduce.3
where the time goes:
time: 609 us; the launch traced here: 601 us
  waiting for transfers between devices  343 us (56%)
  local copies, waits for them, and re-layouts  107 us (18%)
  matrix products  86.6 us (14%)
  other arithmetic  49 us (8%)
  between operations  16.2 us (3%)
    psum x1, waiting for transfers between devices, body(): lax.psum(partial_value.astype(jnp.bfloat16), 'tm').astype(jnp.float32)  232 us
    psum x1, waiting for transfers between devices, from_root(): return lax.psum(jnp.where(mine, x, jnp.zeros_like(x)), axis)  111 us
    unnamed x11, local copies, waits for them, and re-layouts  47.1 us
    dot_general x2, matrix products, to_lags(): jnp.einsum('plf,pfkr->klr', table, cross, preferred_element_type=jnp.floa...  35.5 us
    mul x2, local copies, waits for them, and re-layouts, body(): sources[block] * keep_mask  28.6 us
    dot_general x2, matrix products, cross_spectra(): jnp.einsum('scfk,scfr->fkr', source, spectra, preferred_element_type=jnp....  26.4 us
    another operation x2, other arithmetic, cross_spectra(): return jnp.stack([real_part, imag_part]).astype(jnp.bfloat16)  24.8 us
    dynamic_slice x1, local copies, waits for them, and re-layouts, body(): windows.append(lax.dynamic_slice_in_dim(spectra, offset, SRC_BLK, 3))  24.8 us
  transfers between devices with their start and end apart: 2, of which 2 were waited for; matrix products, arithmetic and copies ran while one was open for 3% of the time, Pallas kernels for 0%

commit v1 on v0

v1 whole, which is shorter than its diff:
```python
import functools

import jax
import jax.numpy as jnp
from jax import lax
from jax.experimental import pallas as pl
from jax.experimental.pallas import tpu as pltpu
from jax.sharding import PartitionSpec as P

LAGS = 101
SRC_BLK = 64
CHUNKS = 4
MIB = 1024 * 1024


def lag_table(bin_count, lag_count, segment_total):
    bins_idx = jnp.arange(bin_count, dtype=jnp.int32) + 1
    lag_steps = jnp.arange(lag_count, dtype=jnp.int32) - (lag_count - 1) // 2
    phase_int = lag_steps[:, None] * bins_idx[None, :] % (2 * bin_count)
    phase = phase_int.astype(jnp.float32) * (2.0 * jnp.pi / (2.0 * bin_count))
    scale = 1.0 / jnp.sqrt(jnp.float32(segment_total * bin_count))
    return jnp.stack([jnp.cos(phase) * scale, -jnp.sin(phase) * scale]).astype(jnp.bfloat16)


def pick_kernel(pick_ref, keep_ref, x_ref, out_ref):
    chunks, bins, rows, depth = out_ref.shape
    for f in range(bins):
        picked = lax.dot_general(
            pick_ref[...], x_ref[f], (((1,), (1,)), ((), ())), preferred_element_type=jnp.float32
        )
        picked = (picked * keep_ref[...]).astype(jnp.bfloat16)
        for j in range(chunks):
            out_ref[j, f] = picked[j * rows:(j + 1) * rows]


def pick_sources(pick, keep, x, bins):
    bin_count, depth, width = x.shape
    rows = pick.shape[0] // CHUNKS
    return pl.pallas_call(
        pick_kernel,
        grid=(bin_count // bins,),
        in_specs=[
            pl.BlockSpec(pick.shape, lambda i: (0, 0)),
            pl.BlockSpec(keep.shape, lambda i: (0, 0)),
            pl.BlockSpec((bins, depth, width), lambda i: (i, 0, 0)),
        ],
        out_specs=pl.BlockSpec((CHUNKS, bins, rows, depth), lambda i: (0, i, 0, 0)),
        out_shape=jax.ShapeDtypeStruct((CHUNKS, bin_count, rows, depth), jnp.bfloat16),
        compiler_params=pltpu.CompilerParams(vmem_limit_bytes=32 * MIB),
        cost_estimate=pl.CostEstimate(
            flops=2 * bin_count * pick.shape[0] * width * depth,
            bytes_accessed=2 * bin_count * depth * (width + pick.shape[0]),
            transcendentals=0,
        ),
    )(pick, keep, x)


def correlate_kernel(stride, bin_count, sign_ref, table_ref, source_ref, x_ref, out_ref, cross):
    bins, rows, depth = source_ref.shape
    width = x_ref.shape[2]
    halves = width // 128
    step = pl.program_id(0)
    sign = sign_ref[...]
    for i in range(bins):
        f = step * bins + i
        real = source_ref[i]
        half = depth // 2
        imag = jnp.concatenate([real[:, half:], real[:, :half]], axis=1) * sign
        both = jnp.concatenate([real, imag], axis=0)
        product = jnp.dot(both, x_ref[i], preferred_element_type=jnp.float32)
        for part in range(2):
            for h in range(halves):
                cross[h, pl.ds(part * bin_count + f, rows, stride=stride), :] = product[
                    part * rows:(part + 1) * rows, h * 128:(h + 1) * 128
                ]

    @pl.when(step == pl.num_programs(0) - 1)
    def _():
        lags = out_ref.shape[1]

        def one_row(k, carry):
            at = pl.multiple_of(k * stride, 8)
            block = jnp.concatenate(
                [cross[h, pl.ds(at, 2 * bin_count), :].astype(jnp.bfloat16) for h in range(halves)], axis=1
            )
            lagged = jnp.dot(table_ref[...], block, preferred_element_type=jnp.float32)
            out_ref[k] = lagged[:lags].astype(jnp.bfloat16)
            return carry

        lax.fori_loop(0, rows, one_row, 0, unroll=4)


def correlate(sign, table, sources, x, chunk, bins):
    _, bin_count, rows, depth = sources.shape
    width = x.shape[2]
    stride = -(-2 * bin_count // 8) * 8
    return pl.pallas_call(
        functools.partial(correlate_kernel, stride, bin_count),
        grid=(bin_count // bins,),
        in_specs=[
            pl.BlockSpec(sign.shape, lambda i: (0, 0)),
            pl.BlockSpec(table.shape, lambda i: (0, 0)),
            pl.BlockSpec((None, bins, rows, depth), lambda i: (chunk, i, 0, 0)),
            pl.BlockSpec((bins, depth, width), lambda i: (i, 0, 0)),
        ],
        out_specs=pl.BlockSpec((rows, LAGS, width), lambda i: (0, 0, 0)),
        out_shape=jax.ShapeDtypeStruct((rows, LAGS, width), jnp.bfloat16),
        scratch_shapes=[pltpu.VMEM((width // 128, rows * stride, 128), jnp.float32)],
        compiler_params=pltpu.CompilerParams(vmem_limit_bytes=48 * MIB),
        cost_estimate=pl.CostEstimate(
            flops=2 * bin_count * 2 * rows * depth * width + 2 * 2 * bin_count * rows * LAGS * width,
            bytes_accessed=2 * bin_count * depth * (width + rows) + 2 * rows * LAGS * width,
            transcendentals=0,
        ),
    )(sign, table, sources, x)


def body(spectra, src_blocks, valid):
    seg_count, _, bin_count, width = spectra.shape
    tm_count = lax.axis_size("tm")
    chan_index = lax.axis_index("chan")
    depth = 2 * seg_count
    sources_all = 2 * SRC_BLK
    per_dev = sources_all // tm_count
    sub = per_dev // CHUNKS

    order = jnp.arange(sources_all, dtype=jnp.int32).reshape(tm_count, CHUNKS, sub)
    order = order.transpose(1, 0, 2).reshape(sources_all)
    channel = src_blocks[order // SRC_BLK] * SRC_BLK + order % SRC_BLK - chan_index * width
    pick = (channel[:, None] == jnp.arange(width, dtype=jnp.int32)[None, :]).astype(jnp.bfloat16)
    keep = jnp.tile(valid.astype(jnp.float32), 2)[None, :]
    sign = jnp.where(jnp.arange(depth) < seg_count, -1.0, 1.0).astype(jnp.bfloat16)[None, :]
    table = lag_table(bin_count, LAGS, seg_count * tm_count)
    table = table.transpose(1, 0, 2).reshape(LAGS, 2 * bin_count)
    table = jnp.pad(table, ((0, -LAGS % 16), (0, 0)))

    x = spectra.transpose(2, 1, 0, 3).reshape(bin_count, depth, width)
    mine = pick_sources(pick, keep, x, 10)
    pieces = []
    for chunk in range(CHUNKS):
        source = lax.psum(mine[chunk], "chan")
        partial_value = correlate(sign, table, source[None], x, 0, 25)
        pieces.append(lax.psum_scatter(partial_value, "tm", scatter_dimension=0, tiled=True))
    return jnp.concatenate(pieces, axis=0)


def solution(mesh):
    placed = (P("tm", None, None, "chan"), P(), P("tm"))
    return jax.shard_map(
        body, mesh=mesh, in_specs=placed, out_specs=P("tm", None, "chan"), check_vma=False
    )
```

time: 609 us -> 358 us (0.59)
  waiting for transfers between devices: 343 us -> 230 us
  matrix products: 86.6 us -> 0 us
  local copies, waits for them, and re-layouts: 107 us -> 25.9 us
  Pallas kernels: 0 us -> 77.3 us
  other arithmetic: 49 us -> 7.37 us
    psum x2 -> x1, waiting for transfers between devices: 343 us -> 123 us  [body(): source = lax.psum(mine[chunk], 'chan')]
    reduce_scatter x0 -> x4, waiting for transfers between devices: none -> 107 us  [body(): lax.psum_scatter(partial_value, 'tm', scatter_dimension=0, tiled=True)]
    dot_general x6 -> x0, matrix products: 86.6 us -> none  [the longest x2 35.5 us: to_lags(): jnp.einsum('plf,pfkr->klr', table, cross, preferred_element_type=jnp.floa...]
    pallas_call x0 -> x5, Pallas kernels: none -> 77.3 us  [the longest x4 58.3 us: correlate(): pl.pallas_call(functools.partial(correlate_kernel, stride, bin_count), gr...]
    unnamed x11 -> x12, local copies, waits for them, and re-layouts: 47.1 us -> 3.16 us
    mul x2 -> x0, local copies, waits for them, and re-layouts: 28.6 us -> none  [body(): sources[block] * keep_mask]
    dynamic_slice x1 -> x0, local copies, waits for them, and re-layouts: 24.8 us -> none  [body(): windows.append(lax.dynamic_slice_in_dim(spectra, offset, SRC_BLK, 3))]
    another operation x3 -> x1, other arithmetic: 25.4 us -> 4.05 us  [the longest x2 24.8 us: cross_spectra(): return jnp.stack([real_part, imag_part]).astype(jnp.bfloat16)]
  transfers between devices with their start and end apart: 2 -> 5, of which waited for: 2 -> 4; matrix products, arithmetic and copies ran while one was open for 3% -> 1% of each run, Pallas kernels for 0% -> 12%
where the time goes in v1:
time: 358 us; the launch traced here: 354 us
  waiting for transfers between devices  230 us (64%)
  Pallas kernels  77.3 us (22%)
  local copies, waits for them, and re-layouts  25.9 us (7%)
  between operations  13.3 us (4%)
  other arithmetic  7.37 us (2%)
    psum x1, waiting for transfers between devices, body(): source = lax.psum(mine[chunk], 'chan')  123 us
    reduce_scatter x4, waiting for transfers between devices, body(): lax.psum_scatter(partial_value, 'tm', scatter_dimension=0, tiled=True)  107 us
    pallas_call x4, Pallas kernels, correlate(): pl.pallas_call(functools.partial(correlate_kernel, stride, bin_count), gr...  58.3 us
    pallas_call x1, Pallas kernels, pick_sources(): pl.pallas_call(pick_kernel, grid=(bin_count // bins,), in_specs=[pl.Block...  19 us
    transpose x1, local copies, waits for them, and re-layouts, body(): x = spectra.transpose(2, 1, 0, 3).reshape(bin_count, depth, width)  16.6 us
  transfers between devices with their start and end apart: 5, of which 4 were waited for; matrix products, arithmetic and copies ran while one was open for 1% of the time, Pallas kernels for 12%

profile of v1, /device:TPU:8, one launch (start us, length us, event | category | flops | bytes accessed | tf_op | source)
XLA Modules:
  0.0 354.1 jit_solution(5641363413223733883)
XLA Ops:
  6.5 0.0 all-reduce.4.cloned.1.call-start
  6.5 0.1 reshape.310
  6.6 0.1 reshape.311
  6.7 0.0 copy-start.4
  6.8 0.0 copy-start.5
  6.8 16.6 %copy.4 = bf16[250,2,64,256]{3,2,1,0:T(8,128)(2,1)} copy(bf16[250,2,64,256]{3,1,0,2:T(2,128)(2,1)} %bitcast.17) | data formatting | bytes 32768000 | tf_op jit(solution)/shard_map/transpose | solution.py:137
  23.3 0.0 copy-done.4
  23.3 0.6 fusion.10
  23.9 1.3 fusion.8
  25.3 0.1 fusion.pick_ref
  25.4 0.0 copy-done.5
  25.4 0.1 broadcast_in_dim_tile.3.keep_ref
  25.5 19.0 %shard_map.37 = bf16[4,250,32,128]{3,2,1,0:T(8,128)(2,1)S(1)} custom-call(bf16[128,256]{1,0:T(8,128)(2,1)S(1)} %fusion.pick_ref, f32[1,128]{1,0:T(1,128)S(1)} %broadcast_in_dim_tile.3.keep_ref, bf16[250,128,256]{2,1,0:T(8,128)(2,1)} %bitcast.12), custom_call_target="tpu_custom_call" | custom-call | flops 2097152000 | bytes 24576000 | tf_op jit(solution)/shard_map/pallas_call | solution.py:39
  44.5 3.6 %fusion.9 = (bf16[1,250,32,128]{3,2,1,0:T(8,128)(2,1)}, bf16[1,250,32,128]{3,2,1,0:T(8,128)(2,1)}, bf16[1,250,32,128]{3,2,1,0:T(8,128)(2,1)}, bf16[1,250,32,128]{3,2,1,0:T(8,128)(2,1)}) fusion(bf16[4,250,32,128]{3,2,1,0:T(8,128)(2,1)S(1)} %shard_map.37), kind=kLoop, calls=%fused_computation.28 | loop fusion | bytes 16384000 | tf_op jit(solution)/shard_map/slice | solution.py:141
  48.1 0.0 all-reduce.4.cloned.1.call-update
  48.1 0.0 reduce-scatter.5.cloned.1.call-start
  48.2 4.0 %multiply_convert_fusion.1 = (bf16[1,101,250]{2,0,1:T(2,128)(2,1)S(1)}, bf16[1,101,250]{2,0,1:T(2,128)(2,1)S(1)}) fusion(s32[250]{0:T(256)S(1)} %iota_add_fusion, s32[101]{0:T(128)S(1)} %iota_add_fusion.1), kind=kLoop, calls=%fused_computation.8 | loop fusion | flops 353500 | bytes 102404 | tf_op jit(solution)/shard_map/convert
  52.3 0.3 maximum_bitcast_fusion
  52.5 0.2 reshape.303
  52.8 122.6 %all-reduce.4.cloned.1.call-done = (bf16[1,250,32,128]{3,2,1,0:T(8,128)(2,1)}, bf16[1,250,32,128]{3,2,1,0:T(8,128)(2,1)}, bf16[1,250,32,128]{3,2,1,0:T(8,128)(2,1)}, bf16[1,250,32,128]{3,2,1,0:T(8,128)(2,1)}) async-done(((bf16[1,250,32,128]{3,2,1,0:T(8,128)(2,1)}, bf16[1,250,32,128]{3,2,1,0:T(8,128)(2,1)}, bf16[1,250,32,128]{3,2,1,0:T(8,128)(2,1)}, bf16[1,250,32,128]{3,2,1,0:T(8,128)(2,1)}), ...) | async-done | bytes 8192016 | tf_op jit(solution)/shard_map/psum | solution.py:141
  175.3 0.0 copy-start.3
  175.4 1.6 copy-done.3
  176.9 0.0 copy-start.2
  176.9 14.6 %shard_map.38 = bf16[32,101,256]{2,1,0:T(8,128)(2,1)} custom-call(bf16[1,128]{1,0:T(2,128)(2,1)S(1)} %fusion.4.sign_ref, bf16[112,500]{1,0:T(8,128)(2,1)S(1)} %pad.4.table_ref, bf16[1,250,32,128]{3,2,1,0:T(8,128)(2,1)S(1)} %copy-done.3, bf16[250,128,256]{2,1,0:T(8,128)(2,1)} %bitcast.13), custom_call_target="tpu_custom_call" | custom-call | flops 1875968000 | bytes 20086784 | tf_op jit(solution)/shard_map/pallas_call | solution.py:97
  191.6 0.0 reduce-scatter.5.cloned.1.call-update
  191.6 0.0 reduce-scatter.7.cloned.1.call-start
  191.6 0.0 copy-done.2
  191.6 14.5 %shard_map.39 = bf16[32,101,256]{2,1,0:T(8,128)(2,1)} custom-call(bf16[1,128]{1,0:T(2,128)(2,1)S(1)} %fusion.4.sign_ref, bf16[112,500]{1,0:T(8,128)(2,1)S(1)} %pad.4.table_ref, bf16[1,250,32,128]{3,2,1,0:T(8,128)(2,1)S(1)} %copy-done.2, bf16[250,128,256]{2,1,0:T(8,128)(2,1)} %bitcast.14), custom_call_target="tpu_custom_call" | custom-call | flops 1875968000 | bytes 20086784 | tf_op jit(solution)/shard_map/pallas_call | solution.py:97
  206.1 0.0 reduce-scatter.7.cloned.1.call-update
  206.1 0.0 reduce-scatter.9.cloned.1.call-start
  206.2 0.0 copy-start.1
  206.2 1.6 copy-done.1
  207.8 0.0 copy-start
  207.8 14.7 %shard_map.40 = bf16[32,101,256]{2,1,0:T(8,128)(2,1)} custom-call(bf16[1,128]{1,0:T(2,128)(2,1)S(1)} %fusion.4.sign_ref, bf16[112,500]{1,0:T(8,128)(2,1)S(1)} %pad.4.table_ref, bf16[1,250,32,128]{3,2,1,0:T(8,128)(2,1)S(1)} %copy-done.1, bf16[250,128,256]{2,1,0:T(8,128)(2,1)} %bitcast.15), custom_call_target="tpu_custom_call" | custom-call | flops 1875968000 | bytes 20086784 | tf_op jit(solution)/shard_map/pallas_call | solution.py:97
  222.4 0.0 reduce-scatter.9.cloned.1.call-update
  222.4 0.0 reduce-scatter.11.cloned.1.call-start
  222.5 0.0 copy-done
  222.5 14.5 %shard_map.41 = bf16[32,101,256]{2,1,0:T(8,128)(2,1)} custom-call(bf16[1,128]{1,0:T(2,128)(2,1)S(1)} %fusion.4.sign_ref, bf16[112,500]{1,0:T(8,128)(2,1)S(1)} %pad.4.table_ref, bf16[1,250,32,128]{3,2,1,0:T(8,128)(2,1)S(1)} %copy-done, bf16[250,128,256]{2,1,0:T(8,128)(2,1)} %bitcast.16), custom_call_target="tpu_custom_call" | custom-call | flops 1875968000 | bytes 20086784 | tf_op jit(solution)/shard_map/pallas_call | solution.py:97
  237.0 0.0 reduce-scatter.11.cloned.1.call-update
  237.0 0.0 reduce-scatter.5.cloned.1.call-done
  237.1 29.9 %reduce-scatter.7.cloned.1.call-done = bf16[8,101,256]{2,1,0:T(8,128)(2,1)} async-done(((bf16[32,101,256]{2,1,0:T(8,128)(2,1)}), bf16[8,101,256]{2,1,0:T(8,128)(2,1)}) %reduce-scatter.7.cloned.1.call-update) | async-done | bytes 413712 | tf_op jit(solution)/shard_map/reduce_scatter | solution.py:143
  267.0 38.7 %reduce-scatter.9.cloned.1.call-done = bf16[8,101,256]{2,1,0:T(8,128)(2,1)} async-done(((bf16[32,101,256]{2,1,0:T(8,128)(2,1)}), bf16[8,101,256]{2,1,0:T(8,128)(2,1)}) %reduce-scatter.9.cloned.1.call-update) | async-done | bytes 413712 | tf_op jit(solution)/shard_map/reduce_scatter | solution.py:143
  305.7 38.7 %reduce-scatter.11.cloned.1.call-done = bf16[8,101,256]{2,1,0:T(8,128)(2,1)} async-done(((bf16[32,101,256]{2,1,0:T(8,128)(2,1)}), bf16[8,101,256]{2,1,0:T(8,128)(2,1)}) %reduce-scatter.11.cloned.1.call-update) | async-done | bytes 413712 | tf_op jit(solution)/shard_map/reduce_scatter | solution.py:143
  344.4 1.6 pad_maximum_fusion
  346.0 1.6 copy.5
  (7 shorter events, 0.0 us)
Async XLA Ops:
  6.5 168.8 %all-reduce.4.cloned.1.call-start = ((), (), s32[]{:S(2)}) async-start(), calls=%async_computation.8 | async-start | bytes 16384000 | tf_op jit(solution)/shard_map/psum | solution.py:141
  6.7 16.6 %copy-start.4 = (s32[2]{0:T(128)S(1)}, s32[2]{0:T(128)}, u32[]{:S(2)}) copy-start(s32[2]{0:T(128)} %param.4) | copy-start | bytes 28
  6.8 18.6 %copy-start.5 = (s32[64]{0:T(128)S(1)}, s32[64]{0:T(128)}, u32[]{:S(2)}) copy-start(s32[64]{0:T(128)} %param.5) | copy-start | bytes 772
  48.1 188.9 %reduce-scatter.5.cloned.1.call-start = ((), (), s32[]{:S(2)}) async-start(), calls=%async_computation.4 | async-start | bytes 2129920 | tf_op jit(solution)/shard_map/reduce_scatter | solution.py:143
  175.3 1.6 copy-start.3
  176.9 14.7 %copy-start.2 = (bf16[1,250,32,128]{3,2,1,0:T(8,128)(2,1)S(1)}, bf16[1,250,32,128]{3,2,1,0:T(8,128)(2,1)}, u32[]{:S(2)}) copy-start(bf16[1,250,32,128]{3,2,1,0:T(8,128)(2,1)} %get-tuple-element.7.source_ref) | copy-start | bytes 6144004
  191.6 75.4 %reduce-scatter.7.cloned.1.call-start = ((), (), s32[]{:S(2)}) async-start(), calls=%async_computation.5 | async-start | bytes 2129920 | tf_op jit(solution)/shard_map/reduce_scatter | solution.py:143
  206.1 99.6 %reduce-scatter.9.cloned.1.call-start = ((), (), s32[]{:S(2)}) async-start(), calls=%async_computation.6 | async-start | bytes 2129920 | tf_op jit(solution)/shard_map/reduce_scatter | solution.py:143
  206.2 1.6 copy-start.1
  207.8 14.7 %copy-start = (bf16[1,250,32,128]{3,2,1,0:T(8,128)(2,1)S(1)}, bf16[1,250,32,128]{3,2,1,0:T(8,128)(2,1)}, u32[]{:S(2)}) copy-start(bf16[1,250,32,128]{3,2,1,0:T(8,128)(2,1)} %get-tuple-element.5.source_ref) | copy-start | bytes 6144004
  222.4 122.0 %reduce-scatter.11.cloned.1.call-start = ((), (), s32[]{:S(2)}) async-start(), calls=%async_computation.7 | async-start | bytes 2129920 | tf_op jit(solution)/shard_map/reduce_scatter | solution.py:143
Sparse Core Ops, SparseCore 0:
  48.3 127.0 all-reduce.3
  191.7 36.4 reduce-scatter.4
  230.6 36.3 reduce-scatter.6
  269.3 36.3 reduce-scatter.8
  308.0 36.3 reduce-scatter.10

commit v2 on v1

v2 whole, which is shorter than its diff:
```python
import functools

import jax
import jax.numpy as jnp
import ml_dtypes
import numpy as np
from jax import lax
from jax.experimental import pallas as pl
from jax.experimental.pallas import tpu as pltpu
from jax.sharding import PartitionSpec as P

LAGS = 101
SRC_BLK = 64
ROWS = (8, 8, 8, 8)
MIB = 1024 * 1024


def lag_table(bin_count, lag_count, segment_total):
    bins_idx = np.arange(bin_count) + 1
    lag_steps = np.arange(lag_count) - (lag_count - 1) // 2
    phase_int = lag_steps[:, None] * bins_idx[None, :] % (2 * bin_count)
    phase = phase_int * (2.0 * np.pi / (2.0 * bin_count))
    scale = 1.0 / np.sqrt(float(segment_total * bin_count))
    return np.stack([np.cos(phase) * scale, -np.sin(phase) * scale]).astype(ml_dtypes.bfloat16)


def pick_kernel(pick_ref, keep_ref, x_ref, out_ref):
    for f in range(out_ref.shape[0]):
        picked = lax.dot_general(
            pick_ref[...], x_ref[f], (((1,), (1,)), ((), ())), preferred_element_type=jnp.float32
        )
        out_ref[f] = (picked * keep_ref[...]).astype(jnp.bfloat16)


def pick_sources(pick, keep, x, bins):
    bin_count, depth, width = x.shape
    rows = pick.shape[0]
    return pl.pallas_call(
        pick_kernel,
        grid=(bin_count // bins,),
        in_specs=[
            pl.BlockSpec(pick.shape, lambda i: (0, 0)),
            pl.BlockSpec(keep.shape, lambda i: (0, 0)),
            pl.BlockSpec((bins, depth, width), lambda i: (i, 0, 0)),
        ],
        out_specs=pl.BlockSpec((bins, rows, depth), lambda i: (i, 0, 0)),
        out_shape=jax.ShapeDtypeStruct((bin_count, rows, depth), jnp.bfloat16),
        compiler_params=pltpu.CompilerParams(vmem_limit_bytes=32 * MIB),
        cost_estimate=pl.CostEstimate(
            flops=2 * bin_count * rows * width * depth,
            bytes_accessed=2 * bin_count * depth * (width + rows),
            transcendentals=0,
        ),
    )(pick, keep, x)


def correlate_kernel(stride, bin_count, sign_ref, table_ref, source_ref, x_ref, out_ref, cross):
    bins, rows, depth = source_ref.shape
    width = x_ref.shape[2]
    halves = width // 128
    step = pl.program_id(0)
    sign = sign_ref[...]
    for i in range(bins):
        f = step * bins + i
        real = source_ref[i]
        half = depth // 2
        imag = jnp.concatenate([real[:, half:], real[:, :half]], axis=1) * sign
        both = jnp.concatenate([real, imag], axis=0)
        product = jnp.dot(both, x_ref[i], preferred_element_type=jnp.float32)
        for part in range(2):
            for h in range(halves):
                cross[h, pl.ds(part * bin_count + f, rows, stride=stride), :] = product[
                    part * rows:(part + 1) * rows, h * 128:(h + 1) * 128
                ]

    @pl.when(step == pl.num_programs(0) - 1)
    def _():
        lags = out_ref.shape[1]

        def one_row(k, carry):
            at = pl.multiple_of(k * stride, 8)
            block = jnp.concatenate(
                [cross[h, pl.ds(at, 2 * bin_count), :].astype(jnp.bfloat16) for h in range(halves)], axis=1
            )
            lagged = jnp.dot(table_ref[...], block, preferred_element_type=jnp.float32)
            out_ref[k] = lagged[:lags].astype(jnp.bfloat16)
            return carry

        lax.fori_loop(0, rows, one_row, 0, unroll=4)


def correlate(sign, table, sources, x, bins):
    bin_count, rows, depth = sources.shape
    width = x.shape[2]
    stride = -(-2 * bin_count // 8) * 8
    return pl.pallas_call(
        functools.partial(correlate_kernel, stride, bin_count),
        grid=(bin_count // bins,),
        in_specs=[
            pl.BlockSpec(sign.shape, lambda i: (0, 0)),
            pl.BlockSpec(table.shape, lambda i: (0, 0)),
            pl.BlockSpec((bins, rows, depth), lambda i: (i, 0, 0)),
            pl.BlockSpec((bins, depth, width), lambda i: (i, 0, 0)),
        ],
        out_specs=pl.BlockSpec((rows, LAGS, width), lambda i: (0, 0, 0)),
        out_shape=jax.ShapeDtypeStruct((rows, LAGS, width), jnp.bfloat16),
        scratch_shapes=[pltpu.VMEM((width // 128, rows * stride, 128), jnp.float32)],
        compiler_params=pltpu.CompilerParams(vmem_limit_bytes=48 * MIB),
        cost_estimate=pl.CostEstimate(
            flops=2 * bin_count * 2 * rows * depth * width + 2 * 2 * bin_count * rows * LAGS * width,
            bytes_accessed=2 * bin_count * depth * (width + rows) + 2 * rows * LAGS * width,
            transcendentals=0,
        ),
    )(sign, table, sources, x)


def add(a, b):
    return (a.astype(jnp.float32) + b.astype(jnp.float32)).astype(jnp.bfloat16)


def chain_scatter(parts, axis):
    n, at = lax.axis_size(axis), lax.axis_index(axis)
    total = None
    from_left = from_right = None
    for t in range(n - 1):
        to_right = lax.dynamic_index_in_dim(parts, jnp.clip(n - 1 - t + at, 0, n - 1), 0, keepdims=False)
        to_left = lax.dynamic_index_in_dim(parts, jnp.clip(t + at - (n - 1), 0, n - 1), 0, keepdims=False)
        if t:
            to_right, to_left = add(to_right, from_left), add(to_left, from_right)
        from_left = lax.ppermute(to_right, axis, [(i, i + 1) for i in range(t + 1)])
        from_right = lax.ppermute(to_left, axis, [(n - 1 - i, n - 2 - i) for i in range(t + 1)])
    own = lax.dynamic_index_in_dim(parts, at, 0, keepdims=False).astype(jnp.float32)
    total = own + from_left.astype(jnp.float32) + from_right.astype(jnp.float32)
    return total.astype(jnp.bfloat16)


def body(spectra, src_blocks, valid):
    seg_count, _, bin_count, width = spectra.shape
    tm_count = lax.axis_size("tm")
    chan_index = lax.axis_index("chan")
    depth = 2 * seg_count
    sources_all = 2 * SRC_BLK
    per_dev = sources_all // tm_count

    keep = jnp.tile(valid.astype(jnp.float32), 2)[None, :]
    sign = np.where(np.arange(depth) < seg_count, -1.0, 1.0).astype(ml_dtypes.bfloat16)[None, :]
    table = lag_table(bin_count, LAGS, seg_count * tm_count)
    table = table.transpose(1, 0, 2).reshape(LAGS, 2 * bin_count)
    table = np.pad(table, ((0, -LAGS % 16), (0, 0)))
    sign, table = jnp.asarray(sign), jnp.asarray(table)

    def pick_of(first, rows):
        order = np.arange(sources_all, dtype=np.int32).reshape(tm_count, per_dev)
        order = order[:, first:first + rows].reshape(-1)
        channel = src_blocks[order // SRC_BLK] * SRC_BLK + order % SRC_BLK - chan_index * width
        return (channel[:, None] == jnp.arange(width, dtype=jnp.int32)[None, :]).astype(jnp.bfloat16)

    x = spectra.transpose(2, 1, 0, 3).reshape(bin_count, depth, width)
    pieces = []
    source = None
    first = 0
    for rows in ROWS:
        mine = pick_sources(pick_of(first, rows), keep, x, 25)
        if source is not None:
            mine, source = lax.optimization_barrier((mine, source))
        if source is not None:
            pieces.append(source)
        source = lax.psum(mine, "chan")
        first += rows
    pieces.append(source)
    outs = []
    for rows, source in zip(ROWS, pieces):
        partial_value = correlate(sign, table, source, x, 25)
        outs.append(chain_scatter(partial_value.reshape(tm_count, rows, LAGS, width), "tm"))
    return jnp.concatenate(outs, axis=0)


def solution(mesh):
    placed = (P("tm", None, None, "chan"), P(), P("tm"))
    return jax.shard_map(
        body, mesh=mesh, in_specs=placed, out_specs=P("tm", None, "chan"), check_vma=False
    )
```

time: 358 us -> 399 us (1.11)
  starting transfers between devices: 0.17 us -> 52.1 us
  waiting for transfers between devices: 230 us -> 180 us
  local copies, waits for them, and re-layouts: 25.9 us -> 47.8 us
  other arithmetic: 7.37 us -> 19.4 us
  Pallas kernels: 77.3 us -> 83.7 us
    reduce_scatter x4 -> x0, waiting for transfers between devices: 107 us -> none  [body(): lax.psum_scatter(partial_value, 'tm', scatter_dimension=0, tiled=True)]
    ppermute x0 -> x24, starting transfers between devices: none -> 52 us  [the longest x12 32.9 us: chain_scatter(): from_left = lax.ppermute(to_right, axis, [(i, i + 1) for i in range(t + 1)])]
    ppermute x0 -> x24, waiting for transfers between devices: none -> 34.3 us  [the longest x12 30 us: chain_scatter(): from_left = lax.ppermute(to_right, axis, [(i, i + 1) for i in range(t + 1)])]
    unnamed x12 -> x46, local copies, waits for them, and re-layouts: 3.16 us -> 29.7 us
    psum x1 -> x4, waiting for transfers between devices: 123 us -> 146 us  [body(): source = lax.psum(mine, 'chan')]
    convert_element_type x2 -> x24, other arithmetic: 0.09 us -> 15.4 us  [the longest x16 13.3 us: add(): return (a.astype(jnp.float32) + b.astype(jnp.float32)).astype(jnp.bfloat16)]
    pallas_call x1 -> x4, Pallas kernels: 19 us -> 29.5 us  [pick_sources(): pl.pallas_call(pick_kernel, grid=(bin_count // bins,), in_specs=[pl.Block...]
    dynamic_slice x0 -> x10, local copies, waits for them, and re-layouts: none -> 5.4 us  [the longest x2 2.42 us: chain_scatter(): lax.dynamic_index_in_dim(parts, at, 0, keepdims=False).astype(jnp.float32)]
  transfers between devices with their start and end apart: 5 -> 28, of which waited for: 4 -> 12; matrix products, arithmetic and copies ran while one was open for 1% -> 4% of each run, Pallas kernels for 12% -> 16%
where the time goes in v2:
time: 399 us; the launch traced here: 397 us
  waiting for transfers between devices  180 us (45%)
  Pallas kernels  83.7 us (21%)
  starting transfers between devices  52.1 us (13%)
  local copies, waits for them, and re-layouts  47.8 us (12%)
  other arithmetic  19.4 us (5%)
  between operations  13.7 us (3%)
    psum x4, waiting for transfers between devices, body(): source = lax.psum(mine, 'chan')  146 us
    pallas_call x4, Pallas kernels, correlate(): pl.pallas_call(functools.partial(correlate_kernel, stride, bin_count), gr...  54.3 us
    ppermute x12, starting transfers between devices, chain_scatter(): from_left = lax.ppermute(to_right, axis, [(i, i + 1) for i in range(t + 1)])  32.9 us
    ppermute x12, waiting for transfers between devices, chain_scatter(): from_left = lax.ppermute(to_right, axis, [(i, i + 1) for i in range(t + 1)])  30 us
    unnamed x46, local copies, waits for them, and re-layouts  29.7 us
    pallas_call x4, Pallas kernels, pick_sources(): pl.pallas_call(pick_kernel, grid=(bin_count // bins,), in_specs=[pl.Block...  29.5 us
    ppermute x12, starting transfers between devices, chain_scatter(): lax.ppermute(to_left, axis, [(n - 1 - i, n - 2 - i) for i in range(t + 1)])  19.1 us
    convert_element_type x16, other arithmetic, add(): return (a.astype(jnp.float32) + b.astype(jnp.float32)).astype(jnp.bfloat16)  13.3 us
  transfers between devices with their start and end apart: 28, of which 12 were waited for; matrix products, arithmetic and copies ran while one was open for 4% of the time, Pallas kernels for 16%

profile of v2, /device:TPU:8, one launch (start us, length us, event | category | flops | bytes accessed | tf_op | source)
XLA Modules:
  0.0 397.1 jit_solution(13280930669561006081)
XLA Ops:
  8.6 1.9 add_subtract_fusion.2
  10.6 11.3 %copy.18 = bf16[250,2,64,256]{3,2,1,0:T(8,128)(2,1)S(1)} copy(bf16[250,2,64,256]{3,1,0,2:T(2,128)(2,1)} %bitcast.144) | data formatting | bytes 32768000 | tf_op jit(solution)/shard_map/transpose | solution.py:158
  21.9 7.6 %shard_map.164 = bf16[250,32,128]{2,1,0:T(8,128)(2,1)} custom-call(bf16[32,256]{1,0:T(8,128)(2,1)S(1)} %fusion.25.pick_ref, f32[1,128]{1,0:T(1,128)S(1)} %broadcast_in_dim_tile.3.keep_ref, bf16[250,128,256]{2,1,0:T(8,128)(2,1)S(1)} %bitcast.132), custom_call_target="tpu_custom_call" | custom-call | flops 524288000 | bytes 18432000 | tf_op jit(solution)/shard_map/pallas_call | solution.py:38
  29.5 5.6 %copy-done = bf16[250,2,64,256]{3,2,1,0:T(8,128)(2,1)} copy-done((bf16[250,2,64,256]{3,2,1,0:T(8,128)(2,1)}, bf16[250,2,64,256]{3,2,1,0:T(8,128)(2,1)S(1)}, u32[]{:S(2)}) %copy-start) | copy-done | bytes 16384024
  35.9 5.7 %copy-done.1 = bf16[250,2,64,256]{3,2,1,0:T(8,128)(2,1)S(1)} copy-done((bf16[250,2,64,256]{3,2,1,0:T(8,128)(2,1)S(1)}, bf16[250,2,64,256]{3,2,1,0:T(8,128)(2,1)}, u32[]{:S(2)}) %copy-start.1) | copy-done | bytes 16384024
  41.5 7.5 %shard_map.163 = bf16[250,32,128]{2,1,0:T(8,128)(2,1)} custom-call(bf16[32,256]{1,0:T(8,128)(2,1)S(1)} %fusion.24.pick_ref, f32[1,128]{1,0:T(1,128)S(1)} %broadcast_in_dim_tile.3.keep_ref, bf16[250,128,256]{2,1,0:T(8,128)(2,1)S(1)} %bitcast.137), custom_call_target="tpu_custom_call" | custom-call | flops 524288000 | bytes 18432000 | tf_op jit(solution)/shard_map/pallas_call | solution.py:38
  49.0 48.8 %all-reduce.5.cloned.1.call-done.source_ref = bf16[250,32,128]{2,1,0:T(8,128)(2,1)} async-done(((bf16[250,32,128]{2,1,0:T(8,128)(2,1)}), bf16[250,32,128]{2,1,0:T(8,128)(2,1)}) %all-reduce.5.cloned.1.call-update) | async-done | bytes 2048016 | tf_op jit(solution)/shard_map/psum | solution.py:168
  98.0 5.7 %copy-done.2 = bf16[250,2,64,256]{3,2,1,0:T(8,128)(2,1)S(1)} copy-done((bf16[250,2,64,256]{3,2,1,0:T(8,128)(2,1)S(1)}, bf16[250,2,64,256]{3,2,1,0:T(8,128)(2,1)}, u32[]{:S(2)}) %copy-start.2) | copy-done | bytes 16384024
  103.7 6.8 %shard_map.166 = bf16[250,32,128]{2,1,0:T(8,128)(2,1)S(1)} custom-call(bf16[32,256]{1,0:T(8,128)(2,1)S(1)} %fusion.26.pick_ref, f32[1,128]{1,0:T(1,128)S(1)} %broadcast_in_dim_tile.3.keep_ref, bf16[250,128,256]{2,1,0:T(8,128)(2,1)S(1)} %bitcast.138), custom_call_target="tpu_custom_call" | custom-call | flops 524288000 | bytes 18432000 | tf_op jit(solution)/shard_map/pallas_call | solution.py:38
  111.9 1.6 copy-done.6
  113.4 13.6 %shard_map.165 = bf16[32,101,256]{2,1,0:T(8,128)(2,1)S(1)} custom-call(bf16[1,128]{1,0:T(2,128)(2,1)S(1)} %copy-done.10, bf16[112,500]{1,0:T(8,128)(2,1)S(1)} %copy-done.9, bf16[250,32,128]{2,1,0:T(8,128)(2,1)S(1)} %copy-done.6, bf16[250,128,256]{2,1,0:T(8,128)(2,1)} %bitcast.133), custom_call_target="tpu_custom_call" | custom-call | flops 1875968000 | bytes 20086784 | tf_op jit(solution)/shard_map/pallas_call | solution.py:96
  127.0 34.8 %all-reduce.7.cloned.1.call-done.source_ref = bf16[250,32,128]{2,1,0:T(8,128)(2,1)} async-done(((bf16[250,32,128]{2,1,0:T(8,128)(2,1)}), bf16[250,32,128]{2,1,0:T(8,128)(2,1)}) %all-reduce.7.cloned.1.call-update) | async-done | bytes 2048016 | tf_op jit(solution)/shard_map/psum | solution.py:168
  161.8 1.6 copy-done.7
  163.4 13.5 %shard_map.167 = bf16[32,101,256]{2,1,0:T(8,128)(2,1)S(1)} custom-call(bf16[1,128]{1,0:T(2,128)(2,1)S(1)} %copy-done.10, bf16[112,500]{1,0:T(8,128)(2,1)S(1)} %copy-done.9, bf16[250,32,128]{2,1,0:T(8,128)(2,1)S(1)} %copy-done.7, bf16[250,128,256]{2,1,0:T(8,128)(2,1)} %bitcast.134), custom_call_target="tpu_custom_call" | custom-call | flops 1875968000 | bytes 20086784 | tf_op jit(solution)/shard_map/pallas_call | solution.py:96
  176.9 1.9 constant_dynamic-slice_fusion.20
  183.4 6.0 %copy-done.3 = bf16[250,2,64,256]{3,2,1,0:T(8,128)(2,1)S(1)} copy-done((bf16[250,2,64,256]{3,2,1,0:T(8,128)(2,1)S(1)}, bf16[250,2,64,256]{3,2,1,0:T(8,128)(2,1)}, u32[]{:S(2)}) %copy-start.3) | copy-done | bytes 16384024
  189.4 7.5 %shard_map.168 = bf16[250,32,128]{2,1,0:T(8,128)(2,1)} custom-call(bf16[32,256]{1,0:T(8,128)(2,1)S(1)} %fusion.27.pick_ref, f32[1,128]{1,0:T(1,128)S(1)} %broadcast_in_dim_tile.3.keep_ref, bf16[250,128,256]{2,1,0:T(8,128)(2,1)S(1)} %bitcast.139), custom_call_target="tpu_custom_call" | custom-call | flops 524288000 | bytes 18432000 | tf_op jit(solution)/shard_map/pallas_call | solution.py:38
  199.9 1.9 fusion.20
  201.8 3.4 collective-permute-start.1
  205.2 2.0 fusion.18
  209.4 1.4 collective-permute-start.10
  210.8 31.1 %all-reduce.9.cloned.1.call-done.source_ref = bf16[250,32,128]{2,1,0:T(8,128)(2,1)} async-done(((bf16[250,32,128]{2,1,0:T(8,128)(2,1)}), bf16[250,32,128]{2,1,0:T(8,128)(2,1)}) %all-reduce.9.cloned.1.call-update) | async-done | bytes 2048016 | tf_op jit(solution)/shard_map/psum | solution.py:168
  242.8 3.5 collective-permute-start.7
  246.3 1.9 fusion.21
  248.2 1.9 collective-permute-start.2
  250.1 1.9 fusion.19
  252.0 4.7 %collective-permute-start.5 = (bf16[8,101,256]{2,0,1:T(8,128)(2,1)}, bf16[8,101,256]{2,0,1:T(8,128)(2,1)}, u32[]{:S(2)}, u32[]{:S(2)}) collective-permute-start(bf16[8,101,256]{2,0,1:T(8,128)(2,1)} %fusion.19), channel_id=1, source_target_pairs={{3,2},{2,1},{1,0},{7,6},{6,5},{5,4},{11,10},{10,9},{9,8},{15,14},{... | collective-permute-start | bytes 1241096 | tf_op jit(solution)/shard_map/ppermute | solution.py:131
  256.7 1.9 fusion.13
  258.6 1.9 collective-permute-start.11
  260.5 13.7 %shard_map.169 = bf16[32,101,256]{2,1,0:T(8,128)(2,1)S(1)} custom-call(bf16[1,128]{1,0:T(2,128)(2,1)S(1)} %copy-done.10, bf16[112,500]{1,0:T(8,128)(2,1)S(1)} %copy-done.9, bf16[250,32,128]{2,1,0:T(8,128)(2,1)S(1)} %copy-done.5, bf16[250,128,256]{2,1,0:T(8,128)(2,1)} %bitcast.135), custom_call_target="tpu_custom_call" | custom-call | flops 1875968000 | bytes 20086784 | tf_op jit(solution)/shard_map/pallas_call | solution.py:96
  274.2 31.4 %all-reduce.11.cloned.1.call-done.source_ref = bf16[250,32,128]{2,1,0:T(8,128)(2,1)} async-done(((bf16[250,32,128]{2,1,0:T(8,128)(2,1)}), bf16[250,32,128]{2,1,0:T(8,128)(2,1)}) %all-reduce.11.cloned.1.call-update) | async-done | bytes 2048016 | tf_op jit(solution)/shard_map/psum | solution.py:168
  305.6 1.6 copy-done.8
  307.2 13.5 %shard_map.170 = bf16[32,101,256]{2,1,0:T(8,128)(2,1)S(1)} custom-call(bf16[1,128]{1,0:T(2,128)(2,1)S(1)} %copy-done.10, bf16[112,500]{1,0:T(8,128)(2,1)S(1)} %copy-done.9, bf16[250,32,128]{2,1,0:T(8,128)(2,1)S(1)} %copy-done.8, bf16[250,128,256]{2,1,0:T(8,128)(2,1)} %bitcast.136), custom_call_target="tpu_custom_call" | custom-call | flops 1875968000 | bytes 20086784 | tf_op jit(solution)/shard_map/pallas_call | solution.py:96
  323.7 2.8 collective-permute-start.8
  329.5 6.2 %collective-permute-done.12 = bf16[8,101,256]{2,0,1:T(8,128)(2,1)S(1)} collective-permute-done((bf16[8,101,256]{2,0,1:T(8,128)(2,1)S(1)}, bf16[8,101,256]{2,0,1:T(8,128)(2,1)S(1)}, u32[]{:S(2)}, u32[]{:S(2)}) %collective-permute-start.12) | collective-permute-done | bytes 413728 | tf_op jit(solution)/shard_map/ppermute | solution.py:130
  337.1 7.3 %collective-permute-start.13 = (bf16[8,101,256]{2,0,1:T(8,128)(2,1)S(1)}, bf16[8,101,256]{2,0,1:T(8,128)(2,1)S(1)}, u32[]{:S(2)}, u32[]{:S(2)}) collective-permute-start(bf16[8,101,256]{2,0,1:T(8,128)(2,1)S(1)} %fusion.8), channel_id=1, source_target_pairs={{0,1},{1,2},{4,5},{5,6},{8,9},{9,10},{12,13},{13,14},{16,17},{17,1... | collective-permute-start | bytes 1241096 | tf_op jit(solution)/shard_map/ppermute | solution.py:130
  346.0 7.5 %collective-permute-done.18 = bf16[8,101,256]{2,0,1:T(8,128)(2,1)S(1)} collective-permute-done((bf16[8,101,256]{2,0,1:T(8,128)(2,1)S(1)}, bf16[8,101,256]{2,0,1:T(8,128)(2,1)S(1)}, u32[]{:S(2)}, u32[]{:S(2)}) %collective-permute-start.18) | collective-permute-done | bytes 413728 | tf_op jit(solution)/shard_map/ppermute | solution.py:130
  354.8 5.2 %collective-permute-done.13 = bf16[8,101,256]{2,0,1:T(8,128)(2,1)S(1)} collective-permute-done((bf16[8,101,256]{2,0,1:T(8,128)(2,1)S(1)}, bf16[8,101,256]{2,0,1:T(8,128)(2,1)S(1)}, u32[]{:S(2)}, u32[]{:S(2)}) %collective-permute-start.13) | collective-permute-done | bytes 413728 | tf_op jit(solution)/shard_map/ppermute | solution.py:130
  360.1 1.9 collective-permute-start.19
  362.1 3.0 collective-permute-start.14
  365.3 1.7 collective-permute-done.22
  367.0 1.9 collective-permute-start.17
  369.0 5.4 %collective-permute-done.19 = bf16[8,101,256]{2,0,1:T(8,128)(2,1)S(1)} collective-permute-done((bf16[8,101,256]{2,0,1:T(8,128)(2,1)S(1)}, bf16[8,101,256]{2,0,1:T(8,128)(2,1)S(1)}, u32[]{:S(2)}, u32[]{:S(2)}) %collective-permute-start.19) | collective-permute-done | bytes 413728 | tf_op jit(solution)/shard_map/ppermute | solution.py:130
  374.4 1.9 collective-permute-start.23
  376.5 3.9 collective-permute-start.20
  380.6 2.7 collective-permute-done.14
  383.5 2.7 collective-permute-done.23
  386.2 2.9 collective-permute-done.20
  (108 shorter events, 27.5 us)
Async XLA Ops:
  6.5 91.3 %all-reduce.5.cloned.1.call-start = ((), (), s32[]{:S(2)}) async-start(), calls=%async_computation | async-start | bytes 4096000 | tf_op jit(solution)/shard_map/psum | solution.py:168
  29.5 5.6 %copy-start = (bf16[250,2,64,256]{3,2,1,0:T(8,128)(2,1)}, bf16[250,2,64,256]{3,2,1,0:T(8,128)(2,1)S(1)}, u32[]{:S(2)}) copy-start(bf16[250,2,64,256]{3,2,1,0:T(8,128)(2,1)S(1)} %copy.18) | copy-start | bytes 49152004
  35.1 126.7 %all-reduce.7.cloned.1.call-start = ((), (), s32[]{:S(2)}) async-start(), calls=%async_computation.1 | async-start | bytes 4096000 | tf_op jit(solution)/shard_map/psum | solution.py:168
  35.9 5.7 %copy-start.1 = (bf16[250,2,64,256]{3,2,1,0:T(8,128)(2,1)S(1)}, bf16[250,2,64,256]{3,2,1,0:T(8,128)(2,1)}, u32[]{:S(2)}) copy-start(bf16[250,2,64,256]{3,2,1,0:T(8,128)(2,1)} %copy-done) | copy-start | bytes 49152004
  97.9 144.0 %all-reduce.9.cloned.1.call-start = ((), (), s32[]{:S(2)}) async-start(), calls=%async_computation.2 | async-start | bytes 4096000 | tf_op jit(solution)/shard_map/psum | solution.py:168
  98.0 5.7 %copy-start.2 = (bf16[250,2,64,256]{3,2,1,0:T(8,128)(2,1)S(1)}, bf16[250,2,64,256]{3,2,1,0:T(8,128)(2,1)}, u32[]{:S(2)}) copy-start(bf16[250,2,64,256]{3,2,1,0:T(8,128)(2,1)} %copy-done) | copy-start | bytes 49152004
  103.7 8.2 %copy-start.9 = (bf16[112,500]{1,0:T(8,128)(2,1)S(1)}, bf16[112,500]{1,0:T(8,128)(2,1)}, u32[]{:S(2)}) copy-start(bf16[112,500]{1,0:T(8,128)(2,1)} %constant.112.clone.table_ref) | copy-start | bytes 336004
  103.7 8.2 %copy-start.10 = (bf16[1,128]{1,0:T(2,128)(2,1)S(1)}, bf16[1,128]{1,0:T(2,128)(2,1)}, u32[]{:S(2)}) copy-start(bf16[1,128]{1,0:T(2,128)(2,1)} %constant.111.clone.sign_ref) | copy-start | bytes 772
  110.5 1.3 copy-start.4
  111.9 1.6 copy-start.6
  161.8 1.6 copy-start.7
  178.8 2.2 copy-start.19
  179.6 20.3 %collective-permute-start = (bf16[8,101,256]{2,0,1:T(8,128)(2,1)}, bf16[8,101,256]{2,0,1:T(8,128)(2,1)}, u32[]{:S(2)}, u32[]{:S(2)}) collective-permute-start(bf16[8,101,256]{2,0,1:T(8,128)(2,1)} %bitcast.131), channel_id=1, source_target_pairs={{0,1},{4,5},{8,9},{12,13},{16,17},{20,21},{24,25},{28,29}} | collective-permute-start | bytes 1241096 | tf_op jit(solution)/shard_map/ppermute | solution.py:130
  181.0 124.7 %all-reduce.11.cloned.1.call-start = ((), (), s32[]{:S(2)}) async-start(), calls=%async_computation.3 | async-start | bytes 4096000 | tf_op jit(solution)/shard_map/psum | solution.py:168
  181.9 23.3 %collective-permute-start.3 = (bf16[8,101,256]{2,0,1:T(8,128)(2,1)}, bf16[8,101,256]{2,0,1:T(8,128)(2,1)}, u32[]{:S(2)}, u32[]{:S(2)}) collective-permute-start(bf16[8,101,256]{2,0,1:T(8,128)(2,1)} %bitcast.130), channel_id=1, source_target_pairs={{3,2},{7,6},{11,10},{15,14},{19,18},{23,22},{27,26},{31,30}} | collective-permute-start | bytes 1241096 | tf_op jit(solution)/shard_map/ppermute | solution.py:131
  183.4 6.1 %copy-start.3 = (bf16[250,2,64,256]{3,2,1,0:T(8,128)(2,1)S(1)}, bf16[250,2,64,256]{3,2,1,0:T(8,128)(2,1)}, u32[]{:S(2)}) copy-start(bf16[250,2,64,256]{3,2,1,0:T(8,128)(2,1)} %copy-done) | copy-start | bytes 49152004
  189.4 7.6 %copy-start.18 = (bf16[1,8,101,256]{3,2,1,0:T(8,128)(2,1)S(1)}, bf16[1,8,101,256]{3,2,1,0:T(8,128)(2,1)}, u32[]{:S(2)}) copy-start(bf16[1,8,101,256]{3,2,1,0:T(8,128)(2,1)} %get-tuple-element.30) | copy-start | bytes 1241092
  189.4 8.4 %copy-start.17 = (bf16[1,8,101,256]{3,2,1,0:T(8,128)(2,1)S(1)}, bf16[1,8,101,256]{3,2,1,0:T(8,128)(2,1)}, u32[]{:S(2)}) copy-start(bf16[1,8,101,256]{3,2,1,0:T(8,128)(2,1)} %get-tuple-element.31) | copy-start | bytes 1241092
  189.4 10.5 %copy-start.16 = (bf16[1,8,101,256]{3,2,1,0:T(8,128)(2,1)S(1)}, bf16[1,8,101,256]{3,2,1,0:T(8,128)(2,1)}, u32[]{:S(2)}) copy-start(bf16[1,8,101,256]{3,2,1,0:T(8,128)(2,1)} %get-tuple-element.63) | copy-start | bytes 1241092
  197.0 8.2 %copy-start.15 = (bf16[1,8,101,256]{3,2,1,0:T(8,128)(2,1)S(1)}, bf16[1,8,101,256]{3,2,1,0:T(8,128)(2,1)}, u32[]{:S(2)}) copy-start(bf16[1,8,101,256]{3,2,1,0:T(8,128)(2,1)} %get-tuple-element.59) | copy-start | bytes 1241092
  197.0 11.5 %copy-start.14 = (bf16[1,8,101,256]{3,2,1,0:T(8,128)(2,1)S(1)}, bf16[1,8,101,256]{3,2,1,0:T(8,128)(2,1)}, u32[]{:S(2)}) copy-start(bf16[1,8,101,256]{3,2,1,0:T(8,128)(2,1)} %get-tuple-element.32) | copy-start | bytes 1241092
  197.9 10.6 %collective-permute-start.9 = (bf16[8,101,256]{2,0,1:T(8,128)(2,1)S(1)}, bf16[8,101,256]{2,0,1:T(8,128)(2,1)S(1)}, u32[]{:S(2)}, u32[]{:S(2)}) collective-permute-start(bf16[8,101,256]{2,0,1:T(8,128)(2,1)S(1)} %bitcast.148), channel_id=1, source_target_pairs={{3,2},{7,6},{11,10},{15,14},{19,18},{23,22},{27,26},{31,30}} | collective-permute-start | bytes 1241096 | tf_op jit(solution)/shard_map/ppermute | solution.py:131
  198.6 43.3 %collective-permute-start.6 = (bf16[8,101,256]{2,0,1:T(8,128)(2,1)}, bf16[8,101,256]{2,0,1:T(8,128)(2,1)S(1)}, u32[]{:S(2)}, u32[]{:S(2)}) collective-permute-start(bf16[8,101,256]{2,0,1:T(8,128)(2,1)} %bitcast.129), channel_id=1, source_target_pairs={{0,1},{4,5},{8,9},{12,13},{16,17},{20,21},{24,25},{28,29}} | collective-permute-start | bytes 1241096 | tf_op jit(solution)/shard_map/ppermute | solution.py:130
  201.8 44.5 %collective-permute-start.1 = (bf16[8,101,256]{2,0,1:T(8,128)(2,1)}, bf16[8,101,256]{2,0,1:T(8,128)(2,1)}, u32[]{:S(2)}, u32[]{:S(2)}) collective-permute-start(bf16[8,101,256]{2,0,1:T(8,128)(2,1)} %fusion.20), channel_id=1, source_target_pairs={{0,1},{1,2},{4,5},{5,6},{8,9},{9,10},{12,13},{13,14},{16,17},{17,1... | collective-permute-start | bytes 1241096 | tf_op jit(solution)/shard_map/ppermute | solution.py:130
  205.2 36.7 %copy-start.13 = (bf16[1,8,101,256]{3,2,1,0:T(8,128)(2,1)S(1)}, bf16[1,8,101,256]{3,2,1,0:T(8,128)(2,1)}, u32[]{:S(2)}) copy-start(bf16[1,8,101,256]{3,2,1,0:T(8,128)(2,1)} %get-tuple-element.28) | copy-start | bytes 1241092
  207.2 42.9 %collective-permute-start.4 = (bf16[8,101,256]{2,0,1:T(8,128)(2,1)}, bf16[8,101,256]{2,0,1:T(8,128)(2,1)}, u32[]{:S(2)}, u32[]{:S(2)}) collective-permute-start(bf16[8,101,256]{2,0,1:T(8,128)(2,1)} %fusion.18), channel_id=1, source_target_pairs={{3,2},{2,1},{7,6},{6,5},{11,10},{10,9},{15,14},{14,13},{19,18},{18... | collective-permute-start | bytes 1241096 | tf_op jit(solution)/shard_map/ppermute | solution.py:131
  208.5 37.8 %copy-start.12 = (bf16[1,8,101,256]{3,2,1,0:T(8,128)(2,1)S(1)}, bf16[1,8,101,256]{3,2,1,0:T(8,128)(2,1)}, u32[]{:S(2)}) copy-start(bf16[1,8,101,256]{3,2,1,0:T(8,128)(2,1)} %get-tuple-element.62) | copy-start | bytes 1241092
  209.4 40.7 %copy-start.11 = (bf16[1,8,101,256]{3,2,1,0:T(8,128)(2,1)S(1)}, bf16[1,8,101,256]{3,2,1,0:T(8,128)(2,1)}, u32[]{:S(2)}) copy-start(bf16[1,8,101,256]{3,2,1,0:T(8,128)(2,1)} %get-tuple-element.64) | copy-start | bytes 1241092
  209.4 47.3 %collective-permute-start.10 = (bf16[8,101,256]{2,0,1:T(8,128)(2,1)}, bf16[8,101,256]{2,0,1:T(8,128)(2,1)}, u32[]{:S(2)}, u32[]{:S(2)}) collective-permute-start(bf16[8,101,256]{2,0,1:T(8,128)(2,1)} %fusion.12), channel_id=1, source_target_pairs={{3,2},{2,1},{7,6},{6,5},{11,10},{10,9},{15,14},{14,13},{19,18},{18... | collective-permute-start | bytes 1241096 | tf_op jit(solution)/shard_map/ppermute | solution.py:131
  242.8 17.7 %copy-start.5 = (bf16[250,32,128]{2,1,0:T(8,128)(2,1)S(1)}, bf16[250,32,128]{2,1,0:T(8,128)(2,1)}, u32[]{:S(2)}) copy-start(bf16[250,32,128]{2,1,0:T(8,128)(2,1)} %all-reduce.9.cloned.1.call-done.source_ref) | copy-start | bytes 6144004
  242.8 79.8 %collective-permute-start.7 = (bf16[8,101,256]{2,0,1:T(8,128)(2,1)}, bf16[8,101,256]{2,0,1:T(8,128)(2,1)}, u32[]{:S(2)}, u32[]{:S(2)}) collective-permute-start(bf16[8,101,256]{2,0,1:T(8,128)(2,1)} %fusion.14), channel_id=1, source_target_pairs={{0,1},{1,2},{4,5},{5,6},{8,9},{9,10},{12,13},{13,14},{16,17},{17,1... | collective-permute-start | bytes 1241096 | tf_op jit(solution)/shard_map/ppermute | solution.py:130
  248.2 78.4 %collective-permute-start.2 = (bf16[8,101,256]{2,0,1:T(8,128)(2,1)}, bf16[8,101,256]{2,0,1:T(8,128)(2,1)}, u32[]{:S(2)}, u32[]{:S(2)}) collective-permute-start(bf16[8,101,256]{2,0,1:T(8,128)(2,1)} %fusion.21), channel_id=1, source_target_pairs={{0,1},{1,2},{2,3},{4,5},{5,6},{6,7},{8,9},{9,10},{10,11},{12,13},{... | collective-permute-start | bytes 1241096 | tf_op jit(solution)/shard_map/ppermute | solution.py:130
  252.0 75.3 %collective-permute-start.5 = (bf16[8,101,256]{2,0,1:T(8,128)(2,1)}, bf16[8,101,256]{2,0,1:T(8,128)(2,1)}, u32[]{:S(2)}, u32[]{:S(2)}) collective-permute-start(bf16[8,101,256]{2,0,1:T(8,128)(2,1)} %fusion.19), channel_id=1, source_target_pairs={{3,2},{2,1},{1,0},{7,6},{6,5},{5,4},{11,10},{10,9},{9,8},{15,14},{... | collective-permute-start | bytes 1241096 | tf_op jit(solution)/shard_map/ppermute | solution.py:131
  258.6 117.9 %collective-permute-start.11 = (bf16[8,101,256]{2,0,1:T(8,128)(2,1)}, bf16[8,101,256]{2,0,1:T(8,128)(2,1)S(1)}, u32[]{:S(2)}, u32[]{:S(2)}) collective-permute-start(bf16[8,101,256]{2,0,1:T(8,128)(2,1)} %fusion.13), channel_id=1, source_target_pairs={{3,2},{2,1},{1,0},{7,6},{6,5},{5,4},{11,10},{10,9},{9,8},{15,14},{... | collective-permute-start | bytes 1241096 | tf_op jit(solution)/shard_map/ppermute | solution.py:131
  305.6 1.6 copy-start.8
  321.3 14.4 %collective-permute-start.12 = (bf16[8,101,256]{2,0,1:T(8,128)(2,1)S(1)}, bf16[8,101,256]{2,0,1:T(8,128)(2,1)S(1)}, u32[]{:S(2)}, u32[]{:S(2)}) collective-permute-start(bf16[8,101,256]{2,0,1:T(8,128)(2,1)S(1)} %bitcast.145), channel_id=1, source_target_pairs={{0,1},{4,5},{8,9},{12,13},{16,17},{20,21},{24,25},{28,29}} | collective-permute-start | bytes 1241096 | tf_op jit(solution)/shard_map/ppermute | solution.py:130
  323.7 56.7 %collective-permute-start.8 = (bf16[8,101,256]{2,0,1:T(8,128)(2,1)S(1)}, bf16[8,101,256]{2,0,1:T(8,128)(2,1)S(1)}, u32[]{:S(2)}, u32[]{:S(2)}) collective-permute-start(bf16[8,101,256]{2,0,1:T(8,128)(2,1)S(1)} %fusion.15), channel_id=1, source_target_pairs={{0,1},{1,2},{2,3},{4,5},{5,6},{6,7},{8,9},{9,10},{10,11},{12,13},{... | collective-permute-start | bytes 1241096 | tf_op jit(solution)/shard_map/ppermute | solution.py:130
  326.6 10.5 %collective-permute-start.15 = (bf16[8,101,256]{2,0,1:T(8,128)(2,1)S(1)}, bf16[8,101,256]{2,0,1:T(8,128)(2,1)S(1)}, u32[]{:S(2)}, u32[]{:S(2)}) collective-permute-start(bf16[8,101,256]{2,0,1:T(8,128)(2,1)S(1)} %bitcast.147), channel_id=1, source_target_pairs={{3,2},{7,6},{11,10},{15,14},{19,18},{23,22},{27,26},{31,30}} | collective-permute-start | bytes 1241096 | tf_op jit(solution)/shard_map/ppermute | solution.py:131
  328.8 15.7 %collective-permute-start.21 = (bf16[8,101,256]{2,0,1:T(8,128)(2,1)S(1)}, bf16[8,101,256]{2,0,1:T(8,128)(2,1)S(1)}, u32[]{:S(2)}, u32[]{:S(2)}) collective-permute-start(bf16[8,101,256]{2,0,1:T(8,128)(2,1)S(1)} %bitcast.149), channel_id=1, source_target_pairs={{3,2},{7,6},{11,10},{15,14},{19,18},{23,22},{27,26},{31,30}} | collective-permute-start | bytes 1241096 | tf_op jit(solution)/shard_map/ppermute | solution.py:131
  335.7 17.7 %collective-permute-start.18 = (bf16[8,101,256]{2,0,1:T(8,128)(2,1)S(1)}, bf16[8,101,256]{2,0,1:T(8,128)(2,1)S(1)}, u32[]{:S(2)}, u32[]{:S(2)}) collective-permute-start(bf16[8,101,256]{2,0,1:T(8,128)(2,1)S(1)} %bitcast.146), channel_id=1, source_target_pairs={{0,1},{4,5},{8,9},{12,13},{16,17},{20,21},{24,25},{28,29}} | collective-permute-start | bytes 1241096 | tf_op jit(solution)/shard_map/ppermute | solution.py:130
  337.1 23.0 %collective-permute-start.13 = (bf16[8,101,256]{2,0,1:T(8,128)(2,1)S(1)}, bf16[8,101,256]{2,0,1:T(8,128)(2,1)S(1)}, u32[]{:S(2)}, u32[]{:S(2)}) collective-permute-start(bf16[8,101,256]{2,0,1:T(8,128)(2,1)S(1)} %fusion.8), channel_id=1, source_target_pairs={{0,1},{1,2},{4,5},{5,6},{8,9},{9,10},{12,13},{13,14},{16,17},{17,1... | collective-permute-start | bytes 1241096 | tf_op jit(solution)/shard_map/ppermute | solution.py:130
  344.5 17.6 %collective-permute-start.16 = (bf16[8,101,256]{2,0,1:T(8,128)(2,1)S(1)}, bf16[8,101,256]{2,0,1:T(8,128)(2,1)S(1)}, u32[]{:S(2)}, u32[]{:S(2)}) collective-permute-start(bf16[8,101,256]{2,0,1:T(8,128)(2,1)S(1)} %fusion.6), channel_id=1, source_target_pairs={{3,2},{2,1},{7,6},{6,5},{11,10},{10,9},{15,14},{14,13},{19,18},{18... | collective-permute-start | bytes 1241096 | tf_op jit(solution)/shard_map/ppermute | solution.py:131
  353.4 13.5 %collective-permute-start.22 = (bf16[8,101,256]{2,0,1:T(8,128)(2,1)S(1)}, bf16[8,101,256]{2,0,1:T(8,128)(2,1)S(1)}, u32[]{:S(2)}, u32[]{:S(2)}) collective-permute-start(bf16[8,101,256]{2,0,1:T(8,128)(2,1)S(1)} %fusion), channel_id=1, source_target_pairs={{3,2},{2,1},{7,6},{6,5},{11,10},{10,9},{15,14},{14,13},{19,18},{18... | collective-permute-start | bytes 1241096 | tf_op jit(solution)/shard_map/ppermute | solution.py:131
  360.1 14.4 %collective-permute-start.19 = (bf16[8,101,256]{2,0,1:T(8,128)(2,1)S(1)}, bf16[8,101,256]{2,0,1:T(8,128)(2,1)S(1)}, u32[]{:S(2)}, u32[]{:S(2)}) collective-permute-start(bf16[8,101,256]{2,0,1:T(8,128)(2,1)S(1)} %fusion.2), channel_id=1, source_target_pairs={{0,1},{1,2},{4,5},{5,6},{8,9},{9,10},{12,13},{13,14},{16,17},{17,1... | collective-permute-start | bytes 1241096 | tf_op jit(solution)/shard_map/ppermute | solution.py:130
  362.1 21.2 %collective-permute-start.14 = (bf16[8,101,256]{2,0,1:T(8,128)(2,1)S(1)}, bf16[8,101,256]{2,0,1:T(8,128)(2,1)S(1)}, u32[]{:S(2)}, u32[]{:S(2)}) collective-permute-start(bf16[8,101,256]{2,0,1:T(8,128)(2,1)S(1)} %fusion.9), channel_id=1, source_target_pairs={{0,1},{1,2},{2,3},{4,5},{5,6},{6,7},{8,9},{9,10},{10,11},{12,13},{... | collective-permute-start | bytes 1241096 | tf_op jit(solution)/shard_map/ppermute | solution.py:130
  367.0 16.4 %collective-permute-start.17 = (bf16[8,101,256]{2,0,1:T(8,128)(2,1)S(1)}, bf16[8,101,256]{2,0,1:T(8,128)(2,1)S(1)}, u32[]{:S(2)}, u32[]{:S(2)}) collective-permute-start(bf16[8,101,256]{2,0,1:T(8,128)(2,1)S(1)} %fusion.7), channel_id=1, source_target_pairs={{3,2},{2,1},{1,0},{7,6},{6,5},{5,4},{11,10},{10,9},{9,8},{15,14},{... | collective-permute-start | bytes 1241096 | tf_op jit(solution)/shard_map/ppermute | solution.py:131
  374.4 11.7 %collective-permute-start.23 = (bf16[8,101,256]{2,0,1:T(8,128)(2,1)S(1)}, bf16[8,101,256]{2,0,1:T(8,128)(2,1)S(1)}, u32[]{:S(2)}, u32[]{:S(2)}) collective-permute-start(bf16[8,101,256]{2,0,1:T(8,128)(2,1)S(1)} %fusion.1), channel_id=1, source_target_pairs={{3,2},{2,1},{1,0},{7,6},{6,5},{5,4},{11,10},{10,9},{9,8},{15,14},{... | collective-permute-start | bytes 1241096 | tf_op jit(solution)/shard_map/ppermute | solution.py:131
  376.5 12.5 %collective-permute-start.20 = (bf16[8,101,256]{2,0,1:T(8,128)(2,1)S(1)}, bf16[8,101,256]{2,0,1:T(8,128)(2,1)S(1)}, u32[]{:S(2)}, u32[]{:S(2)}) collective-permute-start(bf16[8,101,256]{2,0,1:T(8,128)(2,1)S(1)} %fusion.3), channel_id=1, source_target_pairs={{0,1},{1,2},{2,3},{4,5},{5,6},{6,7},{8,9},{9,10},{10,11},{12,13},{... | collective-permute-start | bytes 1241096 | tf_op jit(solution)/shard_map/ppermute | solution.py:130
  (3 other events, 2.0 us)
Sparse Core Ops, SparseCore 0:
  35.2 62.5 all-reduce.4
  101.1 60.6 all-reduce.6
  181.1 60.7 all-reduce.8
  245.0 60.6 all-reduce.10

commit v3 on v2

--- a/solution.py
+++ b/solution.py
@@ -11,7 +11,8 @@
 
 LAGS = 101
 SRC_BLK = 64
-ROWS = (8, 8, 8, 8)
+ROWS = (16, 16)
+PAD = 256
 MIB = 1024 * 1024
 
 
@@ -44,7 +45,7 @@
             pl.BlockSpec((bins, depth, width), lambda i: (i, 0, 0)),
         ],
         out_specs=pl.BlockSpec((bins, rows, depth), lambda i: (i, 0, 0)),
-        out_shape=jax.ShapeDtypeStruct((bin_count, rows, depth), jnp.bfloat16),
+        out_shape=jax.ShapeDtypeStruct((-(-bin_count // PAD) * PAD, rows, depth), jnp.bfloat16),
         compiler_params=pltpu.CompilerParams(vmem_limit_bytes=32 * MIB),
         cost_estimate=pl.CostEstimate(
             flops=2 * bin_count * rows * width * depth,
@@ -90,8 +91,8 @@
 
 
 def correlate(sign, table, sources, x, bins):
-    bin_count, rows, depth = sources.shape
-    width = x.shape[2]
+    _, rows, depth = sources.shape
+    bin_count, _, width = x.shape
     stride = -(-2 * bin_count // 8) * 8
     return pl.pallas_call(
         functools.partial(correlate_kernel, stride, bin_count),
@@ -118,6 +119,45 @@
     return (a.astype(jnp.float32) + b.astype(jnp.float32)).astype(jnp.bfloat16)
 
 
+def swap(x, axis, bit):
+    return lax.ppermute(x, axis, [(i, i ^ (1 << bit)) for i in range(lax.axis_size(axis))])
+
+
+def halve(current, axis, bits):
+    for bit in bits:
+        side = (lax.axis_index(axis) >> bit) & 1
+        length = current.shape[0] // 2
+        sent = lax.dynamic_slice_in_dim(current, (1 - side) * length, length, 0)
+        kept = lax.dynamic_slice_in_dim(current, side * length, length, 0)
+        current = add(kept, swap(sent, axis, bit))
+    return current
+
+
+def double(current, axis, bits):
+    for bit in reversed(bits):
+        side = (lax.axis_index(axis) >> bit) & 1
+        other = swap(current, axis, bit)
+        low, high = jnp.where(side == 0, current, other), jnp.where(side == 0, other, current)
+        current = jnp.concatenate([low, high], axis=0)
+    return current
+
+
+def sum_of_chan(mine, after):
+    bit_count = (lax.axis_size("chan") - 1).bit_length()
+    length = mine.shape[0] // 2
+    orders = [list(range(1, bit_count)), list(range(1, bit_count))[::-1]]
+    parts = [halve(mine[:length], "chan", [0]), halve(mine[length:], "chan", [0])]
+    if after is not None:
+        parts, after = lax.optimization_barrier((parts, after))
+    parts = [halve(part, "chan", order) for part, order in zip(parts, orders)]
+    parts = [double(part, "chan", order) for part, order in zip(parts, orders)]
+    return parts, after
+
+
+def finish(parts):
+    return jnp.concatenate([double(part, "chan", [0]) for part in parts], axis=0)
+
+
 def chain_scatter(parts, axis):
     n, at = lax.axis_size(axis), lax.axis_index(axis)
     total = None
@@ -156,21 +196,20 @@
         return (channel[:, None] == jnp.arange(width, dtype=jnp.int32)[None, :]).astype(jnp.bfloat16)
 
     x = spectra.transpose(2, 1, 0, 3).reshape(bin_count, depth, width)
-    pieces = []
-    source = None
+    summed = []
+    after = None
     first = 0
     for rows in ROWS:
         mine = pick_sources(pick_of(first, rows), keep, x, 25)
-        if source is not None:
-            mine, source = lax.optimization_barrier((mine, source))
-        if source is not None:
-            pieces.append(source)
-        source = lax.psum(mine, "chan")
+        parts, after = sum_of_chan(mine, after)
+        if after is not None:
+            summed.append(after)
+        after = parts
         first += rows
-    pieces.append(source)
+    summed.append(after)
     outs = []
-    for rows, source in zip(ROWS, pieces):
-        partial_value = correlate(sign, table, source, x, 25)
+    for rows, parts in zip(ROWS, summed):
+        partial_value = correlate(sign, table, finish(parts), x, 25)
         outs.append(chain_scatter(partial_value.reshape(tm_count, rows, LAGS, width), "tm"))
     return jnp.concatenate(outs, axis=0)
 

time: 399 us -> 291 us (0.73)
  waiting for transfers between devices: 180 us -> 123 us
  Pallas kernels: 83.7 us -> 52.8 us
  between operations: 13.7 us -> 0.7 us
  starting transfers between devices: 52.1 us -> 42.5 us
  other arithmetic: 19.4 us -> 26.6 us
  local copies, waits for them, and re-layouts: 47.8 us -> 43.5 us
    psum x4 -> x0, waiting for transfers between devices: 146 us -> none  [body(): source = lax.psum(mine, 'chan')]
    ppermute x0 -> x24, waiting for transfers between devices: none -> 59.1 us  [swap(): lax.ppermute(x, axis, [(i, i ^ 1 << bit) for i in range(lax.axis_size(axi...]
    ppermute x12 -> x6, waiting for transfers between devices: 30 us -> 61.4 us  [chain_scatter(): from_left = lax.ppermute(to_right, axis, [(i, i + 1) for i in range(t + 1)])]
    pallas_call x4 -> x2, Pallas kernels: 54.3 us -> 36.2 us  [correlate(): pl.pallas_call(functools.partial(correlate_kernel, stride, bin_count), gr...]
    unnamed x46 -> x28, local copies, waits for them, and re-layouts: 29.7 us -> 11.9 us
    ppermute x0 -> x24, starting transfers between devices: none -> 13 us  [swap(): lax.ppermute(x, axis, [(i, i ^ 1 << bit) for i in range(lax.axis_size(axi...]
    pallas_call x4 -> x2, Pallas kernels: 29.5 us -> 16.6 us  [pick_sources(): pl.pallas_call(pick_kernel, grid=(bin_count // bins,), in_specs=[pl.Block...]
    ppermute x12 -> x6, starting transfers between devices: 19.1 us -> 7.84 us  [chain_scatter(): lax.ppermute(to_left, axis, [(n - 1 - i, n - 2 - i) for i in range(t + 1)])]
  transfers between devices with their start and end apart: 28 -> 36, of which waited for: 12 -> 21; matrix products, arithmetic and copies ran while one was open for 4% -> 11% of each run, Pallas kernels for 16% -> 15%
where the time goes in v3:
time: 291 us; the launch traced here: 289 us
  waiting for transfers between devices  123 us (42%)
  Pallas kernels  52.8 us (18%)
  local copies, waits for them, and re-layouts  43.5 us (15%)
  starting transfers between devices  42.5 us (15%)
  other arithmetic  26.6 us (9%)
    ppermute x6, waiting for transfers between devices, chain_scatter(): from_left = lax.ppermute(to_right, axis, [(i, i + 1) for i in range(t + 1)])  61.4 us
    ppermute x24, waiting for transfers between devices, swap(): lax.ppermute(x, axis, [(i, i ^ 1 << bit) for i in range(lax.axis_size(axi...  59.1 us
    pallas_call x2, Pallas kernels, correlate(): pl.pallas_call(functools.partial(correlate_kernel, stride, bin_count), gr...  36.2 us
    ppermute x6, starting transfers between devices, chain_scatter(): from_left = lax.ppermute(to_right, axis, [(i, i + 1) for i in range(t + 1)])  21.6 us
    pallas_call x2, Pallas kernels, pick_sources(): pl.pallas_call(pick_kernel, grid=(bin_count // bins,), in_specs=[pl.Block...  16.6 us
    transpose x1, local copies, waits for them, and re-layouts, body(): x = spectra.transpose(2, 1, 0, 3).reshape(bin_count, depth, width)  16.6 us
    convert_element_type x20, other arithmetic, add(): return (a.astype(jnp.float32) + b.astype(jnp.float32)).astype(jnp.bfloat16)  14.7 us
    ppermute x24, starting transfers between devices, swap(): lax.ppermute(x, axis, [(i, i ^ 1 << bit) for i in range(lax.axis_size(axi...  13 us
  transfers between devices with their start and end apart: 36, of which 21 were waited for; matrix products, arithmetic and copies ran while one was open for 11% of the time, Pallas kernels for 15%

profile of v3, /device:TPU:8, one launch (start us, length us, event | category | flops | bytes accessed | tf_op | source)
XLA Modules:
  0.0 289.1 jit_solution(15179238559496436631)
XLA Ops:
  0.0 1.3 fusion.16
  2.1 16.6 %copy.12 = bf16[250,2,64,256]{3,2,1,0:T(8,128)(2,1)} copy(bf16[250,2,64,256]{3,1,0,2:T(2,128)(2,1)} %bitcast.74) | data formatting | bytes 32768000 | tf_op jit(solution)/shard_map/transpose | solution.py:198
  20.0 5.6 %copy-done = bf16[250,2,64,256]{3,2,1,0:T(8,128)(2,1)S(1)} copy-done((bf16[250,2,64,256]{3,2,1,0:T(8,128)(2,1)S(1)}, bf16[250,2,64,256]{3,2,1,0:T(8,128)(2,1)}, u32[]{:S(2)}) %copy-start) | copy-done | bytes 16384024
  25.7 8.3 %shard_map.110 = bf16[256,64,128]{2,1,0:T(8,128)(2,1)S(1)} custom-call(bf16[64,256]{1,0:T(8,128)(2,1)S(1)} %get-tuple-element.60.pick_ref, f32[1,128]{1,0:T(1,128)S(1)} %broadcast_in_dim_tile.3.keep_ref, bf16[250,128,256]{2,1,0:T(8,128)(2,1)S(1)} %bitcast.70), custom_call_target="tpu_custom_call" | custom-call | flops 1048576000 | bytes 20480000 | tf_op jit(solution)/shard_map/pallas_call | solution.py:39
  34.0 2.3 fusion.14
  36.3 2.0 constant_dynamic-slice_fusion.23
  40.0 5.7 %copy-done.1 = bf16[250,2,64,256]{3,2,1,0:T(8,128)(2,1)S(1)} copy-done((bf16[250,2,64,256]{3,2,1,0:T(8,128)(2,1)S(1)}, bf16[250,2,64,256]{3,2,1,0:T(8,128)(2,1)}, u32[]{:S(2)}) %copy-start.1) | copy-done | bytes 16384024
  45.6 8.3 %shard_map.109 = bf16[256,64,128]{2,1,0:T(8,128)(2,1)S(1)} custom-call(bf16[64,256]{1,0:T(8,128)(2,1)S(1)} %get-tuple-element.59.pick_ref, f32[1,128]{1,0:T(1,128)S(1)} %broadcast_in_dim_tile.3.keep_ref, bf16[250,128,256]{2,1,0:T(8,128)(2,1)S(1)} %bitcast.71), custom_call_target="tpu_custom_call" | custom-call | flops 1048576000 | bytes 20480000 | tf_op jit(solution)/shard_map/pallas_call | solution.py:39
  55.6 2.4 add_convert_fusion.1
  58.9 1.5 collective-permute-start.3
  60.4 1.6 add_convert_fusion
  63.0 1.5 collective-permute-start.8
  67.1 6.0 %collective-permute-done.3 = bf16[32,64,128]{2,1,0:T(8,128)(2,1)} collective-permute-done((bf16[32,64,128]{2,1,0:T(8,128)(2,1)}, bf16[32,64,128]{2,1,0:T(8,128)(2,1)}, u32[]{:S(2)}, u32[]{:S(2)}) %collective-permute-start.3) | collective-permute-done | bytes 524320 | tf_op jit(solution)/shard_map/ppermute | solution.py:123
  74.4 1.6 collective-permute-start.4
  76.0 1.4 collective-permute-done.8
  78.8 3.6 %collective-permute-done.4 = bf16[16,64,128]{2,1,0:T(8,128)(2,1)S(1)} collective-permute-done((bf16[16,64,128]{2,1,0:T(8,128)(2,1)S(1)}, bf16[16,64,128]{2,1,0:T(8,128)(2,1)S(1)}, u32[]{:S(2)}, u32[]{:S(2)}) %collective-permute-start.4) | collective-permute-done | bytes 262176 | tf_op jit(solution)/shard_map/ppermute | solution.py:123
  82.5 1.6 collective-permute-start.5
  84.1 1.6 add_convert_fusion.3
  86.8 2.7 collective-permute-done.5
  90.1 4.9 %collective-permute-done.10 = bf16[16,64,128]{2,1,0:T(8,128)(2,1)S(1)} collective-permute-done((bf16[16,64,128]{2,1,0:T(8,128)(2,1)S(1)}, bf16[16,64,128]{2,1,0:T(8,128)(2,1)S(1)}, u32[]{:S(2)}, u32[]{:S(2)}) %collective-permute-start.10) | collective-permute-done | bytes 262176 | tf_op jit(solution)/shard_map/ppermute | solution.py:123
  95.2 1.6 add_convert_fusion.2
  96.9 7.0 %collective-permute-done.6 = bf16[32,64,128]{2,1,0:T(8,128)(2,1)S(1)} collective-permute-done((bf16[32,64,128]{2,1,0:T(8,128)(2,1)S(1)}, bf16[32,64,128]{2,1,0:T(8,128)(2,1)S(1)}, u32[]{:S(2)}, u32[]{:S(2)}) %collective-permute-start.6) | collective-permute-done | bytes 524320 | tf_op jit(solution)/shard_map/ppermute | solution.py:123
  105.9 9.9 %collective-permute-done.25 = bf16[32,64,128]{2,1,0:T(8,128)(2,1)S(1)} collective-permute-done((bf16[32,64,128]{2,1,0:T(8,128)(2,1)S(1)}, bf16[32,64,128]{2,1,0:T(8,128)(2,1)S(1)}, u32[]{:S(2)}, u32[]{:S(2)}) %collective-permute-start.25) | collective-permute-done | bytes 524320 | tf_op jit(solution)/shard_map/ppermute | solution.py:123
  116.8 2.2 collective-permute-done.20
  119.9 3.1 %collective-permute-done.26 = bf16[16,64,128]{2,1,0:T(8,128)(2,1)} collective-permute-done((bf16[16,64,128]{2,1,0:T(8,128)(2,1)S(1)}, bf16[16,64,128]{2,1,0:T(8,128)(2,1)}, u32[]{:S(2)}, u32[]{:S(2)}) %collective-permute-start.26) | collective-permute-done | bytes 262176 | tf_op jit(solution)/shard_map/ppermute | solution.py:123
  124.3 3.0 %collective-permute-done.21 = bf16[16,64,128]{2,1,0:T(8,128)(2,1)} collective-permute-done((bf16[16,64,128]{2,1,0:T(8,128)(2,1)}, bf16[16,64,128]{2,1,0:T(8,128)(2,1)}, u32[]{:S(2)}, u32[]{:S(2)}) %collective-permute-start.21) | collective-permute-done | bytes 262176 | tf_op jit(solution)/shard_map/ppermute | solution.py:123
  128.4 1.4 broadcast_select_fusion.5
  130.5 1.4 collective-permute-start.28
  132.0 5.7 %collective-permute-done.22 = bf16[16,64,128]{2,1,0:T(8,128)(2,1)S(1)} collective-permute-done((bf16[16,64,128]{2,1,0:T(8,128)(2,1)S(1)}, bf16[16,64,128]{2,1,0:T(8,128)(2,1)S(1)}, u32[]{:S(2)}, u32[]{:S(2)}) %collective-permute-start.22) | collective-permute-done | bytes 262176 | tf_op jit(solution)/shard_map/ppermute | solution.py:123
  138.1 6.0 %collective-permute-done.28 = bf16[32,64,128]{2,1,0:T(8,128)(2,1)S(1)} collective-permute-done((bf16[32,64,128]{2,1,0:T(8,128)(2,1)S(1)}, bf16[32,64,128]{2,1,0:T(8,128)(2,1)S(1)}, u32[]{:S(2)}, u32[]{:S(2)}) %collective-permute-start.28) | collective-permute-done | bytes 524320 | tf_op jit(solution)/shard_map/ppermute | solution.py:123
  144.4 2.6 collective-permute-done.23
  147.3 2.3 pad_maximum_fusion.source_ref
  149.6 18.2 %shard_map.111 = bf16[64,101,256]{2,1,0:T(8,128)(2,1)S(1)} custom-call(bf16[1,128]{1,0:T(2,128)(2,1)S(1)} %copy-done.3, bf16[112,500]{1,0:T(8,128)(2,1)S(1)} %copy-done.2, bf16[256,64,128]{2,1,0:T(8,128)(2,1)} %pad_maximum_fusion.source_ref, bf16[250,128,256]{2,1,0:T(8,128)(2,1)} %bitcast.68), custom_call_target="tpu_custom_call" | custom-call | flops 3751936000 | bytes 23789568 | tf_op jit(solution)/shard_map/pallas_call | solution.py:97
  171.8 2.3 pad_maximum_fusion.1.source_ref
  174.1 18.0 %shard_map.112 = bf16[64,101,256]{2,1,0:T(8,128)(2,1)S(1)} custom-call(bf16[1,128]{1,0:T(2,128)(2,1)S(1)} %copy-done.3, bf16[112,500]{1,0:T(8,128)(2,1)S(1)} %copy-done.2, bf16[256,64,128]{2,1,0:T(8,128)(2,1)} %pad_maximum_fusion.1.source_ref, bf16[250,128,256]{2,1,0:T(8,128)(2,1)} %bitcast.69), custom_call_target="tpu_custom_call" | custom-call | flops 3751936000 | bytes 23789568 | tf_op jit(solution)/shard_map/pallas_call | solution.py:97
  196.9 4.6 %collective-permute-start.15 = (bf16[16,101,256]{2,0,1:T(8,128)(2,1)S(1)}, bf16[16,101,256]{2,0,1:T(8,128)(2,1)S(1)}, u32[]{:S(2)}, u32[]{:S(2)}) collective-permute-start(bf16[16,101,256]{2,0,1:T(8,128)(2,1)S(1)} %fusion.8), channel_id=1, source_target_pairs={{0,1},{1,2},{4,5},{5,6},{8,9},{9,10},{12,13},{13,14},{16,17},{17,1... | collective-permute-start | bytes 2482184 | tf_op jit(solution)/shard_map/ppermute | solution.py:170
  203.1 13.8 %collective-permute-done.30 = bf16[16,101,256]{2,0,1:T(8,128)(2,1)S(1)} collective-permute-done((bf16[16,101,256]{2,0,1:T(8,128)(2,1)S(1)}, bf16[16,101,256]{2,0,1:T(8,128)(2,1)S(1)}, u32[]{:S(2)}, u32[]{:S(2)}) %collective-permute-start.30) | collective-permute-done | bytes 827424 | tf_op jit(solution)/shard_map/ppermute | solution.py:170
  217.1 4.8 %collective-permute-start.31 = (bf16[16,101,256]{2,0,1:T(8,128)(2,1)S(1)}, bf16[16,101,256]{2,0,1:T(8,128)(2,1)S(1)}, u32[]{:S(2)}, u32[]{:S(2)}) collective-permute-start(bf16[16,101,256]{2,0,1:T(8,128)(2,1)S(1)} %fusion.2), channel_id=1, source_target_pairs={{0,1},{1,2},{4,5},{5,6},{8,9},{9,10},{12,13},{13,14},{16,17},{17,1... | collective-permute-start | bytes 2482184 | tf_op jit(solution)/shard_map/ppermute | solution.py:170
  222.3 1.9 collective-permute-start.19
  224.2 10.4 %collective-permute-done.15 = bf16[16,101,256]{2,0,1:T(8,128)(2,1)S(1)} collective-permute-done((bf16[16,101,256]{2,0,1:T(8,128)(2,1)S(1)}, bf16[16,101,256]{2,0,1:T(8,128)(2,1)S(1)}, u32[]{:S(2)}, u32[]{:S(2)}) %collective-permute-start.15) | collective-permute-done | bytes 827424 | tf_op jit(solution)/shard_map/ppermute | solution.py:170
  234.9 4.8 %collective-permute-start.16 = (bf16[16,101,256]{2,0,1:T(8,128)(2,1)S(1)}, bf16[16,101,256]{2,0,1:T(8,128)(2,1)S(1)}, u32[]{:S(2)}, u32[]{:S(2)}) collective-permute-start(bf16[16,101,256]{2,0,1:T(8,128)(2,1)S(1)} %fusion.9), channel_id=1, source_target_pairs={{0,1},{1,2},{2,3},{4,5},{5,6},{6,7},{8,9},{9,10},{10,11},{12,13},{... | collective-permute-start | bytes 2482184 | tf_op jit(solution)/shard_map/ppermute | solution.py:170
  240.0 1.9 collective-permute-start.35
  242.0 10.4 %collective-permute-done.31 = bf16[16,101,256]{2,0,1:T(8,128)(2,1)S(1)} collective-permute-done((bf16[16,101,256]{2,0,1:T(8,128)(2,1)S(1)}, bf16[16,101,256]{2,0,1:T(8,128)(2,1)S(1)}, u32[]{:S(2)}, u32[]{:S(2)}) %collective-permute-start.31) | collective-permute-done | bytes 827424 | tf_op jit(solution)/shard_map/ppermute | solution.py:170
  252.6 4.8 %collective-permute-start.32 = (bf16[16,101,256]{2,0,1:T(8,128)(2,1)S(1)}, bf16[16,101,256]{2,0,1:T(8,128)(2,1)S(1)}, u32[]{:S(2)}, u32[]{:S(2)}) collective-permute-start(bf16[16,101,256]{2,0,1:T(8,128)(2,1)S(1)} %fusion.3), channel_id=1, source_target_pairs={{0,1},{1,2},{2,3},{4,5},{5,6},{6,7},{8,9},{9,10},{10,11},{12,13},{... | collective-permute-start | bytes 2482184 | tf_op jit(solution)/shard_map/ppermute | solution.py:170
  257.5 12.6 %collective-permute-done.16 = bf16[16,101,256]{2,0,1:T(8,128)(2,1)S(1)} collective-permute-done((bf16[16,101,256]{2,0,1:T(8,128)(2,1)S(1)}, bf16[16,101,256]{2,0,1:T(8,128)(2,1)S(1)}, u32[]{:S(2)}, u32[]{:S(2)}) %collective-permute-start.16) | collective-permute-done | bytes 827424 | tf_op jit(solution)/shard_map/ppermute | solution.py:170
  270.4 2.6 collective-permute-done.35
  273.0 14.3 %collective-permute-done.32 = bf16[16,101,256]{2,0,1:T(8,128)(2,1)S(1)} collective-permute-done((bf16[16,101,256]{2,0,1:T(8,128)(2,1)S(1)}, bf16[16,101,256]{2,0,1:T(8,128)(2,1)S(1)}, u32[]{:S(2)}, u32[]{:S(2)}) %collective-permute-start.32) | collective-permute-done | bytes 827424 | tf_op jit(solution)/shard_map/ppermute | solution.py:170
  287.7 1.4 pad_maximum_fusion.2
  (128 shorter events, 34.7 us)
Async XLA Ops:
  2.1 16.6 %copy-start.11 = (s32[64]{0:T(128)S(1)}, s32[64]{0:T(128)}, u32[]{:S(2)}) copy-start(s32[64]{0:T(128)} %constant.90.clone) | copy-start | bytes 772
  2.1 16.6 %copy-start.12 = (pred[64]{0:T(512)(128)(4,1)S(1)}, pred[64]{0:T(512)(128)(4,1)}, u32[]{:S(2)}) copy-start(pred[64]{0:T(512)(128)(4,1)} %constant.96) | copy-start | bytes 196
  2.1 16.6 %copy-start.13 = (s32[64]{0:T(128)S(1)}, s32[64]{0:T(128)}, u32[]{:S(2)}) copy-start(s32[64]{0:T(128)} %constant.91.clone) | copy-start | bytes 772
  20.0 5.7 %copy-start = (bf16[250,2,64,256]{3,2,1,0:T(8,128)(2,1)S(1)}, bf16[250,2,64,256]{3,2,1,0:T(8,128)(2,1)}, u32[]{:S(2)}) copy-start(bf16[250,2,64,256]{3,2,1,0:T(8,128)(2,1)} %copy.12) | copy-start | bytes 49152004
  36.3 3.2 %copy-start.6 = (bf16[128,64,128]{2,1,0:T(8,128)(2,1)}, bf16[128,64,128]{2,1,0:T(8,128)(2,1)S(1)}, u32[]{:S(2)}) copy-start(bf16[128,64,128]{2,1,0:T(8,128)(2,1)S(1)} %get-tuple-element.13) | copy-start | bytes 6291460
  38.4 16.7 %collective-permute-start.2 = (bf16[64,64,128]{2,1,0:T(8,128)(2,1)S(1)}, bf16[64,64,128]{2,1,0:T(8,128)(2,1)}, u32[]{:S(2)}, u32[]{:S(2)}) collective-permute-start(bf16[64,64,128]{2,1,0:T(8,128)(2,1)S(1)} %constant_dynamic-slice_fusion.23), channel_id=1, source_target_pairs={{0,4},{4,0},{8,12},{12,8},{16,20},{20,16},{24,28},{28,24},{1,5},{5... | collective-permute-start | bytes 3145736 | tf_op jit(solution)/shard_map/ppermute | solution.py:123
  39.5 20.9 %collective-permute-start.7 = (bf16[64,64,128]{2,1,0:T(8,128)(2,1)}, bf16[64,64,128]{2,1,0:T(8,128)(2,1)}, u32[]{:S(2)}, u32[]{:S(2)}) collective-permute-start(bf16[64,64,128]{2,1,0:T(8,128)(2,1)} %constant_dynamic-slice_fusion.20), channel_id=1, source_target_pairs={{0,4},{4,0},{8,12},{12,8},{16,20},{20,16},{24,28},{28,24},{1,5},{5... | collective-permute-start | bytes 3145736 | tf_op jit(solution)/shard_map/ppermute | solution.py:123
  40.0 5.7 %copy-start.1 = (bf16[250,2,64,256]{3,2,1,0:T(8,128)(2,1)S(1)}, bf16[250,2,64,256]{3,2,1,0:T(8,128)(2,1)}, u32[]{:S(2)}) copy-start(bf16[250,2,64,256]{3,2,1,0:T(8,128)(2,1)} %copy.12) | copy-start | bytes 49152004
  55.0 9.5 %copy-start.4 = (bf16[128,64,128]{2,1,0:T(8,128)(2,1)}, bf16[128,64,128]{2,1,0:T(8,128)(2,1)S(1)}, u32[]{:S(2)}) copy-start(bf16[128,64,128]{2,1,0:T(8,128)(2,1)S(1)} %get-tuple-element.16) | copy-start | bytes 6291460
  55.0 5.4 %copy-start.7 = (bf16[128,64,128]{2,1,0:T(8,128)(2,1)S(1)}, bf16[128,64,128]{2,1,0:T(8,128)(2,1)}, u32[]{:S(2)}) copy-start(bf16[128,64,128]{2,1,0:T(8,128)(2,1)} %copy-done.6) | copy-start | bytes 6291460
  58.9 14.2 %collective-permute-start.3 = (bf16[32,64,128]{2,1,0:T(8,128)(2,1)}, bf16[32,64,128]{2,1,0:T(8,128)(2,1)}, u32[]{:S(2)}, u32[]{:S(2)}) collective-permute-start(bf16[32,64,128]{2,1,0:T(8,128)(2,1)} %constant_dynamic-slice_fusion.22), channel_id=1, source_target_pairs={{0,8},{4,12},{8,0},{12,4},{16,24},{20,28},{24,16},{28,20},{1,9},{5... | collective-permute-start | bytes 1572872 | tf_op jit(solution)/shard_map/ppermute | solution.py:123
  62.1 4.5 %copy-start.9 = (bf16[64,64,128]{2,1,0:T(8,128)(2,1)}, bf16[64,64,128]{2,1,0:T(8,128)(2,1)S(1)}, u32[]{:S(2)}) copy-start(bf16[64,64,128]{2,1,0:T(8,128)(2,1)S(1)} %add_convert_fusion) | copy-start | bytes 3145732
  63.0 14.4 %collective-permute-start.8 = (bf16[32,64,128]{2,1,0:T(8,128)(2,1)}, bf16[32,64,128]{2,1,0:T(8,128)(2,1)}, u32[]{:S(2)}, u32[]{:S(2)}) collective-permute-start(bf16[32,64,128]{2,1,0:T(8,128)(2,1)} %constant_dynamic-slice_fusion.19), channel_id=1, source_target_pairs={{0,16},{4,20},{8,24},{12,28},{16,0},{20,4},{24,8},{28,12},{1,17},{... | collective-permute-start | bytes 1572872 | tf_op jit(solution)/shard_map/ppermute | solution.py:123
  65.6 18.5 %collective-permute-start = (bf16[64,64,128]{2,1,0:T(8,128)(2,1)}, bf16[64,64,128]{2,1,0:T(8,128)(2,1)}, u32[]{:S(2)}, u32[]{:S(2)}) collective-permute-start(bf16[64,64,128]{2,1,0:T(8,128)(2,1)} %constant_dynamic-slice_fusion.25), channel_id=1, source_target_pairs={{0,4},{4,0},{8,12},{12,8},{16,20},{20,16},{24,28},{28,24},{1,5},{5... | collective-permute-start | bytes 3145736 | tf_op jit(solution)/shard_map/ppermute | solution.py:123
  66.6 28.6 %collective-permute-start.1 = (bf16[64,64,128]{2,1,0:T(8,128)(2,1)}, bf16[64,64,128]{2,1,0:T(8,128)(2,1)}, u32[]{:S(2)}, u32[]{:S(2)}) collective-permute-start(bf16[64,64,128]{2,1,0:T(8,128)(2,1)} %constant_dynamic-slice_fusion.24), channel_id=1, source_target_pairs={{0,4},{4,0},{8,12},{12,8},{16,20},{20,16},{24,28},{28,24},{1,5},{5... | collective-permute-start | bytes 3145736 | tf_op jit(solution)/shard_map/ppermute | solution.py:123
  67.1 10.2 %copy-start.10 = (bf16[64,64,128]{2,1,0:T(8,128)(2,1)S(1)}, bf16[64,64,128]{2,1,0:T(8,128)(2,1)}, u32[]{:S(2)}) copy-start(bf16[64,64,128]{2,1,0:T(8,128)(2,1)} %copy-done.9) | copy-start | bytes 3145732
  74.3 9.7 %copy-start.5 = (bf16[128,64,128]{2,1,0:T(8,128)(2,1)S(1)}, bf16[128,64,128]{2,1,0:T(8,128)(2,1)}, u32[]{:S(2)}) copy-start(bf16[128,64,128]{2,1,0:T(8,128)(2,1)} %copy-done.4) | copy-start | bytes 6291460
  74.4 8.0 %collective-permute-start.4 = (bf16[16,64,128]{2,1,0:T(8,128)(2,1)S(1)}, bf16[16,64,128]{2,1,0:T(8,128)(2,1)S(1)}, u32[]{:S(2)}, u32[]{:S(2)}) collective-permute-start(bf16[16,64,128]{2,1,0:T(8,128)(2,1)S(1)} %constant_dynamic-slice_fusion.21), channel_id=1, source_target_pairs={{0,16},{4,20},{8,24},{12,28},{16,0},{20,4},{24,8},{28,12},{1,17},{... | collective-permute-start | bytes 786440 | tf_op jit(solution)/shard_map/ppermute | solution.py:123
  78.6 7.1 %collective-permute-start.9 = (bf16[16,64,128]{2,1,0:T(8,128)(2,1)S(1)}, bf16[16,64,128]{2,1,0:T(8,128)(2,1)S(1)}, u32[]{:S(2)}, u32[]{:S(2)}) collective-permute-start(bf16[16,64,128]{2,1,0:T(8,128)(2,1)S(1)} %constant_dynamic-slice_fusion.18), channel_id=1, source_target_pairs={{0,8},{4,12},{8,0},{12,4},{16,24},{20,28},{24,16},{28,20},{1,9},{5... | collective-permute-start | bytes 786440 | tf_op jit(solution)/shard_map/ppermute | solution.py:123
  82.5 7.1 %collective-permute-start.5 = (bf16[16,64,128]{2,1,0:T(8,128)(2,1)S(1)}, bf16[16,64,128]{2,1,0:T(8,128)(2,1)S(1)}, u32[]{:S(2)}, u32[]{:S(2)}) collective-permute-start(bf16[16,64,128]{2,1,0:T(8,128)(2,1)S(1)} %add_convert_fusion.11), channel_id=1, source_target_pairs={{0,16},{4,20},{8,24},{12,28},{16,0},{20,4},{24,8},{28,12},{1,17},{... | collective-permute-start | bytes 786440 | tf_op jit(solution)/shard_map/ppermute | solution.py:123
  85.8 9.2 %collective-permute-start.10 = (bf16[16,64,128]{2,1,0:T(8,128)(2,1)S(1)}, bf16[16,64,128]{2,1,0:T(8,128)(2,1)S(1)}, u32[]{:S(2)}, u32[]{:S(2)}) collective-permute-start(bf16[16,64,128]{2,1,0:T(8,128)(2,1)S(1)} %add_convert_fusion.10), channel_id=1, source_target_pairs={{0,8},{4,12},{8,0},{12,4},{16,24},{20,28},{24,16},{28,20},{1,9},{5... | collective-permute-start | bytes 786440 | tf_op jit(solution)/shard_map/ppermute | solution.py:123
  89.6 14.2 %collective-permute-start.6 = (bf16[32,64,128]{2,1,0:T(8,128)(2,1)S(1)}, bf16[32,64,128]{2,1,0:T(8,128)(2,1)S(1)}, u32[]{:S(2)}, u32[]{:S(2)}) collective-permute-start(bf16[32,64,128]{2,1,0:T(8,128)(2,1)S(1)} %pad_maximum_fusion.7), channel_id=1, source_target_pairs={{0,8},{4,12},{8,0},{12,4},{16,24},{20,28},{24,16},{28,20},{1,9},{5... | collective-permute-start | bytes 1572872 | tf_op jit(solution)/shard_map/ppermute | solution.py:123
  95.1 9.2 %collective-permute-start.11 = (bf16[32,64,128]{2,1,0:T(8,128)(2,1)S(1)}, bf16[32,64,128]{2,1,0:T(8,128)(2,1)S(1)}, u32[]{:S(2)}, u32[]{:S(2)}) collective-permute-start(bf16[32,64,128]{2,1,0:T(8,128)(2,1)S(1)} %pad_maximum_fusion.8), channel_id=1, source_target_pairs={{0,16},{4,20},{8,24},{12,28},{16,0},{20,4},{24,8},{28,12},{1,17},{... | collective-permute-start | bytes 1572872 | tf_op jit(solution)/shard_map/ppermute | solution.py:123
  104.6 11.2 %collective-permute-start.25 = (bf16[32,64,128]{2,1,0:T(8,128)(2,1)S(1)}, bf16[32,64,128]{2,1,0:T(8,128)(2,1)S(1)}, u32[]{:S(2)}, u32[]{:S(2)}) collective-permute-start(bf16[32,64,128]{2,1,0:T(8,128)(2,1)S(1)} %constant_dynamic-slice_fusion.8), channel_id=1, source_target_pairs={{0,16},{4,20},{8,24},{12,28},{16,0},{20,4},{24,8},{28,12},{1,17},{... | collective-permute-start | bytes 1572872 | tf_op jit(solution)/shard_map/ppermute | solution.py:123
  105.1 13.9 %collective-permute-start.20 = (bf16[32,64,128]{2,1,0:T(8,128)(2,1)S(1)}, bf16[32,64,128]{2,1,0:T(8,128)(2,1)S(1)}, u32[]{:S(2)}, u32[]{:S(2)}) collective-permute-start(bf16[32,64,128]{2,1,0:T(8,128)(2,1)S(1)} %constant_dynamic-slice_fusion.10), channel_id=1, source_target_pairs={{0,8},{4,12},{8,0},{12,4},{16,24},{20,28},{24,16},{28,20},{1,9},{5... | collective-permute-start | bytes 1572872 | tf_op jit(solution)/shard_map/ppermute | solution.py:123
  105.9 22.5 %collective-permute-start.13 = (bf16[64,64,128]{2,1,0:T(8,128)(2,1)S(1)}, bf16[64,64,128]{2,1,0:T(8,128)(2,1)}, u32[]{:S(2)}, u32[]{:S(2)}) collective-permute-start(bf16[64,64,128]{2,1,0:T(8,128)(2,1)S(1)} %pad_maximum_fusion.4), channel_id=1, source_target_pairs={{0,4},{4,0},{8,12},{12,8},{16,20},{20,16},{24,28},{28,24},{1,5},{5... | collective-permute-start | bytes 3145736 | tf_op jit(solution)/shard_map/ppermute | solution.py:123
  116.1 6.9 %collective-permute-start.26 = (bf16[16,64,128]{2,1,0:T(8,128)(2,1)S(1)}, bf16[16,64,128]{2,1,0:T(8,128)(2,1)}, u32[]{:S(2)}, u32[]{:S(2)}) collective-permute-start(bf16[16,64,128]{2,1,0:T(8,128)(2,1)S(1)} %constant_dynamic-slice_fusion.7), channel_id=1, source_target_pairs={{0,8},{4,12},{8,0},{12,4},{16,24},{20,28},{24,16},{28,20},{1,9},{5... | collective-permute-start | bytes 786440 | tf_op jit(solution)/shard_map/ppermute | solution.py:123
  119.9 7.4 %collective-permute-start.21 = (bf16[16,64,128]{2,1,0:T(8,128)(2,1)}, bf16[16,64,128]{2,1,0:T(8,128)(2,1)}, u32[]{:S(2)}, u32[]{:S(2)}) collective-permute-start(bf16[16,64,128]{2,1,0:T(8,128)(2,1)} %constant_dynamic-slice_fusion.9), channel_id=1, source_target_pairs={{0,16},{4,20},{8,24},{12,28},{16,0},{20,4},{24,8},{28,12},{1,17},{... | collective-permute-start | bytes 786440 | tf_op jit(solution)/shard_map/ppermute | solution.py:123
  119.9 17.9 %collective-permute-start.12 = (bf16[64,64,128]{2,1,0:T(8,128)(2,1)S(1)}, bf16[64,64,128]{2,1,0:T(8,128)(2,1)S(1)}, u32[]{:S(2)}, u32[]{:S(2)}) collective-permute-start(bf16[64,64,128]{2,1,0:T(8,128)(2,1)S(1)} %pad_maximum_fusion.3), channel_id=1, source_target_pairs={{0,4},{4,0},{8,12},{12,8},{16,20},{20,16},{24,28},{28,24},{1,5},{5... | collective-permute-start | bytes 3145736 | tf_op jit(solution)/shard_map/ppermute | solution.py:123
  124.0 6.4 %collective-permute-start.27 = (bf16[16,64,128]{2,1,0:T(8,128)(2,1)S(1)}, bf16[16,64,128]{2,1,0:T(8,128)(2,1)S(1)}, u32[]{:S(2)}, u32[]{:S(2)}) collective-permute-start(bf16[16,64,128]{2,1,0:T(8,128)(2,1)S(1)} %add_convert_fusion.8), channel_id=1, source_target_pairs={{0,8},{4,12},{8,0},{12,4},{16,24},{20,28},{24,16},{28,20},{1,9},{5... | collective-permute-start | bytes 786440 | tf_op jit(solution)/shard_map/ppermute | solution.py:123
  128.3 9.3 %collective-permute-start.22 = (bf16[16,64,128]{2,1,0:T(8,128)(2,1)S(1)}, bf16[16,64,128]{2,1,0:T(8,128)(2,1)S(1)}, u32[]{:S(2)}, u32[]{:S(2)}) collective-permute-start(bf16[16,64,128]{2,1,0:T(8,128)(2,1)S(1)} %add_convert_fusion.9), channel_id=1, source_target_pairs={{0,16},{4,20},{8,24},{12,28},{16,0},{20,4},{24,8},{28,12},{1,17},{... | collective-permute-start | bytes 786440 | tf_op jit(solution)/shard_map/ppermute | solution.py:123
  130.5 13.6 %collective-permute-start.28 = (bf16[32,64,128]{2,1,0:T(8,128)(2,1)S(1)}, bf16[32,64,128]{2,1,0:T(8,128)(2,1)S(1)}, u32[]{:S(2)}, u32[]{:S(2)}) collective-permute-start(bf16[32,64,128]{2,1,0:T(8,128)(2,1)S(1)} %pad_maximum_fusion.10), channel_id=1, source_target_pairs={{0,16},{4,20},{8,24},{12,28},{16,0},{20,4},{24,8},{28,12},{1,17},{... | collective-permute-start | bytes 1572872 | tf_op jit(solution)/shard_map/ppermute | solution.py:123
  137.8 9.2 %collective-permute-start.23 = (bf16[32,64,128]{2,1,0:T(8,128)(2,1)S(1)}, bf16[32,64,128]{2,1,0:T(8,128)(2,1)S(1)}, u32[]{:S(2)}, u32[]{:S(2)}) collective-permute-start(bf16[32,64,128]{2,1,0:T(8,128)(2,1)S(1)} %pad_maximum_fusion.9), channel_id=1, source_target_pairs={{0,8},{4,12},{8,0},{12,4},{16,24},{20,28},{24,16},{28,20},{1,9},{5... | collective-permute-start | bytes 1572872 | tf_op jit(solution)/shard_map/ppermute | solution.py:123
  144.3 27.2 %collective-permute-start.29 = (bf16[64,64,128]{2,1,0:T(8,128)(2,1)S(1)}, bf16[64,64,128]{2,1,0:T(8,128)(2,1)S(1)}, u32[]{:S(2)}, u32[]{:S(2)}) collective-permute-start(bf16[64,64,128]{2,1,0:T(8,128)(2,1)S(1)} %pad_maximum_fusion.6), channel_id=1, source_target_pairs={{0,4},{4,0},{8,12},{12,8},{16,20},{20,16},{24,28},{28,24},{1,5},{5... | collective-permute-start | bytes 3145736 | tf_op jit(solution)/shard_map/ppermute | solution.py:123
  147.2 24.5 %collective-permute-start.24 = (bf16[64,64,128]{2,1,0:T(8,128)(2,1)S(1)}, bf16[64,64,128]{2,1,0:T(8,128)(2,1)S(1)}, u32[]{:S(2)}, u32[]{:S(2)}) collective-permute-start(bf16[64,64,128]{2,1,0:T(8,128)(2,1)S(1)} %pad_maximum_fusion.5), channel_id=1, source_target_pairs={{0,4},{4,0},{8,12},{12,8},{16,20},{20,16},{24,28},{28,24},{1,5},{5... | collective-permute-start | bytes 3145736 | tf_op jit(solution)/shard_map/ppermute | solution.py:123
  147.3 2.4 copy-start.2
  169.3 25.7 %collective-permute-start.17 = (bf16[16,101,256]{2,0,1:T(8,128)(2,1)}, bf16[16,101,256]{2,0,1:T(8,128)(2,1)S(1)}, u32[]{:S(2)}, u32[]{:S(2)}) collective-permute-start(bf16[16,101,256]{2,0,1:T(8,128)(2,1)} %bitcast.66), channel_id=1, source_target_pairs={{3,2},{7,6},{11,10},{15,14},{19,18},{23,22},{27,26},{31,30}} | collective-permute-start | bytes 2482184 | tf_op jit(solution)/shard_map/ppermute | solution.py:171
  170.2 26.4 %collective-permute-start.14 = (bf16[16,101,256]{2,0,1:T(8,128)(2,1)S(1)}, bf16[16,101,256]{2,0,1:T(8,128)(2,1)S(1)}, u32[]{:S(2)}, u32[]{:S(2)}) collective-permute-start(bf16[16,101,256]{2,0,1:T(8,128)(2,1)S(1)} %bitcast.75), channel_id=1, source_target_pairs={{0,1},{4,5},{8,9},{12,13},{16,17},{20,21},{24,25},{28,29}} | collective-permute-start | bytes 2482184 | tf_op jit(solution)/shard_map/ppermute | solution.py:170
  192.8 8.7 %collective-permute-start.33 = (bf16[16,101,256]{2,0,1:T(8,128)(2,1)S(1)}, bf16[16,101,256]{2,0,1:T(8,128)(2,1)S(1)}, u32[]{:S(2)}, u32[]{:S(2)}) collective-permute-start(bf16[16,101,256]{2,0,1:T(8,128)(2,1)S(1)} %bitcast.77), channel_id=1, source_target_pairs={{3,2},{7,6},{11,10},{15,14},{19,18},{23,22},{27,26},{31,30}} | collective-permute-start | bytes 2482184 | tf_op jit(solution)/shard_map/ppermute | solution.py:171
  193.7 23.2 %collective-permute-start.30 = (bf16[16,101,256]{2,0,1:T(8,128)(2,1)S(1)}, bf16[16,101,256]{2,0,1:T(8,128)(2,1)S(1)}, u32[]{:S(2)}, u32[]{:S(2)}) collective-permute-start(bf16[16,101,256]{2,0,1:T(8,128)(2,1)S(1)} %bitcast.76), channel_id=1, source_target_pairs={{0,1},{4,5},{8,9},{12,13},{16,17},{20,21},{24,25},{28,29}} | collective-permute-start | bytes 2482184 | tf_op jit(solution)/shard_map/ppermute | solution.py:170
  195.3 26.7 %collective-permute-start.18 = (bf16[16,101,256]{2,0,1:T(8,128)(2,1)S(1)}, bf16[16,101,256]{2,0,1:T(8,128)(2,1)S(1)}, u32[]{:S(2)}, u32[]{:S(2)}) collective-permute-start(bf16[16,101,256]{2,0,1:T(8,128)(2,1)S(1)} %fusion.6), channel_id=1, source_target_pairs={{3,2},{2,1},{7,6},{6,5},{11,10},{10,9},{15,14},{14,13},{19,18},{18... | collective-permute-start | bytes 2482184 | tf_op jit(solution)/shard_map/ppermute | solution.py:171
  196.9 37.7 %collective-permute-start.15 = (bf16[16,101,256]{2,0,1:T(8,128)(2,1)S(1)}, bf16[16,101,256]{2,0,1:T(8,128)(2,1)S(1)}, u32[]{:S(2)}, u32[]{:S(2)}) collective-permute-start(bf16[16,101,256]{2,0,1:T(8,128)(2,1)S(1)} %fusion.8), channel_id=1, source_target_pairs={{0,1},{1,2},{4,5},{5,6},{8,9},{9,10},{12,13},{13,14},{16,17},{17,1... | collective-permute-start | bytes 2482184 | tf_op jit(solution)/shard_map/ppermute | solution.py:170
  201.8 38.0 %collective-permute-start.34 = (bf16[16,101,256]{2,0,1:T(8,128)(2,1)S(1)}, bf16[16,101,256]{2,0,1:T(8,128)(2,1)S(1)}, u32[]{:S(2)}, u32[]{:S(2)}) collective-permute-start(bf16[16,101,256]{2,0,1:T(8,128)(2,1)S(1)} %fusion), channel_id=1, source_target_pairs={{3,2},{2,1},{7,6},{6,5},{11,10},{10,9},{15,14},{14,13},{19,18},{18... | collective-permute-start | bytes 2482184 | tf_op jit(solution)/shard_map/ppermute | solution.py:171
  217.1 35.2 %collective-permute-start.31 = (bf16[16,101,256]{2,0,1:T(8,128)(2,1)S(1)}, bf16[16,101,256]{2,0,1:T(8,128)(2,1)S(1)}, u32[]{:S(2)}, u32[]{:S(2)}) collective-permute-start(bf16[16,101,256]{2,0,1:T(8,128)(2,1)S(1)} %fusion.2), channel_id=1, source_target_pairs={{0,1},{1,2},{4,5},{5,6},{8,9},{9,10},{12,13},{13,14},{16,17},{17,1... | collective-permute-start | bytes 2482184 | tf_op jit(solution)/shard_map/ppermute | solution.py:170
  222.3 35.2 %collective-permute-start.19 = (bf16[16,101,256]{2,0,1:T(8,128)(2,1)S(1)}, bf16[16,101,256]{2,0,1:T(8,128)(2,1)S(1)}, u32[]{:S(2)}, u32[]{:S(2)}) collective-permute-start(bf16[16,101,256]{2,0,1:T(8,128)(2,1)S(1)} %fusion.7), channel_id=1, source_target_pairs={{3,2},{2,1},{1,0},{7,6},{6,5},{5,4},{11,10},{10,9},{9,8},{15,14},{... | collective-permute-start | bytes 2482184 | tf_op jit(solution)/shard_map/ppermute | solution.py:171
  234.9 35.2 %collective-permute-start.16 = (bf16[16,101,256]{2,0,1:T(8,128)(2,1)S(1)}, bf16[16,101,256]{2,0,1:T(8,128)(2,1)S(1)}, u32[]{:S(2)}, u32[]{:S(2)}) collective-permute-start(bf16[16,101,256]{2,0,1:T(8,128)(2,1)S(1)} %fusion.9), channel_id=1, source_target_pairs={{0,1},{1,2},{2,3},{4,5},{5,6},{6,7},{8,9},{9,10},{10,11},{12,13},{... | collective-permute-start | bytes 2482184 | tf_op jit(solution)/shard_map/ppermute | solution.py:170
  240.0 33.0 %collective-permute-start.35 = (bf16[16,101,256]{2,0,1:T(8,128)(2,1)S(1)}, bf16[16,101,256]{2,0,1:T(8,128)(2,1)S(1)}, u32[]{:S(2)}, u32[]{:S(2)}) collective-permute-start(bf16[16,101,256]{2,0,1:T(8,128)(2,1)S(1)} %fusion.1), channel_id=1, source_target_pairs={{3,2},{2,1},{1,0},{7,6},{6,5},{5,4},{11,10},{10,9},{9,8},{15,14},{... | collective-permute-start | bytes 2482184 | tf_op jit(solution)/shard_map/ppermute | solution.py:171
  252.6 34.7 %collective-permute-start.32 = (bf16[16,101,256]{2,0,1:T(8,128)(2,1)S(1)}, bf16[16,101,256]{2,0,1:T(8,128)(2,1)S(1)}, u32[]{:S(2)}, u32[]{:S(2)}) collective-permute-start(bf16[16,101,256]{2,0,1:T(8,128)(2,1)S(1)} %fusion.3), channel_id=1, source_target_pairs={{0,1},{1,2},{2,3},{4,5},{5,6},{6,7},{8,9},{9,10},{10,11},{12,13},{... | collective-permute-start | bytes 2482184 | tf_op jit(solution)/shard_map/ppermute | solution.py:170
  (2 other events, 4.0 us)

commit v4 on v3

--- a/solution.py
+++ b/solution.py
@@ -11,7 +11,8 @@
 
 LAGS = 101
 SRC_BLK = 64
-ROWS = (16, 16)
+ROWS = (8, 12, 12)
+AHEAD = (3, 2)
 PAD = 256
 MIB = 1024 * 1024
 
@@ -46,7 +47,7 @@
         ],
         out_specs=pl.BlockSpec((bins, rows, depth), lambda i: (i, 0, 0)),
         out_shape=jax.ShapeDtypeStruct((-(-bin_count // PAD) * PAD, rows, depth), jnp.bfloat16),
-        compiler_params=pltpu.CompilerParams(vmem_limit_bytes=32 * MIB),
+        compiler_params=pltpu.CompilerParams(vmem_limit_bytes=52 * MIB),
         cost_estimate=pl.CostEstimate(
             flops=2 * bin_count * rows * width * depth,
             bytes_accessed=2 * bin_count * depth * (width + rows),
@@ -106,7 +107,7 @@
         out_specs=pl.BlockSpec((rows, LAGS, width), lambda i: (0, 0, 0)),
         out_shape=jax.ShapeDtypeStruct((rows, LAGS, width), jnp.bfloat16),
         scratch_shapes=[pltpu.VMEM((width // 128, rows * stride, 128), jnp.float32)],
-        compiler_params=pltpu.CompilerParams(vmem_limit_bytes=48 * MIB),
+        compiler_params=pltpu.CompilerParams(vmem_limit_bytes=52 * MIB),
         cost_estimate=pl.CostEstimate(
             flops=2 * bin_count * 2 * rows * depth * width + 2 * 2 * bin_count * rows * LAGS * width,
             bytes_accessed=2 * bin_count * depth * (width + rows) + 2 * rows * LAGS * width,
@@ -142,36 +143,48 @@
     return current
 
 
-def sum_of_chan(mine, after):
-    bit_count = (lax.axis_size("chan") - 1).bit_length()
+def orders():
+    rest = list(range(1, (lax.axis_size("chan") - 1).bit_length()))
+    return rest, rest[::-1]
+
+
+def begin(mine):
     length = mine.shape[0] // 2
-    orders = [list(range(1, bit_count)), list(range(1, bit_count))[::-1]]
-    parts = [halve(mine[:length], "chan", [0]), halve(mine[length:], "chan", [0])]
-    if after is not None:
-        parts, after = lax.optimization_barrier((parts, after))
-    parts = [halve(part, "chan", order) for part, order in zip(parts, orders)]
-    parts = [double(part, "chan", order) for part, order in zip(parts, orders)]
-    return parts, after
+    return [halve(mine[:length], "chan", [0]), halve(mine[length:], "chan", [0])]
+
+
+def halve_rest(parts):
+    return [halve(part, "chan", order) for part, order in zip(parts, orders())]
+
+
+def double_rest(parts):
+    return [double(part, "chan", order) for part, order in zip(parts, orders())]
 
 
 def finish(parts):
     return jnp.concatenate([double(part, "chan", [0]) for part in parts], axis=0)
 
 
-def chain_scatter(parts, axis):
+def take(parts, at):
+    return lax.dynamic_index_in_dim(parts, jnp.clip(at, 0, parts.shape[0] - 1), 0, keepdims=False)
+
+
+def chain_steps(parts, state, axis, first, last):
     n, at = lax.axis_size(axis), lax.axis_index(axis)
-    total = None
-    from_left = from_right = None
-    for t in range(n - 1):
-        to_right = lax.dynamic_index_in_dim(parts, jnp.clip(n - 1 - t + at, 0, n - 1), 0, keepdims=False)
-        to_left = lax.dynamic_index_in_dim(parts, jnp.clip(t + at - (n - 1), 0, n - 1), 0, keepdims=False)
+    for t in range(first, last):
+        to_right, to_left = take(parts, n - 1 - t + at), take(parts, t + at - (n - 1))
         if t:
-            to_right, to_left = add(to_right, from_left), add(to_left, from_right)
-        from_left = lax.ppermute(to_right, axis, [(i, i + 1) for i in range(t + 1)])
-        from_right = lax.ppermute(to_left, axis, [(n - 1 - i, n - 2 - i) for i in range(t + 1)])
-    own = lax.dynamic_index_in_dim(parts, at, 0, keepdims=False).astype(jnp.float32)
-    total = own + from_left.astype(jnp.float32) + from_right.astype(jnp.float32)
-    return total.astype(jnp.bfloat16)
+            to_right, to_left = add(to_right, state[0]), add(to_left, state[1])
+        state = (
+            lax.ppermute(to_right, axis, [(i, i + 1) for i in range(t + 1)]),
+            lax.ppermute(to_left, axis, [(n - 1 - i, n - 2 - i) for i in range(t + 1)]),
+        )
+    return state
+
+
+def chain_end(parts, state, axis):
+    own = take(parts, lax.axis_index(axis)).astype(jnp.float32)
+    return (own + state[0].astype(jnp.float32) + state[1].astype(jnp.float32)).astype(jnp.bfloat16)
 
 
 def body(spectra, src_blocks, valid):
@@ -196,21 +209,43 @@
         return (channel[:, None] == jnp.arange(width, dtype=jnp.int32)[None, :]).astype(jnp.bfloat16)
 
     x = spectra.transpose(2, 1, 0, 3).reshape(bin_count, depth, width)
-    summed = []
-    after = None
+    steps = tm_count - 1
+    outs = []
+    done = chain = None
     first = 0
-    for rows in ROWS:
-        mine = pick_sources(pick_of(first, rows), keep, x, 25)
-        parts, after = sum_of_chan(mine, after)
-        if after is not None:
-            summed.append(after)
-        after = parts
+
+    def correlograms(done, rows):
+        return correlate(sign, table, done, x, 25).reshape(tm_count, rows, LAGS, width)
+
+    coming = begin(pick_sources(pick_of(0, ROWS[0]), keep, x, 25))
+    for at, rows in enumerate(ROWS):
+        parts = coming
+        if at:
+            parts, done = lax.optimization_barrier((parts, done))
         first += rows
-    summed.append(after)
-    outs = []
-    for rows, parts in zip(ROWS, summed):
-        partial_value = correlate(sign, table, finish(parts), x, 25)
-        outs.append(chain_scatter(partial_value.reshape(tm_count, rows, LAGS, width), "tm"))
+        if at + 1 < len(ROWS):
+            parts, keep = lax.optimization_barrier((parts, keep))
+            coming = begin(pick_sources(pick_of(first, ROWS[at + 1]), keep, x, 25))
+        parts = halve_rest(parts)
+        if at:
+            source = finish(done)
+            if chain is not None:
+                ahead = min(AHEAD[at - 2], steps)
+                state = chain_steps(chain, None, "tm", 0, ahead)
+                source, state = lax.optimization_barrier((source, state))
+                state = chain_steps(chain, state, "tm", ahead, steps)
+                outs.append(chain_end(chain, state, "tm"))
+            chain = correlograms(source, ROWS[at - 1])
+            parts, chain = lax.optimization_barrier((parts, chain))
+        done = double_rest(parts)
+    source = finish(done)
+    ahead = min(AHEAD[-1], steps)
+    state = chain_steps(chain, None, "tm", 0, ahead)
+    source, state = lax.optimization_barrier((source, state))
+    state = chain_steps(chain, state, "tm", ahead, steps)
+    outs.append(chain_end(chain, state, "tm"))
+    chain = correlograms(source, ROWS[-1])
+    outs.append(chain_end(chain, chain_steps(chain, None, "tm", 0, steps), "tm"))
     return jnp.concatenate(outs, axis=0)
 
 

time: 291 us -> 317 us (1.089)
  Pallas kernels: 52.8 us -> 87.2 us
  starting transfers between devices: 42.5 us -> 64.6 us
  waiting for transfers between devices: 123 us -> 105 us
  local copies, waits for them, and re-layouts: 43.5 us -> 31.7 us
    pallas_call x2 -> x3, Pallas kernels: 16.6 us -> 38.8 us  [pick_sources(): pl.pallas_call(pick_kernel, grid=(bin_count // bins,), in_specs=[pl.Block...]
    ppermute x24 -> x36, waiting for transfers between devices: 59.1 us -> 40.5 us  [swap(): lax.ppermute(x, axis, [(i, i ^ 1 << bit) for i in range(lax.axis_size(axi...]
    ppermute x24 -> x36, starting transfers between devices: 13 us -> 27.8 us  [swap(): lax.ppermute(x, axis, [(i, i ^ 1 << bit) for i in range(lax.axis_size(axi...]
    pallas_call x2 -> x3, Pallas kernels: 36.2 us -> 48.5 us  [correlate(): pl.pallas_call(functools.partial(correlate_kernel, stride, bin_count), gr...]
    unnamed x28 -> x24, local copies, waits for them, and re-layouts: 11.9 us -> 0.06 us
    ppermute x12 -> x18, starting transfers between devices: 29.5 us -> 36.8 us  [the longest x9 24.9 us: chain_steps(): lax.ppermute(to_right, axis, [(i, i + 1) for i in range(t + 1)])]
    convert_element_type x20 -> x26, other arithmetic: 14.7 us -> 8.65 us  [add(): return (a.astype(jnp.float32) + b.astype(jnp.float32)).astype(jnp.bfloat16)]
    dynamic_slice x12 -> x18, local copies, waits for them, and re-layouts: 7.88 us -> 2.96 us  [halve(): sent = lax.dynamic_slice_in_dim(current, (1 - side) * length, length, 0)]
  transfers between devices with their start and end apart: 36 -> 54, of which waited for: 21 -> 23; matrix products, arithmetic and copies ran while one was open for 11% -> 9% of each run, Pallas kernels for 15% -> 13%
where the time goes in v4:
time: 317 us; the launch traced here: 316 us
  waiting for transfers between devices  105 us (33%)
  Pallas kernels  87.2 us (28%)
  starting transfers between devices  64.6 us (20%)
  local copies, waits for them, and re-layouts  31.7 us (10%)
  other arithmetic  26 us (8%)
    pallas_call x3, Pallas kernels, correlate(): pl.pallas_call(functools.partial(correlate_kernel, stride, bin_count), gr...  48.5 us
    ppermute x36, waiting for transfers between devices, swap(): lax.ppermute(x, axis, [(i, i ^ 1 << bit) for i in range(lax.axis_size(axi...  40.5 us
    pallas_call x3, Pallas kernels, pick_sources(): pl.pallas_call(pick_kernel, grid=(bin_count // bins,), in_specs=[pl.Block...  38.8 us
    ppermute x9, waiting for transfers between devices, chain_steps(): lax.ppermute(to_right, axis, [(i, i + 1) for i in range(t + 1)])  36.8 us
    ppermute x9, waiting for transfers between devices, chain_steps(): lax.ppermute(to_left, axis, [(n - 1 - i, n - 2 - i) for i in range(t + 1)])  27.9 us
    ppermute x36, starting transfers between devices, swap(): lax.ppermute(x, axis, [(i, i ^ 1 << bit) for i in range(lax.axis_size(axi...  27.8 us
    ppermute x9, starting transfers between devices, chain_steps(): lax.ppermute(to_right, axis, [(i, i + 1) for i in range(t + 1)])  24.9 us
    transpose x1, local copies, waits for them, and re-layouts, body(): x = spectra.transpose(2, 1, 0, 3).reshape(bin_count, depth, width)  16.6 us
  transfers between devices with their start and end apart: 54, of which 23 were waited for; matrix products, arithmetic and copies ran while one was open for 9% of the time, Pallas kernels for 13%

profile of v4, /device:TPU:8, one launch (start us, length us, event | category | flops | bytes accessed | tf_op | source)
XLA Modules:
  0.0 315.6 jit_solution(10767252527112800272)
XLA Ops:
  2.1 1.9 fusion.22
  4.0 16.6 %copy.37 = bf16[250,2,64,256]{3,2,1,0:T(8,128)(2,1)} copy(bf16[250,2,64,256]{3,1,0,2:T(2,128)(2,1)} %bitcast.84) | data formatting | bytes 32768000 | tf_op jit(solution)/shard_map/transpose | solution.py:211
  20.6 12.7 %shard_map.136 = bf16[256,32,128]{2,1,0:T(8,128)(2,1)} custom-call(bf16[32,256]{1,0:T(8,128)(2,1)S(1)} %fusion.20.pick_ref, f32[1,128]{1,0:T(1,128)S(1)} %broadcast_in_dim_tile.3.keep_ref, bf16[250,128,256]{2,1,0:T(8,128)(2,1)} %bitcast.69), custom_call_target="tpu_custom_call" | custom-call | flops 524288000 | bytes 18432000 | tf_op jit(solution)/shard_map/pallas_call | solution.py:40
  33.3 1.9 fusion.25
  39.4 1.6 collective-permute-start.8
  41.0 1.6 collective-permute-start.4
  42.6 13.0 %shard_map.137 = bf16[256,48,128]{2,1,0:T(8,128)(2,1)} custom-call(bf16[48,256]{1,0:T(8,128)(2,1)S(1)} %get-tuple-element.117.pick_ref, f32[1,128]{1,0:T(1,128)S(1)} %broadcast_in_dim_tile.3.keep_ref, bf16[250,128,256]{2,1,0:T(8,128)(2,1)} %bitcast.70), custom_call_target="tpu_custom_call" | custom-call | flops 786432000 | bytes 19456000 | tf_op jit(solution)/shard_map/pallas_call | solution.py:40
  55.6 2.4 fusion.24
  59.6 4.7 %collective-permute-done.9 = bf16[16,32,128]{2,1,0:T(8,128)(2,1)S(1)} collective-permute-done((bf16[16,32,128]{2,1,0:T(8,128)(2,1)S(1)}, bf16[16,32,128]{2,1,0:T(8,128)(2,1)S(1)}, u32[]{:S(2)}, u32[]{:S(2)}) %collective-permute-start.9) | collective-permute-done | bytes 131104 | tf_op jit(solution)/shard_map/ppermute | solution.py:124
  65.5 4.0 %collective-permute-done.10 = bf16[16,32,128]{2,1,0:T(8,128)(2,1)S(1)} collective-permute-done((bf16[16,32,128]{2,1,0:T(8,128)(2,1)S(1)}, bf16[16,32,128]{2,1,0:T(8,128)(2,1)S(1)}, u32[]{:S(2)}, u32[]{:S(2)}) %collective-permute-start.10) | collective-permute-done | bytes 131104 | tf_op jit(solution)/shard_map/ppermute | solution.py:124
  71.7 4.9 %collective-permute-done.11 = bf16[32,32,128]{2,1,0:T(8,128)(2,1)S(1)} collective-permute-done((bf16[32,32,128]{2,1,0:T(8,128)(2,1)S(1)}, bf16[32,32,128]{2,1,0:T(8,128)(2,1)S(1)}, u32[]{:S(2)}, u32[]{:S(2)}) %collective-permute-start.11) | collective-permute-done | bytes 262176 | tf_op jit(solution)/shard_map/ppermute | solution.py:124
  77.7 1.6 collective-permute-start.14
  80.3 13.0 %shard_map.139 = bf16[256,48,128]{2,1,0:T(8,128)(2,1)} custom-call(bf16[48,256]{1,0:T(8,128)(2,1)S(1)} %get-tuple-element.118.pick_ref, f32[1,128]{1,0:T(1,128)S(1)} %broadcast_in_dim_tile.3.keep_ref, bf16[250,128,256]{2,1,0:T(8,128)(2,1)} %bitcast.71), custom_call_target="tpu_custom_call" | custom-call | flops 786432000 | bytes 19456000 | tf_op jit(solution)/shard_map/pallas_call | solution.py:40
  93.3 2.4 fusion.23
  96.6 1.6 collective-permute-start.15
  99.1 1.6 pad_maximum_fusion.2.source_ref
  100.7 13.7 %shard_map.138 = bf16[32,101,256]{2,1,0:T(8,128)(2,1)S(1)} custom-call(bf16[1,128]{1,0:T(2,128)(2,1)S(1)} %copy-done.1, bf16[112,500]{1,0:T(8,128)(2,1)S(1)} %copy-done, bf16[256,32,128]{2,1,0:T(8,128)(2,1)} %pad_maximum_fusion.2.source_ref, bf16[250,128,256]{2,1,0:T(8,128)(2,1)} %bitcast.72), custom_call_target="tpu_custom_call" | custom-call | flops 1875968000 | bytes 20086784 | tf_op jit(solution)/shard_map/pallas_call | solution.py:98
  114.5 1.6 collective-permute-start.20
  125.4 5.3 %collective-permute-done.21 = bf16[32,48,128]{2,1,0:T(8,128)(2,1)S(1)} collective-permute-done((bf16[32,48,128]{2,1,0:T(8,128)(2,1)S(1)}, bf16[32,48,128]{2,1,0:T(8,128)(2,1)S(1)}, u32[]{:S(2)}, u32[]{:S(2)}) %collective-permute-start.21) | collective-permute-done | bytes 393248 | tf_op jit(solution)/shard_map/ppermute | solution.py:124
  135.4 1.6 collective-permute-start.32
  137.5 5.2 %collective-permute-done.30 = bf16[8,101,256]{2,1,0:T(8,128)(2,1)} collective-permute-done((bf16[8,101,256]{2,1,0:T(8,128)(2,1)}, bf16[8,101,256]{2,1,0:T(8,128)(2,1)}, u32[]{:S(2)}, u32[]{:S(2)}) %collective-permute-start.30) | collective-permute-done | bytes 413728 | tf_op jit(solution)/shard_map/ppermute | solution.py:180
  144.1 1.9 collective-permute-start.31
  146.0 4.1 %collective-permute-start.27 = (bf16[8,101,256]{2,1,0:T(8,128)(2,1)S(1)}, bf16[8,101,256]{2,1,0:T(8,128)(2,1)S(1)}, u32[]{:S(2)}, u32[]{:S(2)}) collective-permute-start(bf16[8,101,256]{2,1,0:T(8,128)(2,1)S(1)} %get-tuple-element.74), channel_id=1, source_target_pairs={{0,1},{1,2},{4,5},{5,6},{8,9},{9,10},{12,13},{13,14},{16,17},{17,1... | collective-permute-start | bytes 1241096 | tf_op jit(solution)/shard_map/ppermute | solution.py:179
  153.0 4.0 %collective-permute-done.35 = bf16[16,48,128]{2,1,0:T(8,128)(2,1)S(1)} collective-permute-done((bf16[16,48,128]{2,1,0:T(8,128)(2,1)S(1)}, bf16[16,48,128]{2,1,0:T(8,128)(2,1)S(1)}, u32[]{:S(2)}, u32[]{:S(2)}) %collective-permute-start.35) | collective-permute-done | bytes 196640 | tf_op jit(solution)/shard_map/ppermute | solution.py:124
  158.4 4.2 %collective-permute-done.33 = bf16[16,48,128]{2,1,0:T(8,128)(2,1)S(1)} collective-permute-done((bf16[16,48,128]{2,1,0:T(8,128)(2,1)S(1)}, bf16[16,48,128]{2,1,0:T(8,128)(2,1)S(1)}, u32[]{:S(2)}, u32[]{:S(2)}) %collective-permute-start.33) | collective-permute-done | bytes 196640 | tf_op jit(solution)/shard_map/ppermute | solution.py:124
  162.9 2.1 collective-permute-start.28
  165.3 1.9 pad_maximum_fusion.source_ref
  167.2 5.8 %collective-permute-done.28 = bf16[8,101,256]{2,1,0:T(8,128)(2,1)S(1)} collective-permute-done((bf16[8,101,256]{2,1,0:T(8,128)(2,1)S(1)}, bf16[8,101,256]{2,1,0:T(8,128)(2,1)S(1)}, u32[]{:S(2)}, u32[]{:S(2)}) %collective-permute-start.28) | collective-permute-done | bytes 413728 | tf_op jit(solution)/shard_map/ppermute | solution.py:179
  173.0 17.5 %shard_map.140 = bf16[48,101,256]{2,1,0:T(8,128)(2,1)} custom-call(bf16[1,128]{1,0:T(2,128)(2,1)S(1)} %copy-done.1, bf16[112,500]{1,0:T(8,128)(2,1)S(1)} %copy-done, bf16[256,48,128]{2,1,0:T(8,128)(2,1)} %pad_maximum_fusion.source_ref, bf16[250,128,256]{2,1,0:T(8,128)(2,1)} %bitcast.73), custom_call_target="tpu_custom_call" | custom-call | flops 2813952000 | bytes 21938176 | tf_op jit(solution)/shard_map/pallas_call | solution.py:98
  192.6 5.8 %collective-permute-done.36 = bf16[16,48,128]{2,1,0:T(8,128)(2,1)S(1)} collective-permute-done((bf16[16,48,128]{2,1,0:T(8,128)(2,1)S(1)}, bf16[16,48,128]{2,1,0:T(8,128)(2,1)S(1)}, u32[]{:S(2)}, u32[]{:S(2)}) %collective-permute-start.36) | collective-permute-done | bytes 196640 | tf_op jit(solution)/shard_map/ppermute | solution.py:124
  202.8 3.5 %collective-permute-done.37 = bf16[32,48,128]{2,1,0:T(8,128)(2,1)S(1)} collective-permute-done((bf16[32,48,128]{2,1,0:T(8,128)(2,1)S(1)}, bf16[32,48,128]{2,1,0:T(8,128)(2,1)S(1)}, u32[]{:S(2)}, u32[]{:S(2)}) %collective-permute-start.37) | collective-permute-done | bytes 393248 | tf_op jit(solution)/shard_map/ppermute | solution.py:124
  208.0 5.8 %collective-permute-done.42 = bf16[12,101,256]{2,1,0:T(8,128)(2,1)S(1)} collective-permute-done((bf16[12,101,256]{2,1,0:T(8,128)(2,1)S(1)}, bf16[12,101,256]{2,1,0:T(8,128)(2,1)S(1)}, u32[]{:S(2)}, u32[]{:S(2)}) %collective-permute-start.42) | collective-permute-done | bytes 620576 | tf_op jit(solution)/shard_map/ppermute | solution.py:179
  215.5 4.6 %collective-permute-start.43 = (bf16[12,101,256]{2,1,0:T(8,128)(2,1)S(1)}, bf16[12,101,256]{2,1,0:T(8,128)(2,1)S(1)}, u32[]{:S(2)}, u32[]{:S(2)}) collective-permute-start(bf16[12,101,256]{2,1,0:T(8,128)(2,1)S(1)} %get-tuple-element.68), channel_id=1, source_target_pairs={{0,1},{1,2},{4,5},{5,6},{8,9},{9,10},{12,13},{13,14},{16,17},{17,1... | collective-permute-start | bytes 1861640 | tf_op jit(solution)/shard_map/ppermute | solution.py:179
  220.3 1.9 pad_maximum_fusion.1.source_ref
  222.2 4.9 %collective-permute-done.45 = bf16[12,101,256]{2,1,0:T(8,128)(2,1)S(1)} collective-permute-done((bf16[12,101,256]{2,1,0:T(8,128)(2,1)S(1)}, bf16[12,101,256]{2,1,0:T(8,128)(2,1)S(1)}, u32[]{:S(2)}, u32[]{:S(2)}) %collective-permute-start.45) | collective-permute-done | bytes 620576 | tf_op jit(solution)/shard_map/ppermute | solution.py:180
  228.4 17.3 %shard_map.141 = bf16[48,101,256]{2,1,0:T(8,128)(2,1)} custom-call(bf16[1,128]{1,0:T(2,128)(2,1)S(1)} %copy-done.1, bf16[112,500]{1,0:T(8,128)(2,1)S(1)} %copy-done, bf16[256,48,128]{2,1,0:T(8,128)(2,1)} %pad_maximum_fusion.1.source_ref, bf16[250,128,256]{2,1,0:T(8,128)(2,1)} %bitcast.74), custom_call_target="tpu_custom_call" | custom-call | flops 2813952000 | bytes 21938176 | tf_op jit(solution)/shard_map/pallas_call | solution.py:98
  249.2 12.9 %collective-permute-done.48 = bf16[12,101,256]{2,1,0:T(8,128)(2,1)S(1)} collective-permute-done((bf16[12,101,256]{2,1,0:T(8,128)(2,1)S(1)}, bf16[12,101,256]{2,1,0:T(8,128)(2,1)S(1)}, u32[]{:S(2)}, u32[]{:S(2)}) %collective-permute-start.48) | collective-permute-done | bytes 620576 | tf_op jit(solution)/shard_map/ppermute | solution.py:179
  262.3 1.9 collective-permute-start.49
  264.3 10.9 %collective-permute-done.49 = bf16[12,101,256]{2,1,0:T(8,128)(2,1)S(1)} collective-permute-done((bf16[12,101,256]{2,1,0:T(8,128)(2,1)S(1)}, bf16[12,101,256]{2,1,0:T(8,128)(2,1)S(1)}, u32[]{:S(2)}, u32[]{:S(2)}) %collective-permute-start.49) | collective-permute-done | bytes 620576 | tf_op jit(solution)/shard_map/ppermute | solution.py:179
  278.2 4.7 %collective-permute-start.46 = (bf16[12,101,256]{2,1,0:T(8,128)(2,1)}, bf16[12,101,256]{2,1,0:T(8,128)(2,1)}, u32[]{:S(2)}, u32[]{:S(2)}) collective-permute-start(bf16[12,101,256]{2,1,0:T(8,128)(2,1)} %get-tuple-element.61), channel_id=1, source_target_pairs={{0,1},{1,2},{2,3},{4,5},{5,6},{6,7},{8,9},{9,10},{10,11},{12,13},{... | collective-permute-start | bytes 1861640 | tf_op jit(solution)/shard_map/ppermute | solution.py:179
  282.9 2.1 collective-permute-start.47
  285.0 3.7 %collective-permute-start.50 = (bf16[12,101,256]{2,1,0:T(8,128)(2,1)S(1)}, bf16[12,101,256]{2,1,0:T(8,128)(2,1)S(1)}, u32[]{:S(2)}, u32[]{:S(2)}) collective-permute-start(bf16[12,101,256]{2,1,0:T(8,128)(2,1)S(1)} %get-tuple-element.63), channel_id=1, source_target_pairs={{0,1},{1,2},{2,3},{4,5},{5,6},{6,7},{8,9},{9,10},{10,11},{12,13},{... | collective-permute-start | bytes 1861640 | tf_op jit(solution)/shard_map/ppermute | solution.py:179
  288.7 6.0 %collective-permute-done.52 = bf16[12,101,256]{2,1,0:T(8,128)(2,1)S(1)} collective-permute-done((bf16[12,101,256]{2,1,0:T(8,128)(2,1)S(1)}, bf16[12,101,256]{2,1,0:T(8,128)(2,1)S(1)}, u32[]{:S(2)}, u32[]{:S(2)}) %collective-permute-start.52) | collective-permute-done | bytes 620576 | tf_op jit(solution)/shard_map/ppermute | solution.py:180
  295.7 1.9 collective-permute-start.53
  298.8 6.7 %collective-permute-done.47 = bf16[12,101,256]{2,1,0:T(8,128)(2,1)} collective-permute-done((bf16[12,101,256]{2,1,0:T(8,128)(2,1)}, bf16[12,101,256]{2,1,0:T(8,128)(2,1)}, u32[]{:S(2)}, u32[]{:S(2)}) %collective-permute-start.47) | collective-permute-done | bytes 620576 | tf_op jit(solution)/shard_map/ppermute | solution.py:180
  305.5 1.7 fusion.11
  307.2 5.1 %collective-permute-done.53 = bf16[12,101,256]{2,1,0:T(8,128)(2,1)} collective-permute-done((bf16[12,101,256]{2,1,0:T(8,128)(2,1)}, bf16[12,101,256]{2,1,0:T(8,128)(2,1)}, u32[]{:S(2)}, u32[]{:S(2)}) %collective-permute-start.53) | collective-permute-done | bytes 620576 | tf_op jit(solution)/shard_map/ppermute | solution.py:180
  314.0 1.6 copy.38
  (186 shorter events, 57.5 us)
Async XLA Ops:
  39.4 18.8 %collective-permute-start.8 = (bf16[32,32,128]{2,1,0:T(8,128)(2,1)S(1)}, bf16[32,32,128]{2,1,0:T(8,128)(2,1)S(1)}, u32[]{:S(2)}, u32[]{:S(2)}) collective-permute-start(bf16[32,32,128]{2,1,0:T(8,128)(2,1)S(1)} %constant_dynamic-slice_fusion.11), channel_id=1, source_target_pairs={{0,16},{4,20},{8,24},{12,28},{16,0},{20,4},{24,8},{28,12},{1,17},{... | collective-permute-start | bytes 786440 | tf_op jit(solution)/shard_map/ppermute | solution.py:124
  41.0 17.9 %collective-permute-start.4 = (bf16[32,32,128]{2,1,0:T(8,128)(2,1)S(1)}, bf16[32,32,128]{2,1,0:T(8,128)(2,1)S(1)}, u32[]{:S(2)}, u32[]{:S(2)}) collective-permute-start(bf16[32,32,128]{2,1,0:T(8,128)(2,1)S(1)} %constant_dynamic-slice_fusion.13), channel_id=1, source_target_pairs={{0,8},{4,12},{8,0},{12,4},{16,24},{20,28},{24,16},{28,20},{1,9},{5... | collective-permute-start | bytes 786440 | tf_op jit(solution)/shard_map/ppermute | solution.py:124
  58.1 19.0 %collective-permute-start.2 = (bf16[64,48,128]{2,1,0:T(8,128)(2,1)S(1)}, bf16[64,48,128]{2,1,0:T(8,128)(2,1)S(1)}, u32[]{:S(2)}, u32[]{:S(2)}) collective-permute-start(bf16[64,48,128]{2,1,0:T(8,128)(2,1)S(1)} %constant_dynamic-slice_fusion.15), channel_id=1, source_target_pairs={{0,4},{4,0},{8,12},{12,8},{16,20},{20,16},{24,28},{28,24},{1,5},{5... | collective-permute-start | bytes 2359304 | tf_op jit(solution)/shard_map/ppermute | solution.py:124
  58.3 6.0 %collective-permute-start.9 = (bf16[16,32,128]{2,1,0:T(8,128)(2,1)S(1)}, bf16[16,32,128]{2,1,0:T(8,128)(2,1)S(1)}, u32[]{:S(2)}, u32[]{:S(2)}) collective-permute-start(bf16[16,32,128]{2,1,0:T(8,128)(2,1)S(1)} %constant_dynamic-slice_fusion.10), channel_id=1, source_target_pairs={{0,8},{4,12},{8,0},{12,4},{16,24},{20,28},{24,16},{28,20},{1,9},{5... | collective-permute-start | bytes 393224 | tf_op jit(solution)/shard_map/ppermute | solution.py:124
  59.0 5.9 %collective-permute-start.5 = (bf16[16,32,128]{2,1,0:T(8,128)(2,1)S(1)}, bf16[16,32,128]{2,1,0:T(8,128)(2,1)S(1)}, u32[]{:S(2)}, u32[]{:S(2)}) collective-permute-start(bf16[16,32,128]{2,1,0:T(8,128)(2,1)S(1)} %constant_dynamic-slice_fusion.12), channel_id=1, source_target_pairs={{0,16},{4,20},{8,24},{12,28},{16,0},{20,4},{24,8},{28,12},{1,17},{... | collective-permute-start | bytes 393224 | tf_op jit(solution)/shard_map/ppermute | solution.py:124
  69.5 7.1 %collective-permute-start.11 = (bf16[32,32,128]{2,1,0:T(8,128)(2,1)S(1)}, bf16[32,32,128]{2,1,0:T(8,128)(2,1)S(1)}, u32[]{:S(2)}, u32[]{:S(2)}) collective-permute-start(bf16[32,32,128]{2,1,0:T(8,128)(2,1)S(1)} %pad_maximum_fusion.15), channel_id=1, source_target_pairs={{0,16},{4,20},{8,24},{12,28},{16,0},{20,4},{24,8},{28,12},{1,17},{... | collective-permute-start | bytes 786440 | tf_op jit(solution)/shard_map/ppermute | solution.py:124
  70.1 6.8 %collective-permute-start.7 = (bf16[32,32,128]{2,1,0:T(8,128)(2,1)S(1)}, bf16[32,32,128]{2,1,0:T(8,128)(2,1)S(1)}, u32[]{:S(2)}, u32[]{:S(2)}) collective-permute-start(bf16[32,32,128]{2,1,0:T(8,128)(2,1)S(1)} %pad_maximum_fusion.14), channel_id=1, source_target_pairs={{0,8},{4,12},{8,0},{12,4},{16,24},{20,28},{24,16},{28,20},{1,9},{5... | collective-permute-start | bytes 786440 | tf_op jit(solution)/shard_map/ppermute | solution.py:124
  77.7 18.3 %collective-permute-start.14 = (bf16[32,48,128]{2,1,0:T(8,128)(2,1)S(1)}, bf16[32,48,128]{2,1,0:T(8,128)(2,1)S(1)}, u32[]{:S(2)}, u32[]{:S(2)}) collective-permute-start(bf16[32,48,128]{2,1,0:T(8,128)(2,1)S(1)} %constant_dynamic-slice_fusion.7), channel_id=1, source_target_pairs={{0,16},{4,20},{8,24},{12,28},{16,0},{20,4},{24,8},{28,12},{1,17},{... | collective-permute-start | bytes 1179656 | tf_op jit(solution)/shard_map/ppermute | solution.py:124
  79.2 17.4 %collective-permute-start.12 = (bf16[32,48,128]{2,1,0:T(8,128)(2,1)S(1)}, bf16[32,48,128]{2,1,0:T(8,128)(2,1)S(1)}, u32[]{:S(2)}, u32[]{:S(2)}) collective-permute-start(bf16[32,48,128]{2,1,0:T(8,128)(2,1)S(1)} %constant_dynamic-slice_fusion.9), channel_id=1, source_target_pairs={{0,8},{4,12},{8,0},{12,4},{16,24},{20,28},{24,16},{28,20},{1,9},{5... | collective-permute-start | bytes 1179656 | tf_op jit(solution)/shard_map/ppermute | solution.py:124
  79.8 18.5 %collective-permute-start.16 = (bf16[64,32,128]{2,1,0:T(8,128)(2,1)S(1)}, bf16[64,32,128]{2,1,0:T(8,128)(2,1)S(1)}, u32[]{:S(2)}, u32[]{:S(2)}) collective-permute-start(bf16[64,32,128]{2,1,0:T(8,128)(2,1)S(1)} %get-tuple-element.38), channel_id=1, source_target_pairs={{0,4},{4,0},{8,12},{12,8},{16,20},{20,16},{24,28},{28,24},{1,5},{5... | collective-permute-start | bytes 1572872 | tf_op jit(solution)/shard_map/ppermute | solution.py:124
  79.8 19.2 %collective-permute-start.17 = (bf16[64,32,128]{2,1,0:T(8,128)(2,1)S(1)}, bf16[64,32,128]{2,1,0:T(8,128)(2,1)S(1)}, u32[]{:S(2)}, u32[]{:S(2)}) collective-permute-start(bf16[64,32,128]{2,1,0:T(8,128)(2,1)S(1)} %get-tuple-element.39), channel_id=1, source_target_pairs={{0,4},{4,0},{8,12},{12,8},{16,20},{20,16},{24,28},{28,24},{1,5},{5... | collective-permute-start | bytes 1572872 | tf_op jit(solution)/shard_map/ppermute | solution.py:124
  95.8 22.3 %collective-permute-start.18 = (bf16[64,48,128]{2,1,0:T(8,128)(2,1)S(1)}, bf16[64,48,128]{2,1,0:T(8,128)(2,1)S(1)}, u32[]{:S(2)}, u32[]{:S(2)}) collective-permute-start(bf16[64,48,128]{2,1,0:T(8,128)(2,1)S(1)} %constant_dynamic-slice_fusion.5), channel_id=1, source_target_pairs={{0,4},{4,0},{8,12},{12,8},{16,20},{20,16},{24,28},{28,24},{1,5},{5... | collective-permute-start | bytes 2359304 | tf_op jit(solution)/shard_map/ppermute | solution.py:124
  95.9 23.7 %collective-permute-start.19 = (bf16[64,48,128]{2,1,0:T(8,128)(2,1)S(1)}, bf16[64,48,128]{2,1,0:T(8,128)(2,1)S(1)}, u32[]{:S(2)}, u32[]{:S(2)}) collective-permute-start(bf16[64,48,128]{2,1,0:T(8,128)(2,1)S(1)} %constant_dynamic-slice_fusion.4), channel_id=1, source_target_pairs={{0,4},{4,0},{8,12},{12,8},{16,20},{20,16},{24,28},{28,24},{1,5},{5... | collective-permute-start | bytes 2359304 | tf_op jit(solution)/shard_map/ppermute | solution.py:124
  96.6 17.8 %collective-permute-start.15 = (bf16[16,48,128]{2,1,0:T(8,128)(2,1)S(1)}, bf16[16,48,128]{2,1,0:T(8,128)(2,1)S(1)}, u32[]{:S(2)}, u32[]{:S(2)}) collective-permute-start(bf16[16,48,128]{2,1,0:T(8,128)(2,1)S(1)} %constant_dynamic-slice_fusion.6), channel_id=1, source_target_pairs={{0,8},{4,12},{8,0},{12,4},{16,24},{20,28},{24,16},{28,20},{1,9},{5... | collective-permute-start | bytes 589832 | tf_op jit(solution)/shard_map/ppermute | solution.py:124
  98.3 16.1 %collective-permute-start.13 = (bf16[16,48,128]{2,1,0:T(8,128)(2,1)S(1)}, bf16[16,48,128]{2,1,0:T(8,128)(2,1)S(1)}, u32[]{:S(2)}, u32[]{:S(2)}) collective-permute-start(bf16[16,48,128]{2,1,0:T(8,128)(2,1)S(1)} %constant_dynamic-slice_fusion.8), channel_id=1, source_target_pairs={{0,16},{4,20},{8,24},{12,28},{16,0},{20,4},{24,8},{28,12},{1,17},{... | collective-permute-start | bytes 589832 | tf_op jit(solution)/shard_map/ppermute | solution.py:124
  114.5 6.4 %collective-permute-start.20 = (bf16[16,48,128]{2,1,0:T(8,128)(2,1)S(1)}, bf16[16,48,128]{2,1,0:T(8,128)(2,1)S(1)}, u32[]{:S(2)}, u32[]{:S(2)}) collective-permute-start(bf16[16,48,128]{2,1,0:T(8,128)(2,1)S(1)} %add_convert_fusion.15), channel_id=1, source_target_pairs={{0,16},{4,20},{8,24},{12,28},{16,0},{20,4},{24,8},{28,12},{1,17},{... | collective-permute-start | bytes 589832 | tf_op jit(solution)/shard_map/ppermute | solution.py:124
  116.1 6.4 %collective-permute-start.22 = (bf16[16,48,128]{2,1,0:T(8,128)(2,1)S(1)}, bf16[16,48,128]{2,1,0:T(8,128)(2,1)S(1)}, u32[]{:S(2)}, u32[]{:S(2)}) collective-permute-start(bf16[16,48,128]{2,1,0:T(8,128)(2,1)S(1)} %add_convert_fusion.14), channel_id=1, source_target_pairs={{0,8},{4,12},{8,0},{12,4},{16,24},{20,28},{24,16},{28,20},{1,9},{5... | collective-permute-start | bytes 589832 | tf_op jit(solution)/shard_map/ppermute | solution.py:124
  117.5 5.8 %collective-permute-start.29 = (bf16[8,101,256]{2,1,0:T(8,128)(2,1)S(1)}, bf16[8,101,256]{2,1,0:T(8,128)(2,1)S(1)}, u32[]{:S(2)}, u32[]{:S(2)}) collective-permute-start(bf16[8,101,256]{2,1,0:T(8,128)(2,1)S(1)} %get-tuple-element.75), channel_id=1, source_target_pairs={{3,2},{7,6},{11,10},{15,14},{19,18},{23,22},{27,26},{31,30}} | collective-permute-start | bytes 1241096 | tf_op jit(solution)/shard_map/ppermute | solution.py:180
  118.2 18.8 %collective-permute-start.26 = (bf16[8,101,256]{2,1,0:T(8,128)(2,1)}, bf16[8,101,256]{2,1,0:T(8,128)(2,1)}, u32[]{:S(2)}, u32[]{:S(2)}) collective-permute-start(bf16[8,101,256]{2,1,0:T(8,128)(2,1)} %get-tuple-element.76), channel_id=1, source_target_pairs={{0,1},{4,5},{8,9},{12,13},{16,17},{20,21},{24,25},{28,29}} | collective-permute-start | bytes 1241096 | tf_op jit(solution)/shard_map/ppermute | solution.py:179
  121.0 9.7 %collective-permute-start.21 = (bf16[32,48,128]{2,1,0:T(8,128)(2,1)S(1)}, bf16[32,48,128]{2,1,0:T(8,128)(2,1)S(1)}, u32[]{:S(2)}, u32[]{:S(2)}) collective-permute-start(bf16[32,48,128]{2,1,0:T(8,128)(2,1)S(1)} %pad_maximum_fusion.10), channel_id=1, source_target_pairs={{0,8},{4,12},{8,0},{12,4},{16,24},{20,28},{24,16},{28,20},{1,9},{5... | collective-permute-start | bytes 1179656 | tf_op jit(solution)/shard_map/ppermute | solution.py:124
  122.5 9.4 %collective-permute-start.23 = (bf16[32,48,128]{2,1,0:T(8,128)(2,1)S(1)}, bf16[32,48,128]{2,1,0:T(8,128)(2,1)S(1)}, u32[]{:S(2)}, u32[]{:S(2)}) collective-permute-start(bf16[32,48,128]{2,1,0:T(8,128)(2,1)S(1)} %pad_maximum_fusion.11), channel_id=1, source_target_pairs={{0,16},{4,20},{8,24},{12,28},{16,0},{20,4},{24,8},{28,12},{1,17},{... | collective-permute-start | bytes 1179656 | tf_op jit(solution)/shard_map/ppermute | solution.py:124
  124.1 18.6 %collective-permute-start.30 = (bf16[8,101,256]{2,1,0:T(8,128)(2,1)}, bf16[8,101,256]{2,1,0:T(8,128)(2,1)}, u32[]{:S(2)}, u32[]{:S(2)}) collective-permute-start(bf16[8,101,256]{2,1,0:T(8,128)(2,1)} %fusion.12), channel_id=1, source_target_pairs={{3,2},{2,1},{7,6},{6,5},{11,10},{10,9},{15,14},{14,13},{19,18},{18... | collective-permute-start | bytes 1241096 | tf_op jit(solution)/shard_map/ppermute | solution.py:180
  134.7 11.2 %collective-permute-start.34 = (bf16[32,48,128]{2,1,0:T(8,128)(2,1)}, bf16[32,48,128]{2,1,0:T(8,128)(2,1)}, u32[]{:S(2)}, u32[]{:S(2)}) collective-permute-start(bf16[32,48,128]{2,1,0:T(8,128)(2,1)} %constant_dynamic-slice_fusion.1), channel_id=1, source_target_pairs={{0,16},{4,20},{8,24},{12,28},{16,0},{20,4},{24,8},{28,12},{1,17},{... | collective-permute-start | bytes 1179656 | tf_op jit(solution)/shard_map/ppermute | solution.py:124
  135.4 15.8 %collective-permute-start.32 = (bf16[32,48,128]{2,1,0:T(8,128)(2,1)S(1)}, bf16[32,48,128]{2,1,0:T(8,128)(2,1)S(1)}, u32[]{:S(2)}, u32[]{:S(2)}) collective-permute-start(bf16[32,48,128]{2,1,0:T(8,128)(2,1)S(1)} %constant_dynamic-slice_fusion.3), channel_id=1, source_target_pairs={{0,8},{4,12},{8,0},{12,4},{16,24},{20,28},{24,16},{28,20},{1,9},{5... | collective-permute-start | bytes 1179656 | tf_op jit(solution)/shard_map/ppermute | solution.py:124
  137.0 28.0 %collective-permute-start.24 = (bf16[64,48,128]{2,1,0:T(8,128)(2,1)}, bf16[64,48,128]{2,1,0:T(8,128)(2,1)S(1)}, u32[]{:S(2)}, u32[]{:S(2)}) collective-permute-start(bf16[64,48,128]{2,1,0:T(8,128)(2,1)} %pad_maximum_fusion.4), channel_id=1, source_target_pairs={{0,4},{4,0},{8,12},{12,8},{16,20},{20,16},{24,28},{28,24},{1,5},{5... | collective-permute-start | bytes 2359304 | tf_op jit(solution)/shard_map/ppermute | solution.py:124
  137.0 28.2 %collective-permute-start.25 = (bf16[64,48,128]{2,1,0:T(8,128)(2,1)}, bf16[64,48,128]{2,1,0:T(8,128)(2,1)S(1)}, u32[]{:S(2)}, u32[]{:S(2)}) collective-permute-start(bf16[64,48,128]{2,1,0:T(8,128)(2,1)} %pad_maximum_fusion.5), channel_id=1, source_target_pairs={{0,4},{4,0},{8,12},{12,8},{16,20},{20,16},{24,28},{28,24},{1,5},{5... | collective-permute-start | bytes 2359304 | tf_op jit(solution)/shard_map/ppermute | solution.py:124
  144.1 23.1 %collective-permute-start.31 = (bf16[8,101,256]{2,1,0:T(8,128)(2,1)S(1)}, bf16[8,101,256]{2,1,0:T(8,128)(2,1)S(1)}, u32[]{:S(2)}, u32[]{:S(2)}) collective-permute-start(bf16[8,101,256]{2,1,0:T(8,128)(2,1)S(1)} %get-tuple-element.73), channel_id=1, source_target_pairs={{3,2},{2,1},{1,0},{7,6},{6,5},{5,4},{11,10},{10,9},{9,8},{15,14},{... | collective-permute-start | bytes 1241096 | tf_op jit(solution)/shard_map/ppermute | solution.py:180
  146.0 16.7 %collective-permute-start.27 = (bf16[8,101,256]{2,1,0:T(8,128)(2,1)S(1)}, bf16[8,101,256]{2,1,0:T(8,128)(2,1)S(1)}, u32[]{:S(2)}, u32[]{:S(2)}) collective-permute-start(bf16[8,101,256]{2,1,0:T(8,128)(2,1)S(1)} %get-tuple-element.74), channel_id=1, source_target_pairs={{0,1},{1,2},{4,5},{5,6},{8,9},{9,10},{12,13},{13,14},{16,17},{17,1... | collective-permute-start | bytes 1241096 | tf_op jit(solution)/shard_map/ppermute | solution.py:179
  151.3 5.7 %collective-permute-start.35 = (bf16[16,48,128]{2,1,0:T(8,128)(2,1)S(1)}, bf16[16,48,128]{2,1,0:T(8,128)(2,1)S(1)}, u32[]{:S(2)}, u32[]{:S(2)}) collective-permute-start(bf16[16,48,128]{2,1,0:T(8,128)(2,1)S(1)} %constant_dynamic-slice_fusion), channel_id=1, source_target_pairs={{0,8},{4,12},{8,0},{12,4},{16,24},{20,28},{24,16},{28,20},{1,9},{5... | collective-permute-start | bytes 589832 | tf_op jit(solution)/shard_map/ppermute | solution.py:124
  162.9 10.2 %collective-permute-start.28 = (bf16[8,101,256]{2,1,0:T(8,128)(2,1)S(1)}, bf16[8,101,256]{2,1,0:T(8,128)(2,1)S(1)}, u32[]{:S(2)}, u32[]{:S(2)}) collective-permute-start(bf16[8,101,256]{2,1,0:T(8,128)(2,1)S(1)} %fusion.15), channel_id=1, source_target_pairs={{0,1},{1,2},{2,3},{4,5},{5,6},{6,7},{8,9},{9,10},{10,11},{12,13},{... | collective-permute-start | bytes 1241096 | tf_op jit(solution)/shard_map/ppermute | solution.py:179
  190.5 7.9 %collective-permute-start.36 = (bf16[16,48,128]{2,1,0:T(8,128)(2,1)S(1)}, bf16[16,48,128]{2,1,0:T(8,128)(2,1)S(1)}, u32[]{:S(2)}, u32[]{:S(2)}) collective-permute-start(bf16[16,48,128]{2,1,0:T(8,128)(2,1)S(1)} %add_convert_fusion.13), channel_id=1, source_target_pairs={{0,16},{4,20},{8,24},{12,28},{16,0},{20,4},{24,8},{28,12},{1,17},{... | collective-permute-start | bytes 589832 | tf_op jit(solution)/shard_map/ppermute | solution.py:124
  191.9 7.9 %collective-permute-start.39 = (bf16[16,48,128]{2,1,0:T(8,128)(2,1)S(1)}, bf16[16,48,128]{2,1,0:T(8,128)(2,1)S(1)}, u32[]{:S(2)}, u32[]{:S(2)}) collective-permute-start(bf16[16,48,128]{2,1,0:T(8,128)(2,1)S(1)} %add_convert_fusion.12), channel_id=1, source_target_pairs={{0,8},{4,12},{8,0},{12,4},{16,24},{20,28},{24,16},{28,20},{1,9},{5... | collective-permute-start | bytes 589832 | tf_op jit(solution)/shard_map/ppermute | solution.py:124
  198.5 7.8 %collective-permute-start.37 = (bf16[32,48,128]{2,1,0:T(8,128)(2,1)S(1)}, bf16[32,48,128]{2,1,0:T(8,128)(2,1)S(1)}, u32[]{:S(2)}, u32[]{:S(2)}) collective-permute-start(bf16[32,48,128]{2,1,0:T(8,128)(2,1)S(1)} %pad_maximum_fusion.12), channel_id=1, source_target_pairs={{0,8},{4,12},{8,0},{12,4},{16,24},{20,28},{24,16},{28,20},{1,9},{5... | collective-permute-start | bytes 1179656 | tf_op jit(solution)/shard_map/ppermute | solution.py:124
  200.0 7.8 %collective-permute-start.40 = (bf16[32,48,128]{2,1,0:T(8,128)(2,1)S(1)}, bf16[32,48,128]{2,1,0:T(8,128)(2,1)S(1)}, u32[]{:S(2)}, u32[]{:S(2)}) collective-permute-start(bf16[32,48,128]{2,1,0:T(8,128)(2,1)S(1)} %pad_maximum_fusion.13), channel_id=1, source_target_pairs={{0,16},{4,20},{8,24},{12,28},{16,0},{20,4},{24,8},{28,12},{1,17},{... | collective-permute-start | bytes 1179656 | tf_op jit(solution)/shard_map/ppermute | solution.py:124
  200.8 7.2 %collective-permute-start.44 = (bf16[12,101,256]{2,1,0:T(8,128)(2,1)S(1)}, bf16[12,101,256]{2,1,0:T(8,128)(2,1)S(1)}, u32[]{:S(2)}, u32[]{:S(2)}) collective-permute-start(bf16[12,101,256]{2,1,0:T(8,128)(2,1)S(1)} %get-tuple-element.69), channel_id=1, source_target_pairs={{3,2},{7,6},{11,10},{15,14},{19,18},{23,22},{27,26},{31,30}} | collective-permute-start | bytes 1861640 | tf_op jit(solution)/shard_map/ppermute | solution.py:180
  201.5 12.3 %collective-permute-start.42 = (bf16[12,101,256]{2,1,0:T(8,128)(2,1)S(1)}, bf16[12,101,256]{2,1,0:T(8,128)(2,1)S(1)}, u32[]{:S(2)}, u32[]{:S(2)}) collective-permute-start(bf16[12,101,256]{2,1,0:T(8,128)(2,1)S(1)} %get-tuple-element.70), channel_id=1, source_target_pairs={{0,1},{4,5},{8,9},{12,13},{16,17},{20,21},{24,25},{28,29}} | collective-permute-start | bytes 1861640 | tf_op jit(solution)/shard_map/ppermute | solution.py:179
  206.4 13.6 %collective-permute-start.38 = (bf16[64,48,128]{2,1,0:T(8,128)(2,1)S(1)}, bf16[64,48,128]{2,1,0:T(8,128)(2,1)S(1)}, u32[]{:S(2)}, u32[]{:S(2)}) collective-permute-start(bf16[64,48,128]{2,1,0:T(8,128)(2,1)S(1)} %pad_maximum_fusion.6), channel_id=1, source_target_pairs={{0,4},{4,0},{8,12},{12,8},{16,20},{20,16},{24,28},{28,24},{1,5},{5... | collective-permute-start | bytes 2359304 | tf_op jit(solution)/shard_map/ppermute | solution.py:124
  207.9 12.2 %collective-permute-start.41 = (bf16[64,48,128]{2,1,0:T(8,128)(2,1)S(1)}, bf16[64,48,128]{2,1,0:T(8,128)(2,1)S(1)}, u32[]{:S(2)}, u32[]{:S(2)}) collective-permute-start(bf16[64,48,128]{2,1,0:T(8,128)(2,1)S(1)} %pad_maximum_fusion.7), channel_id=1, source_target_pairs={{0,4},{4,0},{8,12},{12,8},{16,20},{20,16},{24,28},{28,24},{1,5},{5... | collective-permute-start | bytes 2359304 | tf_op jit(solution)/shard_map/ppermute | solution.py:124
  214.2 12.9 %collective-permute-start.45 = (bf16[12,101,256]{2,1,0:T(8,128)(2,1)S(1)}, bf16[12,101,256]{2,1,0:T(8,128)(2,1)S(1)}, u32[]{:S(2)}, u32[]{:S(2)}) collective-permute-start(bf16[12,101,256]{2,1,0:T(8,128)(2,1)S(1)} %get-tuple-element.67), channel_id=1, source_target_pairs={{3,2},{2,1},{7,6},{6,5},{11,10},{10,9},{15,14},{14,13},{19,18},{18... | collective-permute-start | bytes 1861640 | tf_op jit(solution)/shard_map/ppermute | solution.py:180
  215.5 12.9 %collective-permute-start.43 = (bf16[12,101,256]{2,1,0:T(8,128)(2,1)S(1)}, bf16[12,101,256]{2,1,0:T(8,128)(2,1)S(1)}, u32[]{:S(2)}, u32[]{:S(2)}) collective-permute-start(bf16[12,101,256]{2,1,0:T(8,128)(2,1)S(1)} %get-tuple-element.68), channel_id=1, source_target_pairs={{0,1},{1,2},{4,5},{5,6},{8,9},{9,10},{12,13},{13,14},{16,17},{17,1... | collective-permute-start | bytes 1861640 | tf_op jit(solution)/shard_map/ppermute | solution.py:179
  247.2 14.9 %collective-permute-start.48 = (bf16[12,101,256]{2,1,0:T(8,128)(2,1)S(1)}, bf16[12,101,256]{2,1,0:T(8,128)(2,1)S(1)}, u32[]{:S(2)}, u32[]{:S(2)}) collective-permute-start(bf16[12,101,256]{2,1,0:T(8,128)(2,1)S(1)} %get-tuple-element.65), channel_id=1, source_target_pairs={{0,1},{4,5},{8,9},{12,13},{16,17},{20,21},{24,25},{28,29}} | collective-permute-start | bytes 1861640 | tf_op jit(solution)/shard_map/ppermute | solution.py:179
  248.5 15.7 %collective-permute-start.51 = (bf16[12,101,256]{2,1,0:T(8,128)(2,1)S(1)}, bf16[12,101,256]{2,1,0:T(8,128)(2,1)S(1)}, u32[]{:S(2)}, u32[]{:S(2)}) collective-permute-start(bf16[12,101,256]{2,1,0:T(8,128)(2,1)S(1)} %get-tuple-element.66), channel_id=1, source_target_pairs={{3,2},{7,6},{11,10},{15,14},{19,18},{23,22},{27,26},{31,30}} | collective-permute-start | bytes 1861640 | tf_op jit(solution)/shard_map/ppermute | solution.py:180
  262.3 12.8 %collective-permute-start.49 = (bf16[12,101,256]{2,1,0:T(8,128)(2,1)S(1)}, bf16[12,101,256]{2,1,0:T(8,128)(2,1)S(1)}, u32[]{:S(2)}, u32[]{:S(2)}) collective-permute-start(bf16[12,101,256]{2,1,0:T(8,128)(2,1)S(1)} %fusion.2), channel_id=1, source_target_pairs={{0,1},{1,2},{4,5},{5,6},{8,9},{9,10},{12,13},{13,14},{16,17},{17,1... | collective-permute-start | bytes 1861640 | tf_op jit(solution)/shard_map/ppermute | solution.py:179
  275.5 19.2 %collective-permute-start.52 = (bf16[12,101,256]{2,1,0:T(8,128)(2,1)S(1)}, bf16[12,101,256]{2,1,0:T(8,128)(2,1)S(1)}, u32[]{:S(2)}, u32[]{:S(2)}) collective-permute-start(bf16[12,101,256]{2,1,0:T(8,128)(2,1)S(1)} %get-tuple-element.64), channel_id=1, source_target_pairs={{3,2},{2,1},{7,6},{6,5},{11,10},{10,9},{15,14},{14,13},{19,18},{18... | collective-permute-start | bytes 1861640 | tf_op jit(solution)/shard_map/ppermute | solution.py:180
  278.2 20.6 %collective-permute-start.46 = (bf16[12,101,256]{2,1,0:T(8,128)(2,1)}, bf16[12,101,256]{2,1,0:T(8,128)(2,1)}, u32[]{:S(2)}, u32[]{:S(2)}) collective-permute-start(bf16[12,101,256]{2,1,0:T(8,128)(2,1)} %get-tuple-element.61), channel_id=1, source_target_pairs={{0,1},{1,2},{2,3},{4,5},{5,6},{6,7},{8,9},{9,10},{10,11},{12,13},{... | collective-permute-start | bytes 1861640 | tf_op jit(solution)/shard_map/ppermute | solution.py:179
  282.9 22.6 %collective-permute-start.47 = (bf16[12,101,256]{2,1,0:T(8,128)(2,1)}, bf16[12,101,256]{2,1,0:T(8,128)(2,1)}, u32[]{:S(2)}, u32[]{:S(2)}) collective-permute-start(bf16[12,101,256]{2,1,0:T(8,128)(2,1)} %get-tuple-element.62), channel_id=1, source_target_pairs={{3,2},{2,1},{1,0},{7,6},{6,5},{5,4},{11,10},{10,9},{9,8},{15,14},{... | collective-permute-start | bytes 1861640 | tf_op jit(solution)/shard_map/ppermute | solution.py:180
  285.0 22.2 %collective-permute-start.50 = (bf16[12,101,256]{2,1,0:T(8,128)(2,1)S(1)}, bf16[12,101,256]{2,1,0:T(8,128)(2,1)S(1)}, u32[]{:S(2)}, u32[]{:S(2)}) collective-permute-start(bf16[12,101,256]{2,1,0:T(8,128)(2,1)S(1)} %get-tuple-element.63), channel_id=1, source_target_pairs={{0,1},{1,2},{2,3},{4,5},{5,6},{6,7},{8,9},{9,10},{10,11},{12,13},{... | collective-permute-start | bytes 1861640 | tf_op jit(solution)/shard_map/ppermute | solution.py:179
  295.7 16.7 %collective-permute-start.53 = (bf16[12,101,256]{2,1,0:T(8,128)(2,1)}, bf16[12,101,256]{2,1,0:T(8,128)(2,1)}, u32[]{:S(2)}, u32[]{:S(2)}) collective-permute-start(bf16[12,101,256]{2,1,0:T(8,128)(2,1)} %fusion.1), channel_id=1, source_target_pairs={{3,2},{2,1},{1,0},{7,6},{6,5},{5,4},{11,10},{10,9},{9,8},{15,14},{... | collective-permute-start | bytes 1861640 | tf_op jit(solution)/shard_map/ppermute | solution.py:180
  (18 other events, 137.7 us)

commit v5 on v4

--- a/solution.py
+++ b/solution.py
@@ -11,8 +11,8 @@
 
 LAGS = 101
 SRC_BLK = 64
-ROWS = (8, 12, 12)
-AHEAD = (3, 2)
+ROWS = (20, 12)
+AHEAD = (2,)
 PAD = 256
 MIB = 1024 * 1024
 
@@ -107,7 +107,7 @@
         out_specs=pl.BlockSpec((rows, LAGS, width), lambda i: (0, 0, 0)),
         out_shape=jax.ShapeDtypeStruct((rows, LAGS, width), jnp.bfloat16),
         scratch_shapes=[pltpu.VMEM((width // 128, rows * stride, 128), jnp.float32)],
-        compiler_params=pltpu.CompilerParams(vmem_limit_bytes=52 * MIB),
+        compiler_params=pltpu.CompilerParams(vmem_limit_bytes=58 * MIB),
         cost_estimate=pl.CostEstimate(
             flops=2 * bin_count * 2 * rows * depth * width + 2 * 2 * bin_count * rows * LAGS * width,
             bytes_accessed=2 * bin_count * depth * (width + rows) + 2 * rows * LAGS * width,

time: 317 us -> 321 us (1.013)
  waiting for transfers between devices: 105 us -> 133 us
  Pallas kernels: 87.2 us -> 66 us
  starting transfers between devices: 64.6 us -> 44.8 us
  other arithmetic: 26 us -> 38 us
  local copies, waits for them, and re-layouts: 31.7 us -> 37.3 us
    ppermute x9 -> x6, waiting for transfers between devices: 36.8 us -> 52.2 us  [chain_steps(): lax.ppermute(to_right, axis, [(i, i + 1) for i in range(t + 1)])]
    pallas_call x3 -> x2, Pallas kernels: 38.8 us -> 26.5 us  [pick_sources(): pl.pallas_call(pick_kernel, grid=(bin_count // bins,), in_specs=[pl.Block...]
    ppermute x36 -> x24, waiting for transfers between devices: 40.5 us -> 52.7 us  [swap(): lax.ppermute(x, axis, [(i, i ^ 1 << bit) for i in range(lax.axis_size(axi...]
    ppermute x9 -> x6, starting transfers between devices: 24.9 us -> 15.8 us  [chain_steps(): lax.ppermute(to_right, axis, [(i, i + 1) for i in range(t + 1)])]
    pallas_call x3 -> x2, Pallas kernels: 48.5 us -> 39.5 us  [correlate(): pl.pallas_call(functools.partial(correlate_kernel, stride, bin_count), gr...]
    convert_element_type x26 -> x17, other arithmetic: 8.65 us -> 17.1 us  [add(): return (a.astype(jnp.float32) + b.astype(jnp.float32)).astype(jnp.bfloat16)]
    ppermute x36 -> x24, starting transfers between devices: 27.8 us -> 20 us  [swap(): lax.ppermute(x, axis, [(i, i ^ 1 << bit) for i in range(lax.axis_size(axi...]
    select_n x18 -> x12, other arithmetic: 1.14 us -> 4.48 us  [double(): jnp.where(side == 0, current, other)]
  transfers between devices with their start and end apart: 54 -> 36, of which waited for: 23 -> 21; matrix products, arithmetic and copies ran while one was open for 9% -> 10% of each run, Pallas kernels for 13% -> 4%
where the time goes in v5:
time: 321 us; the launch traced here: 320 us
  waiting for transfers between devices  133 us (41%)
  Pallas kernels  66 us (21%)
  starting transfers between devices  44.8 us (14%)
  other arithmetic  38 us (12%)
  local copies, waits for them, and re-layouts  37.3 us (12%)
    ppermute x24, waiting for transfers between devices, swap(): lax.ppermute(x, axis, [(i, i ^ 1 << bit) for i in range(lax.axis_size(axi...  52.7 us
    ppermute x6, waiting for transfers between devices, chain_steps(): lax.ppermute(to_right, axis, [(i, i + 1) for i in range(t + 1)])  52.2 us
    pallas_call x2, Pallas kernels, correlate(): pl.pallas_call(functools.partial(correlate_kernel, stride, bin_count), gr...  39.5 us
    ppermute x6, waiting for transfers between devices, chain_steps(): lax.ppermute(to_left, axis, [(n - 1 - i, n - 2 - i) for i in range(t + 1)])  28 us
    pallas_call x2, Pallas kernels, pick_sources(): pl.pallas_call(pick_kernel, grid=(bin_count // bins,), in_specs=[pl.Block...  26.5 us
    ppermute x24, starting transfers between devices, swap(): lax.ppermute(x, axis, [(i, i ^ 1 << bit) for i in range(lax.axis_size(axi...  20 us
    convert_element_type x17, other arithmetic, add(): return (a.astype(jnp.float32) + b.astype(jnp.float32)).astype(jnp.bfloat16)  17.1 us
    transpose x1, local copies, waits for them, and re-layouts, body(): x = spectra.transpose(2, 1, 0, 3).reshape(bin_count, depth, width)  16.5 us
  transfers between devices with their start and end apart: 36, of which 21 were waited for; matrix products, arithmetic and copies ran while one was open for 10% of the time, Pallas kernels for 4%

profile of v5, /device:TPU:8, one launch (start us, length us, event | category | flops | bytes accessed | tf_op | source)
XLA Modules:
  0.0 319.5 jit_solution(5737235670741632382)
XLA Ops:
  1.4 2.0 fusion.15
  4.2 16.5 %copy.27 = bf16[250,2,64,256]{3,2,1,0:T(8,128)(2,1)} copy(bf16[250,2,64,256]{3,1,0,2:T(2,128)(2,1)} %bitcast.57) | data formatting | bytes 32768000 | tf_op jit(solution)/shard_map/transpose | solution.py:211
  20.7 13.4 %shard_map.109 = bf16[256,80,128]{2,1,0:T(8,128)(2,1)} custom-call(bf16[80,256]{1,0:T(8,128)(2,1)S(1)} %fusion.12.pick_ref, f32[1,128]{1,0:T(1,128)S(1)} %broadcast_in_dim_tile.3.keep_ref, bf16[250,128,256]{2,1,0:T(8,128)(2,1)} %bitcast.44), custom_call_target="tpu_custom_call" | custom-call | flops 1310720000 | bytes 21504000 | tf_op jit(solution)/shard_map/pallas_call | solution.py:40
  34.2 4.9 %fusion.18 = (bf16[128,80,128]{2,1,0:T(8,128)(2,1)S(1)}, bf16[128,80,128]{2,1,0:T(8,128)(2,1)}) fusion(bf16[256,80,128]{2,1,0:T(8,128)(2,1)} %shard_map.109), kind=kLoop, calls=%fused_computation.95 | loop fusion | bytes 10485760 | tf_op jit(solution)/shard_map/slice | solution.py:153
  39.1 2.5 constant_dynamic-slice_fusion.11
  44.9 2.1 add_convert_fusion.1
  47.0 1.7 add_convert_fusion
  48.7 1.6 collective-permute-start.4
  50.3 1.6 collective-permute-start.8
  51.9 13.0 %shard_map.110 = bf16[256,48,128]{2,1,0:T(8,128)(2,1)} custom-call(bf16[48,256]{1,0:T(8,128)(2,1)S(1)} %fusion.13.pick_ref, f32[1,128]{1,0:T(1,128)S(1)} %broadcast_in_dim_tile.3.keep_ref, bf16[250,128,256]{2,1,0:T(8,128)(2,1)} %bitcast.45), custom_call_target="tpu_custom_call" | custom-call | flops 786432000 | bytes 19456000 | tf_op jit(solution)/shard_map/pallas_call | solution.py:40
  64.9 2.4 fusion.19
  69.1 8.7 %collective-permute-done.5 = bf16[16,80,128]{2,1,0:T(8,128)(2,1)S(1)} collective-permute-done((bf16[16,80,128]{2,1,0:T(8,128)(2,1)S(1)}, bf16[16,80,128]{2,1,0:T(8,128)(2,1)S(1)}, u32[]{:S(2)}, u32[]{:S(2)}) %collective-permute-start.5) | collective-permute-done | bytes 327712 | tf_op jit(solution)/shard_map/ppermute | solution.py:124
  79.4 8.0 %collective-permute-done.6 = bf16[16,80,128]{2,1,0:T(8,128)(2,1)S(1)} collective-permute-done((bf16[16,80,128]{2,1,0:T(8,128)(2,1)S(1)}, bf16[16,80,128]{2,1,0:T(8,128)(2,1)S(1)}, u32[]{:S(2)}, u32[]{:S(2)}) %collective-permute-start.6) | collective-permute-done | bytes 327712 | tf_op jit(solution)/shard_map/ppermute | solution.py:124
  89.1 2.0 collective-permute-start.11
  91.5 11.5 %collective-permute-done.7 = bf16[32,80,128]{2,1,0:T(8,128)(2,1)S(1)} collective-permute-done((bf16[32,80,128]{2,1,0:T(8,128)(2,1)S(1)}, bf16[32,80,128]{2,1,0:T(8,128)(2,1)S(1)}, u32[]{:S(2)}, u32[]{:S(2)}) %collective-permute-start.7) | collective-permute-done | bytes 655392 | tf_op jit(solution)/shard_map/ppermute | solution.py:124
  103.1 2.4 collective-permute-done.11
  109.7 7.1 %collective-permute-done.12 = bf16[32,48,128]{2,1,0:T(8,128)(2,1)} collective-permute-done((bf16[32,48,128]{2,1,0:T(8,128)(2,1)}, bf16[32,48,128]{2,1,0:T(8,128)(2,1)}, u32[]{:S(2)}, u32[]{:S(2)}) %collective-permute-start.12) | collective-permute-done | bytes 393248 | tf_op jit(solution)/shard_map/ppermute | solution.py:124
  121.3 1.6 collective-permute-start.15
  123.9 3.6 %collective-permute-done.15 = bf16[16,48,128]{2,1,0:T(8,128)(2,1)S(1)} collective-permute-done((bf16[16,48,128]{2,1,0:T(8,128)(2,1)S(1)}, bf16[16,48,128]{2,1,0:T(8,128)(2,1)S(1)}, u32[]{:S(2)}, u32[]{:S(2)}) %collective-permute-start.15) | collective-permute-done | bytes 196640 | tf_op jit(solution)/shard_map/ppermute | solution.py:124
  129.4 5.3 %pad_maximum_fusion.source_ref = bf16[256,80,128]{2,1,0:T(8,128)(2,1)} fusion(bf16[64,80,128]{2,1,0:T(8,128)(2,1)S(1)} %get-tuple-element.44, bf16[64,80,128]{2,1,0:T(8,128)(2,1)S(1)} %get-tuple-element.43, bf16[64,80,128]{2,1,0:T(8,128)(2,1)S(1)} %get-tuple-element.42, bf16[64,80,128]{2,1,0:T(8,128)(2,1)S(1)} %get-tuple-element.41), kind=kLoop, calls=%fused_computation | loop fusion | flops 7864320 | bytes 10485760 | tf_op jit(solution)/shard_map/concatenate | solution.py:165
  134.7 22.2 %shard_map.111 = bf16[80,101,256]{2,1,0:T(8,128)(2,1)} custom-call(bf16[1,128]{1,0:T(2,128)(2,1)} %constant.94.clone.sign_ref, bf16[112,500]{1,0:T(8,128)(2,1)} %constant.95.clone.table_ref, bf16[256,80,128]{2,1,0:T(8,128)(2,1)} %pad_maximum_fusion.source_ref, bf16[250,128,256]{2,1,0:T(8,128)(2,1)} %bitcast.46), custom_call_target="tpu_custom_call" | custom-call | flops 4689920000 | bytes 25640960 | tf_op jit(solution)/shard_map/pallas_call | solution.py:98
  159.9 2.7 collective-permute-done.21
  162.7 1.6 collective-permute-start.22
  164.3 1.7 dynamic-slice_bitcast_fusion
  166.0 1.9 collective-permute-start.26
  173.9 4.4 %collective-permute-done.19 = bf16[32,48,128]{2,1,0:T(8,128)(2,1)} collective-permute-done((bf16[32,48,128]{2,1,0:T(8,128)(2,1)}, bf16[32,48,128]{2,1,0:T(8,128)(2,1)}, u32[]{:S(2)}, u32[]{:S(2)}) %collective-permute-start.19) | collective-permute-done | bytes 393248 | tf_op jit(solution)/shard_map/ppermute | solution.py:124
  179.5 12.7 %collective-permute-done.24 = bf16[20,101,256]{2,1,0:T(8,128)(2,1)} collective-permute-done((bf16[20,101,256]{2,1,0:T(8,128)(2,1)S(1)}, bf16[20,101,256]{2,1,0:T(8,128)(2,1)}, u32[]{:S(2)}, u32[]{:S(2)}) %collective-permute-start.24) | collective-permute-done | bytes 1034272 | tf_op jit(solution)/shard_map/ppermute | solution.py:179
  192.2 2.2 fusion.1
  194.4 1.9 collective-permute-start.25
  197.9 1.9 pad_maximum_fusion.1.source_ref
  199.8 18.1 %collective-permute-done.25 = bf16[20,101,256]{2,1,0:T(8,128)(2,1)} collective-permute-done((bf16[20,101,256]{2,1,0:T(8,128)(2,1)S(1)}, bf16[20,101,256]{2,1,0:T(8,128)(2,1)}, u32[]{:S(2)}, u32[]{:S(2)}) %collective-permute-start.25) | collective-permute-done | bytes 1034272 | tf_op jit(solution)/shard_map/ppermute | solution.py:179
  217.9 1.9 collective-permute-done.27
  219.8 17.3 %shard_map.112 = bf16[48,101,256]{2,1,0:T(8,128)(2,1)} custom-call(bf16[1,128]{1,0:T(2,128)(2,1)} %constant.94.clone.sign_ref, bf16[112,500]{1,0:T(8,128)(2,1)} %constant.95.clone.table_ref, bf16[256,48,128]{2,1,0:T(8,128)(2,1)} %pad_maximum_fusion.1.source_ref, bf16[250,128,256]{2,1,0:T(8,128)(2,1)} %bitcast.47), custom_call_target="tpu_custom_call" | custom-call | flops 2813952000 | bytes 21938176 | tf_op jit(solution)/shard_map/pallas_call | solution.py:98
  237.1 2.3 dynamic-slice_bitcast_fusion.3
  241.5 11.3 %collective-permute-done.30 = bf16[12,101,256]{2,1,0:T(8,128)(2,1)S(1)} collective-permute-done((bf16[12,101,256]{2,1,0:T(8,128)(2,1)S(1)}, bf16[12,101,256]{2,1,0:T(8,128)(2,1)S(1)}, u32[]{:S(2)}, u32[]{:S(2)}) %collective-permute-start.30) | collective-permute-done | bytes 620576 | tf_op jit(solution)/shard_map/ppermute | solution.py:179
  253.8 1.9 collective-permute-start.31
  256.6 10.0 %collective-permute-done.31 = bf16[12,101,256]{2,1,0:T(8,128)(2,1)} collective-permute-done((bf16[12,101,256]{2,1,0:T(8,128)(2,1)}, bf16[12,101,256]{2,1,0:T(8,128)(2,1)}, u32[]{:S(2)}, u32[]{:S(2)}) %collective-permute-start.31) | collective-permute-done | bytes 620576 | tf_op jit(solution)/shard_map/ppermute | solution.py:179
  266.6 1.6 fusion.9
  269.4 4.1 %fusion.3 = (bf16[20,101,256]{2,1,0:T(8,128)(2,1)}, bf16[20,101,256]{2,1,0:T(8,128)(2,1)}) fusion(bf16[20,101,256]{2,1,0:T(8,128)(2,1)} %collective-permute-done.25, bf16[4,20,101,256]{3,2,1,0:T(8,128)(2,1)} %bitcast.49, s32[]{:T(128)S(6)} %min.30, bf16[20,101,256]{2,1,0:T(8,128)(2,1)} %collective-permute-done.27, s32[]{:T(128)S(6)} %min.35), kind=kLoop, calls=%fused_computation.11 | loop fusion | flops 4136960 | bytes 6205448 | tf_op jit(solution)/shard_map/convert_element_type | solution.py:120
  273.6 1.9 collective-permute-start.29
  275.5 4.6 %collective-permute-start.28 = (bf16[20,101,256]{2,1,0:T(8,128)(2,1)}, bf16[20,101,256]{2,1,0:T(8,128)(2,1)}, u32[]{:S(2)}, u32[]{:S(2)}) collective-permute-start(bf16[20,101,256]{2,1,0:T(8,128)(2,1)} %get-tuple-element.33), channel_id=1, source_target_pairs={{0,1},{1,2},{2,3},{4,5},{5,6},{6,7},{8,9},{9,10},{10,11},{12,13},{... | collective-permute-start | bytes 3102728 | tf_op jit(solution)/shard_map/ppermute | solution.py:179
  280.1 4.9 %collective-permute-start.32 = (bf16[12,101,256]{2,1,0:T(8,128)(2,1)S(1)}, bf16[12,101,256]{2,1,0:T(8,128)(2,1)}, u32[]{:S(2)}, u32[]{:S(2)}) collective-permute-start(bf16[12,101,256]{2,1,0:T(8,128)(2,1)S(1)} %get-tuple-element.45), channel_id=1, source_target_pairs={{0,1},{1,2},{2,3},{4,5},{5,6},{6,7},{8,9},{9,10},{10,11},{12,13},{... | collective-permute-start | bytes 1861640 | tf_op jit(solution)/shard_map/ppermute | solution.py:179
  285.0 2.4 collective-permute-done.34
  288.4 1.9 collective-permute-start.35
  290.3 19.1 %collective-permute-done.29 = bf16[20,101,256]{2,1,0:T(8,128)(2,1)} collective-permute-done((bf16[20,101,256]{2,1,0:T(8,128)(2,1)}, bf16[20,101,256]{2,1,0:T(8,128)(2,1)}, u32[]{:S(2)}, u32[]{:S(2)}) %collective-permute-start.29) | collective-permute-done | bytes 1034272 | tf_op jit(solution)/shard_map/ppermute | solution.py:180
  309.5 2.3 fusion.5
  311.7 4.6 %collective-permute-done.35 = bf16[12,101,256]{2,1,0:T(8,128)(2,1)} collective-permute-done((bf16[12,101,256]{2,1,0:T(8,128)(2,1)}, bf16[12,101,256]{2,1,0:T(8,128)(2,1)}, u32[]{:S(2)}, u32[]{:S(2)}) %collective-permute-start.35) | collective-permute-done | bytes 620576 | tf_op jit(solution)/shard_map/ppermute | solution.py:180
  318.0 1.6 copy.28
  (107 shorter events, 42.4 us)
Async XLA Ops:
  41.5 3.4 %collective-permute-start = (bf16[64,80,128]{2,1,0:T(8,128)(2,1)}, bf16[64,80,128]{2,1,0:T(8,128)(2,1)}, u32[]{:S(2)}, u32[]{:S(2)}) collective-permute-start(bf16[64,80,128]{2,1,0:T(8,128)(2,1)} %constant_dynamic-slice_fusion.11), channel_id=1, source_target_pairs={{0,4},{4,0},{8,12},{12,8},{16,20},{20,16},{24,28},{28,24},{1,5},{5... | collective-permute-start | bytes 3932168 | tf_op jit(solution)/shard_map/ppermute | solution.py:124
  41.5 1.7 copy-start.4
  41.5 1.7 copy-start.5
  42.7 4.2 %collective-permute-start.1 = (bf16[64,80,128]{2,1,0:T(8,128)(2,1)}, bf16[64,80,128]{2,1,0:T(8,128)(2,1)}, u32[]{:S(2)}, u32[]{:S(2)}) collective-permute-start(bf16[64,80,128]{2,1,0:T(8,128)(2,1)} %constant_dynamic-slice_fusion.10), channel_id=1, source_target_pairs={{0,4},{4,0},{8,12},{12,8},{16,20},{20,16},{24,28},{28,24},{1,5},{5... | collective-permute-start | bytes 3932168 | tf_op jit(solution)/shard_map/ppermute | solution.py:124
  48.7 18.8 %collective-permute-start.4 = (bf16[32,80,128]{2,1,0:T(8,128)(2,1)S(1)}, bf16[32,80,128]{2,1,0:T(8,128)(2,1)S(1)}, u32[]{:S(2)}, u32[]{:S(2)}) collective-permute-start(bf16[32,80,128]{2,1,0:T(8,128)(2,1)S(1)} %constant_dynamic-slice_fusion.7), channel_id=1, source_target_pairs={{0,8},{4,12},{8,0},{12,4},{16,24},{20,28},{24,16},{28,20},{1,9},{5... | collective-permute-start | bytes 1966088 | tf_op jit(solution)/shard_map/ppermute | solution.py:124
  50.3 18.0 %collective-permute-start.8 = (bf16[32,80,128]{2,1,0:T(8,128)(2,1)S(1)}, bf16[32,80,128]{2,1,0:T(8,128)(2,1)S(1)}, u32[]{:S(2)}, u32[]{:S(2)}) collective-permute-start(bf16[32,80,128]{2,1,0:T(8,128)(2,1)S(1)} %constant_dynamic-slice_fusion.5), channel_id=1, source_target_pairs={{0,16},{4,20},{8,24},{12,28},{16,0},{20,4},{24,8},{28,12},{1,17},{... | collective-permute-start | bytes 1966088 | tf_op jit(solution)/shard_map/ppermute | solution.py:124
  67.4 23.7 %collective-permute-start.2 = (bf16[64,48,128]{2,1,0:T(8,128)(2,1)S(1)}, bf16[64,48,128]{2,1,0:T(8,128)(2,1)S(1)}, u32[]{:S(2)}, u32[]{:S(2)}) collective-permute-start(bf16[64,48,128]{2,1,0:T(8,128)(2,1)S(1)} %constant_dynamic-slice_fusion.9), channel_id=1, source_target_pairs={{0,4},{4,0},{8,12},{12,8},{16,20},{20,16},{24,28},{28,24},{1,5},{5... | collective-permute-start | bytes 2359304 | tf_op jit(solution)/shard_map/ppermute | solution.py:124
  67.7 10.2 %collective-permute-start.5 = (bf16[16,80,128]{2,1,0:T(8,128)(2,1)S(1)}, bf16[16,80,128]{2,1,0:T(8,128)(2,1)S(1)}, u32[]{:S(2)}, u32[]{:S(2)}) collective-permute-start(bf16[16,80,128]{2,1,0:T(8,128)(2,1)S(1)} %constant_dynamic-slice_fusion.6), channel_id=1, source_target_pairs={{0,16},{4,20},{8,24},{12,28},{16,0},{20,4},{24,8},{28,12},{1,17},{... | collective-permute-start | bytes 983048 | tf_op jit(solution)/shard_map/ppermute | solution.py:124
  68.5 10.2 %collective-permute-start.9 = (bf16[16,80,128]{2,1,0:T(8,128)(2,1)S(1)}, bf16[16,80,128]{2,1,0:T(8,128)(2,1)S(1)}, u32[]{:S(2)}, u32[]{:S(2)}) collective-permute-start(bf16[16,80,128]{2,1,0:T(8,128)(2,1)S(1)} %constant_dynamic-slice_fusion.4), channel_id=1, source_target_pairs={{0,8},{4,12},{8,0},{12,4},{16,24},{20,28},{24,16},{28,20},{1,9},{5... | collective-permute-start | bytes 983048 | tf_op jit(solution)/shard_map/ppermute | solution.py:124
  78.0 9.4 %collective-permute-start.6 = (bf16[16,80,128]{2,1,0:T(8,128)(2,1)S(1)}, bf16[16,80,128]{2,1,0:T(8,128)(2,1)S(1)}, u32[]{:S(2)}, u32[]{:S(2)}) collective-permute-start(bf16[16,80,128]{2,1,0:T(8,128)(2,1)S(1)} %add_convert_fusion.9), channel_id=1, source_target_pairs={{0,16},{4,20},{8,24},{12,28},{16,0},{20,4},{24,8},{28,12},{1,17},{... | collective-permute-start | bytes 983048 | tf_op jit(solution)/shard_map/ppermute | solution.py:124
  78.6 12.7 %collective-permute-start.3 = (bf16[64,48,128]{2,1,0:T(8,128)(2,1)S(1)}, bf16[64,48,128]{2,1,0:T(8,128)(2,1)S(1)}, u32[]{:S(2)}, u32[]{:S(2)}) collective-permute-start(bf16[64,48,128]{2,1,0:T(8,128)(2,1)S(1)} %constant_dynamic-slice_fusion.8), channel_id=1, source_target_pairs={{0,4},{4,0},{8,12},{12,8},{16,20},{20,16},{24,28},{28,24},{1,5},{5... | collective-permute-start | bytes 2359304 | tf_op jit(solution)/shard_map/ppermute | solution.py:124
  78.8 10.2 %collective-permute-start.10 = (bf16[16,80,128]{2,1,0:T(8,128)(2,1)S(1)}, bf16[16,80,128]{2,1,0:T(8,128)(2,1)S(1)}, u32[]{:S(2)}, u32[]{:S(2)}) collective-permute-start(bf16[16,80,128]{2,1,0:T(8,128)(2,1)S(1)} %add_convert_fusion.8), channel_id=1, source_target_pairs={{0,8},{4,12},{8,0},{12,4},{16,24},{20,28},{24,16},{28,20},{1,9},{5... | collective-permute-start | bytes 983048 | tf_op jit(solution)/shard_map/ppermute | solution.py:124
  87.5 15.5 %collective-permute-start.7 = (bf16[32,80,128]{2,1,0:T(8,128)(2,1)S(1)}, bf16[32,80,128]{2,1,0:T(8,128)(2,1)S(1)}, u32[]{:S(2)}, u32[]{:S(2)}) collective-permute-start(bf16[32,80,128]{2,1,0:T(8,128)(2,1)S(1)} %pad_maximum_fusion.7), channel_id=1, source_target_pairs={{0,8},{4,12},{8,0},{12,4},{16,24},{20,28},{24,16},{28,20},{1,9},{5... | collective-permute-start | bytes 1966088 | tf_op jit(solution)/shard_map/ppermute | solution.py:124
  89.1 16.4 %collective-permute-start.11 = (bf16[32,80,128]{2,1,0:T(8,128)(2,1)S(1)}, bf16[32,80,128]{2,1,0:T(8,128)(2,1)S(1)}, u32[]{:S(2)}, u32[]{:S(2)}) collective-permute-start(bf16[32,80,128]{2,1,0:T(8,128)(2,1)S(1)} %pad_maximum_fusion.8), channel_id=1, source_target_pairs={{0,16},{4,20},{8,24},{12,28},{16,0},{20,4},{24,8},{28,12},{1,17},{... | collective-permute-start | bytes 1966088 | tf_op jit(solution)/shard_map/ppermute | solution.py:124
  91.3 14.5 %copy-start.2 = (bf16[64,48,128]{2,1,0:T(8,128)(2,1)}, bf16[64,48,128]{2,1,0:T(8,128)(2,1)S(1)}, u32[]{:S(2)}) copy-start(bf16[64,48,128]{2,1,0:T(8,128)(2,1)S(1)} %add_convert_fusion.3) | copy-start | bytes 2359300
  106.6 10.1 %collective-permute-start.12 = (bf16[32,48,128]{2,1,0:T(8,128)(2,1)}, bf16[32,48,128]{2,1,0:T(8,128)(2,1)}, u32[]{:S(2)}, u32[]{:S(2)}) collective-permute-start(bf16[32,48,128]{2,1,0:T(8,128)(2,1)} %constant_dynamic-slice_fusion.3), channel_id=1, source_target_pairs={{0,8},{4,12},{8,0},{12,4},{16,24},{20,28},{24,16},{28,20},{1,9},{5... | collective-permute-start | bytes 1179656 | tf_op jit(solution)/shard_map/ppermute | solution.py:124
  107.1 20.4 %collective-permute-start.17 = (bf16[64,80,128]{2,1,0:T(8,128)(2,1)S(1)}, bf16[64,80,128]{2,1,0:T(8,128)(2,1)}, u32[]{:S(2)}, u32[]{:S(2)}) collective-permute-start(bf16[64,80,128]{2,1,0:T(8,128)(2,1)S(1)} %get-tuple-element.24), channel_id=1, source_target_pairs={{0,4},{4,0},{8,12},{12,8},{16,20},{20,16},{24,28},{28,24},{1,5},{5... | collective-permute-start | bytes 3932168 | tf_op jit(solution)/shard_map/ppermute | solution.py:124
  107.9 12.2 %collective-permute-start.14 = (bf16[32,48,128]{2,1,0:T(8,128)(2,1)}, bf16[32,48,128]{2,1,0:T(8,128)(2,1)}, u32[]{:S(2)}, u32[]{:S(2)}) collective-permute-start(bf16[32,48,128]{2,1,0:T(8,128)(2,1)} %constant_dynamic-slice_fusion.1), channel_id=1, source_target_pairs={{0,16},{4,20},{8,24},{12,28},{16,0},{20,4},{24,8},{28,12},{1,17},{... | collective-permute-start | bytes 1179656 | tf_op jit(solution)/shard_map/ppermute | solution.py:124
  109.4 19.6 %collective-permute-start.16 = (bf16[64,80,128]{2,1,0:T(8,128)(2,1)S(1)}, bf16[64,80,128]{2,1,0:T(8,128)(2,1)S(1)}, u32[]{:S(2)}, u32[]{:S(2)}) collective-permute-start(bf16[64,80,128]{2,1,0:T(8,128)(2,1)S(1)} %get-tuple-element.23), channel_id=1, source_target_pairs={{0,4},{4,0},{8,12},{12,8},{16,20},{20,16},{24,28},{28,24},{1,5},{5... | collective-permute-start | bytes 3932168 | tf_op jit(solution)/shard_map/ppermute | solution.py:124
  118.0 5.9 %collective-permute-start.13 = (bf16[16,48,128]{2,1,0:T(8,128)(2,1)S(1)}, bf16[16,48,128]{2,1,0:T(8,128)(2,1)S(1)}, u32[]{:S(2)}, u32[]{:S(2)}) collective-permute-start(bf16[16,48,128]{2,1,0:T(8,128)(2,1)S(1)} %constant_dynamic-slice_fusion.2), channel_id=1, source_target_pairs={{0,16},{4,20},{8,24},{12,28},{16,0},{20,4},{24,8},{28,12},{1,17},{... | collective-permute-start | bytes 589832 | tf_op jit(solution)/shard_map/ppermute | solution.py:124
  121.3 6.2 %collective-permute-start.15 = (bf16[16,48,128]{2,1,0:T(8,128)(2,1)S(1)}, bf16[16,48,128]{2,1,0:T(8,128)(2,1)S(1)}, u32[]{:S(2)}, u32[]{:S(2)}) collective-permute-start(bf16[16,48,128]{2,1,0:T(8,128)(2,1)S(1)} %constant_dynamic-slice_fusion), channel_id=1, source_target_pairs={{0,8},{4,12},{8,0},{12,4},{16,24},{20,28},{24,16},{28,20},{1,9},{5... | collective-permute-start | bytes 589832 | tf_op jit(solution)/shard_map/ppermute | solution.py:124
  156.9 5.7 %collective-permute-start.21 = (bf16[16,48,128]{2,1,0:T(8,128)(2,1)S(1)}, bf16[16,48,128]{2,1,0:T(8,128)(2,1)S(1)}, u32[]{:S(2)}, u32[]{:S(2)}) collective-permute-start(bf16[16,48,128]{2,1,0:T(8,128)(2,1)S(1)} %add_convert_fusion.10), channel_id=1, source_target_pairs={{0,8},{4,12},{8,0},{12,4},{16,24},{20,28},{24,16},{28,20},{1,9},{5... | collective-permute-start | bytes 589832 | tf_op jit(solution)/shard_map/ppermute | solution.py:124
  158.4 10.7 %collective-permute-start.18 = (bf16[16,48,128]{2,1,0:T(8,128)(2,1)S(1)}, bf16[16,48,128]{2,1,0:T(8,128)(2,1)S(1)}, u32[]{:S(2)}, u32[]{:S(2)}) collective-permute-start(bf16[16,48,128]{2,1,0:T(8,128)(2,1)S(1)} %add_convert_fusion.11), channel_id=1, source_target_pairs={{0,16},{4,20},{8,24},{12,28},{16,0},{20,4},{24,8},{28,12},{1,17},{... | collective-permute-start | bytes 589832 | tf_op jit(solution)/shard_map/ppermute | solution.py:124
  162.7 9.9 %collective-permute-start.22 = (bf16[32,48,128]{2,1,0:T(8,128)(2,1)S(1)}, bf16[32,48,128]{2,1,0:T(8,128)(2,1)}, u32[]{:S(2)}, u32[]{:S(2)}) collective-permute-start(bf16[32,48,128]{2,1,0:T(8,128)(2,1)S(1)} %pad_maximum_fusion.10), channel_id=1, source_target_pairs={{0,16},{4,20},{8,24},{12,28},{16,0},{20,4},{24,8},{28,12},{1,17},{... | collective-permute-start | bytes 1179656 | tf_op jit(solution)/shard_map/ppermute | solution.py:124
  166.0 13.5 %collective-permute-start.26 = (bf16[20,101,256]{2,1,0:T(8,128)(2,1)S(1)}, bf16[20,101,256]{2,1,0:T(8,128)(2,1)}, u32[]{:S(2)}, u32[]{:S(2)}) collective-permute-start(bf16[20,101,256]{2,1,0:T(8,128)(2,1)S(1)} %get-tuple-element.37), channel_id=1, source_target_pairs={{3,2},{7,6},{11,10},{15,14},{19,18},{23,22},{27,26},{31,30}} | collective-permute-start | bytes 3102728 | tf_op jit(solution)/shard_map/ppermute | solution.py:180
  167.8 24.4 %collective-permute-start.24 = (bf16[20,101,256]{2,1,0:T(8,128)(2,1)S(1)}, bf16[20,101,256]{2,1,0:T(8,128)(2,1)}, u32[]{:S(2)}, u32[]{:S(2)}) collective-permute-start(bf16[20,101,256]{2,1,0:T(8,128)(2,1)S(1)} %get-tuple-element.38), channel_id=1, source_target_pairs={{0,1},{4,5},{8,9},{12,13},{16,17},{20,21},{24,25},{28,29}} | collective-permute-start | bytes 3102728 | tf_op jit(solution)/shard_map/ppermute | solution.py:179
  170.0 8.3 %collective-permute-start.19 = (bf16[32,48,128]{2,1,0:T(8,128)(2,1)}, bf16[32,48,128]{2,1,0:T(8,128)(2,1)}, u32[]{:S(2)}, u32[]{:S(2)}) collective-permute-start(bf16[32,48,128]{2,1,0:T(8,128)(2,1)} %pad_maximum_fusion.9), channel_id=1, source_target_pairs={{0,8},{4,12},{8,0},{12,4},{16,24},{20,28},{24,16},{28,20},{1,9},{5... | collective-permute-start | bytes 1179656 | tf_op jit(solution)/shard_map/ppermute | solution.py:124
  173.7 18.5 %copy-start = (bf16[80,101,256]{2,1,0:T(8,128)(2,1)S(1)}, bf16[80,101,256]{2,1,0:T(8,128)(2,1)}, u32[]{:S(2)}) copy-start(bf16[80,101,256]{2,1,0:T(8,128)(2,1)} %shard_map.111) | copy-start | bytes 12410884
  173.8 23.9 %collective-permute-start.23 = (bf16[64,48,128]{2,1,0:T(8,128)(2,1)S(1)}, bf16[64,48,128]{2,1,0:T(8,128)(2,1)S(1)}, u32[]{:S(2)}, u32[]{:S(2)}) collective-permute-start(bf16[64,48,128]{2,1,0:T(8,128)(2,1)S(1)} %pad_maximum_fusion.6), channel_id=1, source_target_pairs={{0,4},{4,0},{8,12},{12,8},{16,20},{20,16},{24,28},{28,24},{1,5},{5... | collective-permute-start | bytes 2359304 | tf_op jit(solution)/shard_map/ppermute | solution.py:124
  179.4 18.4 %collective-permute-start.20 = (bf16[64,48,128]{2,1,0:T(8,128)(2,1)S(1)}, bf16[64,48,128]{2,1,0:T(8,128)(2,1)S(1)}, u32[]{:S(2)}, u32[]{:S(2)}) collective-permute-start(bf16[64,48,128]{2,1,0:T(8,128)(2,1)S(1)} %pad_maximum_fusion.5), channel_id=1, source_target_pairs={{0,4},{4,0},{8,12},{12,8},{16,20},{20,16},{24,28},{28,24},{1,5},{5... | collective-permute-start | bytes 2359304 | tf_op jit(solution)/shard_map/ppermute | solution.py:124
  194.4 23.5 %collective-permute-start.25 = (bf16[20,101,256]{2,1,0:T(8,128)(2,1)S(1)}, bf16[20,101,256]{2,1,0:T(8,128)(2,1)}, u32[]{:S(2)}, u32[]{:S(2)}) collective-permute-start(bf16[20,101,256]{2,1,0:T(8,128)(2,1)S(1)} %get-tuple-element.36), channel_id=1, source_target_pairs={{0,1},{1,2},{4,5},{5,6},{8,9},{9,10},{12,13},{13,14},{16,17},{17,1... | collective-permute-start | bytes 3102728 | tf_op jit(solution)/shard_map/ppermute | solution.py:179
  196.3 23.5 %collective-permute-start.27 = (bf16[20,101,256]{2,1,0:T(8,128)(2,1)S(1)}, bf16[20,101,256]{2,1,0:T(8,128)(2,1)}, u32[]{:S(2)}, u32[]{:S(2)}) collective-permute-start(bf16[20,101,256]{2,1,0:T(8,128)(2,1)S(1)} %get-tuple-element.35), channel_id=1, source_target_pairs={{3,2},{2,1},{7,6},{6,5},{11,10},{10,9},{15,14},{14,13},{19,18},{18... | collective-permute-start | bytes 3102728 | tf_op jit(solution)/shard_map/ppermute | solution.py:180
  237.1 15.7 %copy-start.1 = (bf16[48,101,256]{2,1,0:T(8,128)(2,1)S(1)}, bf16[48,101,256]{2,1,0:T(8,128)(2,1)}, u32[]{:S(2)}) copy-start(bf16[48,101,256]{2,1,0:T(8,128)(2,1)} %shard_map.112) | copy-start | bytes 7446532
  239.5 13.3 %collective-permute-start.30 = (bf16[12,101,256]{2,1,0:T(8,128)(2,1)S(1)}, bf16[12,101,256]{2,1,0:T(8,128)(2,1)S(1)}, u32[]{:S(2)}, u32[]{:S(2)}) collective-permute-start(bf16[12,101,256]{2,1,0:T(8,128)(2,1)S(1)} %get-tuple-element.47), channel_id=1, source_target_pairs={{0,1},{4,5},{8,9},{12,13},{16,17},{20,21},{24,25},{28,29}} | collective-permute-start | bytes 1861640 | tf_op jit(solution)/shard_map/ppermute | solution.py:179
  240.7 15.0 %collective-permute-start.33 = (bf16[12,101,256]{2,1,0:T(8,128)(2,1)}, bf16[12,101,256]{2,1,0:T(8,128)(2,1)S(1)}, u32[]{:S(2)}, u32[]{:S(2)}) collective-permute-start(bf16[12,101,256]{2,1,0:T(8,128)(2,1)} %get-tuple-element.48), channel_id=1, source_target_pairs={{3,2},{7,6},{11,10},{15,14},{19,18},{23,22},{27,26},{31,30}} | collective-permute-start | bytes 1861640 | tf_op jit(solution)/shard_map/ppermute | solution.py:180
  253.8 12.8 %collective-permute-start.31 = (bf16[12,101,256]{2,1,0:T(8,128)(2,1)}, bf16[12,101,256]{2,1,0:T(8,128)(2,1)}, u32[]{:S(2)}, u32[]{:S(2)}) collective-permute-start(bf16[12,101,256]{2,1,0:T(8,128)(2,1)} %fusion.8), channel_id=1, source_target_pairs={{0,1},{1,2},{4,5},{5,6},{8,9},{9,10},{12,13},{13,14},{16,17},{17,1... | collective-permute-start | bytes 1861640 | tf_op jit(solution)/shard_map/ppermute | solution.py:179
  255.7 0.8 copy-start.3
  268.1 19.2 %collective-permute-start.34 = (bf16[12,101,256]{2,1,0:T(8,128)(2,1)S(1)}, bf16[12,101,256]{2,1,0:T(8,128)(2,1)S(1)}, u32[]{:S(2)}, u32[]{:S(2)}) collective-permute-start(bf16[12,101,256]{2,1,0:T(8,128)(2,1)S(1)} %get-tuple-element.46), channel_id=1, source_target_pairs={{3,2},{2,1},{7,6},{6,5},{11,10},{10,9},{15,14},{14,13},{19,18},{18... | collective-permute-start | bytes 1861640 | tf_op jit(solution)/shard_map/ppermute | solution.py:180
  273.6 35.9 %collective-permute-start.29 = (bf16[20,101,256]{2,1,0:T(8,128)(2,1)}, bf16[20,101,256]{2,1,0:T(8,128)(2,1)}, u32[]{:S(2)}, u32[]{:S(2)}) collective-permute-start(bf16[20,101,256]{2,1,0:T(8,128)(2,1)} %get-tuple-element.34), channel_id=1, source_target_pairs={{3,2},{2,1},{1,0},{7,6},{6,5},{5,4},{11,10},{10,9},{9,8},{15,14},{... | collective-permute-start | bytes 3102728 | tf_op jit(solution)/shard_map/ppermute | solution.py:180
  275.5 34.0 %collective-permute-start.28 = (bf16[20,101,256]{2,1,0:T(8,128)(2,1)}, bf16[20,101,256]{2,1,0:T(8,128)(2,1)}, u32[]{:S(2)}, u32[]{:S(2)}) collective-permute-start(bf16[20,101,256]{2,1,0:T(8,128)(2,1)} %get-tuple-element.33), channel_id=1, source_target_pairs={{0,1},{1,2},{2,3},{4,5},{5,6},{6,7},{8,9},{9,10},{10,11},{12,13},{... | collective-permute-start | bytes 3102728 | tf_op jit(solution)/shard_map/ppermute | solution.py:179
  280.1 31.7 %collective-permute-start.32 = (bf16[12,101,256]{2,1,0:T(8,128)(2,1)S(1)}, bf16[12,101,256]{2,1,0:T(8,128)(2,1)}, u32[]{:S(2)}, u32[]{:S(2)}) collective-permute-start(bf16[12,101,256]{2,1,0:T(8,128)(2,1)S(1)} %get-tuple-element.45), channel_id=1, source_target_pairs={{0,1},{1,2},{2,3},{4,5},{5,6},{6,7},{8,9},{9,10},{10,11},{12,13},{... | collective-permute-start | bytes 1861640 | tf_op jit(solution)/shard_map/ppermute | solution.py:179
  288.4 27.9 %collective-permute-start.35 = (bf16[12,101,256]{2,1,0:T(8,128)(2,1)}, bf16[12,101,256]{2,1,0:T(8,128)(2,1)}, u32[]{:S(2)}, u32[]{:S(2)}) collective-permute-start(bf16[12,101,256]{2,1,0:T(8,128)(2,1)} %fusion.7), channel_id=1, source_target_pairs={{3,2},{2,1},{1,0},{7,6},{6,5},{5,4},{11,10},{10,9},{9,8},{15,14},{... | collective-permute-start | bytes 1861640 | tf_op jit(solution)/shard_map/ppermute | solution.py:180

commit v6 on v5

--- a/solution.py
+++ b/solution.py
@@ -11,7 +11,7 @@
 
 LAGS = 101
 SRC_BLK = 64
-ROWS = (20, 12)
+ROWS = (16, 16)
 AHEAD = (2,)
 PAD = 256
 MIB = 1024 * 1024
@@ -226,7 +226,6 @@
         if at + 1 < len(ROWS):
             parts, keep = lax.optimization_barrier((parts, keep))
             coming = begin(pick_sources(pick_of(first, ROWS[at + 1]), keep, x, 25))
-        parts = halve_rest(parts)
         if at:
             source = finish(done)
             if chain is not None:
@@ -237,7 +236,7 @@
                 outs.append(chain_end(chain, state, "tm"))
             chain = correlograms(source, ROWS[at - 1])
             parts, chain = lax.optimization_barrier((parts, chain))
-        done = double_rest(parts)
+        done = double_rest(halve_rest(parts))
     source = finish(done)
     ahead = min(AHEAD[-1], steps)
     state = chain_steps(chain, None, "tm", 0, ahead)

time: 321 us -> 304 us (0.947)
  other arithmetic: 38 us -> 29 us
  starting transfers between devices: 44.8 us -> 40.7 us
  waiting for transfers between devices: 133 us -> 129 us
    ppermute x6, waiting for transfers between devices: 52.2 us -> 43.4 us  [chain_steps(): lax.ppermute(to_right, axis, [(i, i + 1) for i in range(t + 1)])]
    convert_element_type x17 -> x18, other arithmetic: 17.1 us -> 10.7 us  [add(): return (a.astype(jnp.float32) + b.astype(jnp.float32)).astype(jnp.bfloat16)]
    dynamic_slice x0 -> x6, local copies, waits for them, and re-layouts: none -> 5.92 us  [take(): lax.dynamic_index_in_dim(parts, jnp.clip(at, 0, parts.shape[0] - 1), 0, k...]
    squeeze x2 -> x0, local copies, waits for them, and re-layouts: 4.03 us -> none  [take(): lax.dynamic_index_in_dim(parts, jnp.clip(at, 0, parts.shape[0] - 1), 0, k...]
    ppermute x6, starting transfers between devices: 15.8 us -> 12.6 us  [chain_steps(): lax.ppermute(to_right, axis, [(i, i + 1) for i in range(t + 1)])]
  transfers between devices with their start and end apart: 36 -> 36, of which waited for: 21 -> 24; matrix products, arithmetic and copies ran while one was open for 10% -> 9% of each run, Pallas kernels for 4% -> 4%
where the time goes in v6:
time: 304 us; the launch traced here: 302 us
  waiting for transfers between devices  129 us (42%)
  Pallas kernels  66.2 us (22%)
  starting transfers between devices  40.7 us (13%)
  local copies, waits for them, and re-layouts  35.9 us (12%)
  other arithmetic  29 us (10%)
    ppermute x24, waiting for transfers between devices, swap(): lax.ppermute(x, axis, [(i, i ^ 1 << bit) for i in range(lax.axis_size(axi...  55.5 us
    ppermute x6, waiting for transfers between devices, chain_steps(): lax.ppermute(to_right, axis, [(i, i + 1) for i in range(t + 1)])  43.4 us
    pallas_call x2, Pallas kernels, correlate(): pl.pallas_call(functools.partial(correlate_kernel, stride, bin_count), gr...  39.6 us
    ppermute x6, waiting for transfers between devices, chain_steps(): lax.ppermute(to_left, axis, [(n - 1 - i, n - 2 - i) for i in range(t + 1)])  30.5 us
    pallas_call x2, Pallas kernels, pick_sources(): pl.pallas_call(pick_kernel, grid=(bin_count // bins,), in_specs=[pl.Block...  26.5 us
    ppermute x24, starting transfers between devices, swap(): lax.ppermute(x, axis, [(i, i ^ 1 << bit) for i in range(lax.axis_size(axi...  17.9 us
    transpose x1, local copies, waits for them, and re-layouts, body(): x = spectra.transpose(2, 1, 0, 3).reshape(bin_count, depth, width)  16.6 us
    ppermute x6, starting transfers between devices, chain_steps(): lax.ppermute(to_right, axis, [(i, i + 1) for i in range(t + 1)])  12.6 us
  transfers between devices with their start and end apart: 36, of which 24 were waited for; matrix products, arithmetic and copies ran while one was open for 9% of the time, Pallas kernels for 4%

profile of v6, /device:TPU:8, one launch (start us, length us, event | category | flops | bytes accessed | tf_op | source)
XLA Modules:
  0.0 301.8 jit_solution(1776261084959967018)
XLA Ops:
  2.1 16.6 %copy.12 = bf16[250,2,64,256]{3,2,1,0:T(8,128)(2,1)} copy(bf16[250,2,64,256]{3,1,0,2:T(2,128)(2,1)} %bitcast.65) | data formatting | bytes 32768000 | tf_op jit(solution)/shard_map/transpose | solution.py:211
  20.0 13.3 %shard_map.109 = bf16[256,64,128]{2,1,0:T(8,128)(2,1)} custom-call(bf16[64,256]{1,0:T(8,128)(2,1)S(1)} %get-tuple-element.77.pick_ref, f32[1,128]{1,0:T(1,128)S(1)} %broadcast_in_dim_tile.3.keep_ref, bf16[250,128,256]{2,1,0:T(8,128)(2,1)} %bitcast.58), custom_call_target="tpu_custom_call" | custom-call | flops 1048576000 | bytes 20480000 | tf_op jit(solution)/shard_map/pallas_call | solution.py:40
  33.2 4.5 %fusion.15 = (bf16[128,64,128]{2,1,0:T(8,128)(2,1)S(1)}, bf16[128,64,128]{2,1,0:T(8,128)(2,1)}) fusion(bf16[256,64,128]{2,1,0:T(8,128)(2,1)} %shard_map.109), kind=kLoop, calls=%fused_computation.107 | loop fusion | bytes 8388608 | tf_op jit(solution)/shard_map/slice | solution.py:153
  37.7 2.3 constant_dynamic-slice_fusion.20
  40.7 2.4 collective-permute-done
  43.1 1.9 add_convert_fusion.3
  45.0 1.6 add_convert_fusion.2
  46.7 1.6 collective-permute-start.4
  48.3 1.6 collective-permute-start.8
  49.9 13.3 %shard_map.110 = bf16[256,64,128]{2,1,0:T(8,128)(2,1)} custom-call(bf16[64,256]{1,0:T(8,128)(2,1)S(1)} %get-tuple-element.76.pick_ref, f32[1,128]{1,0:T(1,128)S(1)} %broadcast_in_dim_tile.3.keep_ref, bf16[250,128,256]{2,1,0:T(8,128)(2,1)} %bitcast.59), custom_call_target="tpu_custom_call" | custom-call | flops 1048576000 | bytes 20480000 | tf_op jit(solution)/shard_map/pallas_call | solution.py:40
  63.2 3.2 %fusion.14 = (bf16[128,64,128]{2,1,0:T(8,128)(2,1)S(1)}, bf16[128,64,128]{2,1,0:T(8,128)(2,1)S(1)}) fusion(bf16[256,64,128]{2,1,0:T(8,128)(2,1)} %shard_map.110), kind=kLoop, calls=%fused_computation.106 | loop fusion | bytes 8388608 | tf_op jit(solution)/shard_map/slice | solution.py:153
  68.2 7.4 %collective-permute-done.5 = bf16[16,64,128]{2,1,0:T(8,128)(2,1)S(1)} collective-permute-done((bf16[16,64,128]{2,1,0:T(8,128)(2,1)S(1)}, bf16[16,64,128]{2,1,0:T(8,128)(2,1)S(1)}, u32[]{:S(2)}, u32[]{:S(2)}) %collective-permute-start.5) | collective-permute-done | bytes 262176 | tf_op jit(solution)/shard_map/ppermute | solution.py:124
  77.0 6.6 %collective-permute-done.6 = bf16[16,64,128]{2,1,0:T(8,128)(2,1)S(1)} collective-permute-done((bf16[16,64,128]{2,1,0:T(8,128)(2,1)S(1)}, bf16[16,64,128]{2,1,0:T(8,128)(2,1)S(1)}, u32[]{:S(2)}, u32[]{:S(2)}) %collective-permute-start.6) | collective-permute-done | bytes 262176 | tf_op jit(solution)/shard_map/ppermute | solution.py:124
  85.3 2.0 collective-permute-start.11
  89.1 7.3 %collective-permute-done.7 = bf16[32,64,128]{2,1,0:T(8,128)(2,1)S(1)} collective-permute-done((bf16[32,64,128]{2,1,0:T(8,128)(2,1)S(1)}, bf16[32,64,128]{2,1,0:T(8,128)(2,1)S(1)}, u32[]{:S(2)}, u32[]{:S(2)}) %collective-permute-start.7) | collective-permute-done | bytes 524320 | tf_op jit(solution)/shard_map/ppermute | solution.py:124
  96.6 2.3 collective-permute-done.11
  99.7 2.3 collective-permute-done.13
  104.8 2.3 pad_maximum_fusion.source_ref
  107.1 19.8 %shard_map.111 = bf16[64,101,256]{2,1,0:T(8,128)(2,1)} custom-call(bf16[1,128]{1,0:T(2,128)(2,1)} %constant.86.clone.sign_ref, bf16[112,500]{1,0:T(8,128)(2,1)} %constant.87.clone.table_ref, bf16[256,64,128]{2,1,0:T(8,128)(2,1)} %pad_maximum_fusion.source_ref, bf16[250,128,256]{2,1,0:T(8,128)(2,1)} %bitcast.60), custom_call_target="tpu_custom_call" | custom-call | flops 3751936000 | bytes 23789568 | tf_op jit(solution)/shard_map/pallas_call | solution.py:98
  127.0 1.6 collective-permute-start.19
  129.2 11.8 %collective-permute-done.19 = bf16[32,64,128]{2,1,0:T(8,128)(2,1)S(1)} collective-permute-done((bf16[32,64,128]{2,1,0:T(8,128)(2,1)S(1)}, bf16[32,64,128]{2,1,0:T(8,128)(2,1)S(1)}, u32[]{:S(2)}, u32[]{:S(2)}) %collective-permute-start.19) | collective-permute-done | bytes 524320 | tf_op jit(solution)/shard_map/ppermute | solution.py:124
  143.6 5.2 %collective-permute-done.20 = bf16[16,64,128]{2,1,0:T(8,128)(2,1)S(1)} collective-permute-done((bf16[16,64,128]{2,1,0:T(8,128)(2,1)S(1)}, bf16[16,64,128]{2,1,0:T(8,128)(2,1)S(1)}, u32[]{:S(2)}, u32[]{:S(2)}) %collective-permute-start.20) | collective-permute-done | bytes 262176 | tf_op jit(solution)/shard_map/ppermute | solution.py:124
  150.2 1.6 collective-permute-start.16
  151.8 4.7 %collective-permute-done.21 = bf16[16,64,128]{2,1,0:T(8,128)(2,1)} collective-permute-done((bf16[16,64,128]{2,1,0:T(8,128)(2,1)}, bf16[16,64,128]{2,1,0:T(8,128)(2,1)}, u32[]{:S(2)}, u32[]{:S(2)}) %collective-permute-start.21) | collective-permute-done | bytes 262176 | tf_op jit(solution)/shard_map/ppermute | solution.py:124
  157.6 1.6 collective-permute-start.22
  161.2 1.5 collective-permute-start.26
  165.0 3.9 %collective-permute-done.22 = bf16[32,64,128]{2,1,0:T(8,128)(2,1)S(1)} collective-permute-done((bf16[32,64,128]{2,1,0:T(8,128)(2,1)S(1)}, bf16[32,64,128]{2,1,0:T(8,128)(2,1)S(1)}, u32[]{:S(2)}, u32[]{:S(2)}) %collective-permute-start.22) | collective-permute-done | bytes 524320 | tf_op jit(solution)/shard_map/ppermute | solution.py:124
  173.4 9.7 %collective-permute-done.24 = bf16[16,101,256]{2,0,1:T(8,128)(2,1)} collective-permute-done((bf16[16,101,256]{2,0,1:T(8,128)(2,1)}, bf16[16,101,256]{2,0,1:T(8,128)(2,1)}, u32[]{:S(2)}, u32[]{:S(2)}) %collective-permute-start.24) | collective-permute-done | bytes 827424 | tf_op jit(solution)/shard_map/ppermute | solution.py:179
  183.2 1.9 fusion.7
  185.1 1.9 collective-permute-start.25
  187.0 1.4 collective-permute-start.27
  191.3 2.3 pad_maximum_fusion.1.source_ref
  193.6 9.7 %collective-permute-done.25 = bf16[16,101,256]{2,0,1:T(8,128)(2,1)S(1)} collective-permute-done((bf16[16,101,256]{2,0,1:T(8,128)(2,1)S(1)}, bf16[16,101,256]{2,0,1:T(8,128)(2,1)S(1)}, u32[]{:S(2)}, u32[]{:S(2)}) %collective-permute-start.25) | collective-permute-done | bytes 827424 | tf_op jit(solution)/shard_map/ppermute | solution.py:179
  203.3 2.1 collective-permute-done.27
  205.4 19.8 %shard_map.112 = bf16[64,101,256]{2,1,0:T(8,128)(2,1)} custom-call(bf16[1,128]{1,0:T(2,128)(2,1)} %constant.86.clone.sign_ref, bf16[112,500]{1,0:T(8,128)(2,1)} %constant.87.clone.table_ref, bf16[256,64,128]{2,1,0:T(8,128)(2,1)} %pad_maximum_fusion.1.source_ref, bf16[250,128,256]{2,1,0:T(8,128)(2,1)} %bitcast.61), custom_call_target="tpu_custom_call" | custom-call | flops 3751936000 | bytes 23789568 | tf_op jit(solution)/shard_map/pallas_call | solution.py:98
  225.2 3.3 %constant_dynamic-slice_fusion.6 = (bf16[1,16,101,256]{3,2,1,0:T(8,128)(2,1)S(1)}, bf16[1,16,101,256]{3,2,1,0:T(8,128)(2,1)S(1)}, bf16[1,16,101,256]{3,2,1,0:T(8...) fusion(bf16[4,16,101,256]{3,2,1,0:T(8,128)(2,1)} %bitcast.62, ...), kind=kLoop, calls=%fused_computation.88 | loop fusion | bytes 11583516 | tf_op jit(solution)/shard_map/jit(dynamic_index_in_dim)/dynamic_slice | solution.py:169
  231.2 1.4 collective-permute-start.34
  232.6 15.2 %collective-permute-done.30 = bf16[16,101,256]{2,0,1:T(8,128)(2,1)S(1)} collective-permute-done((bf16[16,101,256]{2,0,1:T(8,128)(2,1)S(1)}, bf16[16,101,256]{2,0,1:T(8,128)(2,1)S(1)}, u32[]{:S(2)}, u32[]{:S(2)}) %collective-permute-start.30) | collective-permute-done | bytes 827424 | tf_op jit(solution)/shard_map/ppermute | solution.py:179
  248.2 2.7 collective-permute-start.31
  251.4 3.2 %collective-permute-start.29 = (bf16[16,101,256]{2,0,1:T(8,128)(2,1)S(1)}, bf16[16,101,256]{2,0,1:T(8,128)(2,1)S(1)}, u32[]{:S(2)}, u32[]{:S(2)}) collective-permute-start(bf16[16,101,256]{2,0,1:T(8,128)(2,1)S(1)} %get-tuple-element.45), channel_id=1, source_target_pairs={{3,2},{2,1},{1,0},{7,6},{6,5},{5,4},{11,10},{10,9},{9,8},{15,14},{... | collective-permute-start | bytes 2482184 | tf_op jit(solution)/shard_map/ppermute | solution.py:180
  254.6 2.7 collective-permute-start.28
  257.2 10.7 %collective-permute-done.34 = bf16[16,101,256]{2,0,1:T(8,128)(2,1)S(1)} collective-permute-done((bf16[16,101,256]{2,0,1:T(8,128)(2,1)S(1)}, bf16[16,101,256]{2,0,1:T(8,128)(2,1)S(1)}, u32[]{:S(2)}, u32[]{:S(2)}) %collective-permute-start.34) | collective-permute-done | bytes 827424 | tf_op jit(solution)/shard_map/ppermute | solution.py:180
  268.2 1.9 collective-permute-start.35
  271.7 2.7 collective-permute-start.32
  274.4 11.3 %collective-permute-done.29 = bf16[16,101,256]{2,0,1:T(8,128)(2,1)S(1)} collective-permute-done((bf16[16,101,256]{2,0,1:T(8,128)(2,1)S(1)}, bf16[16,101,256]{2,0,1:T(8,128)(2,1)S(1)}, u32[]{:S(2)}, u32[]{:S(2)}) %collective-permute-start.29) | collective-permute-done | bytes 827424 | tf_op jit(solution)/shard_map/ppermute | solution.py:180
  285.7 3.4 %collective-permute-done.28 = bf16[16,101,256]{2,0,1:T(8,128)(2,1)S(1)} collective-permute-done((bf16[16,101,256]{2,0,1:T(8,128)(2,1)S(1)}, bf16[16,101,256]{2,0,1:T(8,128)(2,1)S(1)}, u32[]{:S(2)}, u32[]{:S(2)}) %collective-permute-start.28) | collective-permute-done | bytes 827424 | tf_op jit(solution)/shard_map/ppermute | solution.py:179
  289.5 6.4 %collective-permute-done.35 = bf16[16,101,256]{2,0,1:T(8,128)(2,1)S(1)} collective-permute-done((bf16[16,101,256]{2,0,1:T(8,128)(2,1)S(1)}, bf16[16,101,256]{2,0,1:T(8,128)(2,1)S(1)}, u32[]{:S(2)}, u32[]{:S(2)}) %collective-permute-start.35) | collective-permute-done | bytes 827424 | tf_op jit(solution)/shard_map/ppermute | solution.py:180
  295.9 4.1 %collective-permute-done.32 = bf16[16,101,256]{2,0,1:T(8,128)(2,1)S(1)} collective-permute-done((bf16[16,101,256]{2,0,1:T(8,128)(2,1)S(1)}, bf16[16,101,256]{2,0,1:T(8,128)(2,1)S(1)}, u32[]{:S(2)}, u32[]{:S(2)}) %collective-permute-start.32) | collective-permute-done | bytes 827424 | tf_op jit(solution)/shard_map/ppermute | solution.py:179
  (129 shorter events, 39.1 us)
Async XLA Ops:
  2.1 16.6 %copy-start.12 = (s32[64]{0:T(128)S(1)}, s32[64]{0:T(128)}, u32[]{:S(2)}) copy-start(s32[64]{0:T(128)} %constant.90.clone) | copy-start | bytes 772
  2.1 16.6 %copy-start.13 = (pred[64]{0:T(512)(128)(4,1)S(1)}, pred[64]{0:T(512)(128)(4,1)}, u32[]{:S(2)}) copy-start(pred[64]{0:T(512)(128)(4,1)} %constant.96) | copy-start | bytes 196
  2.1 16.6 %copy-start.14 = (s32[64]{0:T(128)S(1)}, s32[64]{0:T(128)}, u32[]{:S(2)}) copy-start(s32[64]{0:T(128)} %constant.91.clone) | copy-start | bytes 772
  40.0 3.1 %collective-permute-start = (bf16[64,64,128]{2,1,0:T(8,128)(2,1)}, bf16[64,64,128]{2,1,0:T(8,128)(2,1)}, u32[]{:S(2)}, u32[]{:S(2)}) collective-permute-start(bf16[64,64,128]{2,1,0:T(8,128)(2,1)} %constant_dynamic-slice_fusion.20), channel_id=1, source_target_pairs={{0,4},{4,0},{8,12},{12,8},{16,20},{20,16},{24,28},{28,24},{1,5},{5... | collective-permute-start | bytes 3145736 | tf_op jit(solution)/shard_map/ppermute | solution.py:124
  40.1 4.9 %collective-permute-start.1 = (bf16[64,64,128]{2,1,0:T(8,128)(2,1)S(1)}, bf16[64,64,128]{2,1,0:T(8,128)(2,1)}, u32[]{:S(2)}, u32[]{:S(2)}) collective-permute-start(bf16[64,64,128]{2,1,0:T(8,128)(2,1)S(1)} %constant_dynamic-slice_fusion.19), channel_id=1, source_target_pairs={{0,4},{4,0},{8,12},{12,8},{16,20},{20,16},{24,28},{28,24},{1,5},{5... | collective-permute-start | bytes 3145736 | tf_op jit(solution)/shard_map/ppermute | solution.py:124
  46.7 19.8 %collective-permute-start.4 = (bf16[32,64,128]{2,1,0:T(8,128)(2,1)S(1)}, bf16[32,64,128]{2,1,0:T(8,128)(2,1)S(1)}, u32[]{:S(2)}, u32[]{:S(2)}) collective-permute-start(bf16[32,64,128]{2,1,0:T(8,128)(2,1)S(1)} %constant_dynamic-slice_fusion.16), channel_id=1, source_target_pairs={{0,8},{4,12},{8,0},{12,4},{16,24},{20,28},{24,16},{28,20},{1,9},{5... | collective-permute-start | bytes 1572872 | tf_op jit(solution)/shard_map/ppermute | solution.py:124
  48.3 19.0 %collective-permute-start.8 = (bf16[32,64,128]{2,1,0:T(8,128)(2,1)S(1)}, bf16[32,64,128]{2,1,0:T(8,128)(2,1)S(1)}, u32[]{:S(2)}, u32[]{:S(2)}) collective-permute-start(bf16[32,64,128]{2,1,0:T(8,128)(2,1)S(1)} %constant_dynamic-slice_fusion.14), channel_id=1, source_target_pairs={{0,16},{4,20},{8,24},{12,28},{16,0},{20,4},{24,8},{28,12},{1,17},{... | collective-permute-start | bytes 1572872 | tf_op jit(solution)/shard_map/ppermute | solution.py:124
  66.4 20.9 %collective-permute-start.2 = (bf16[64,64,128]{2,1,0:T(8,128)(2,1)S(1)}, bf16[64,64,128]{2,1,0:T(8,128)(2,1)S(1)}, u32[]{:S(2)}, u32[]{:S(2)}) collective-permute-start(bf16[64,64,128]{2,1,0:T(8,128)(2,1)S(1)} %constant_dynamic-slice_fusion.18), channel_id=1, source_target_pairs={{0,4},{4,0},{8,12},{12,8},{16,20},{20,16},{24,28},{28,24},{1,5},{5... | collective-permute-start | bytes 3145736 | tf_op jit(solution)/shard_map/ppermute | solution.py:124
  66.8 8.8 %collective-permute-start.5 = (bf16[16,64,128]{2,1,0:T(8,128)(2,1)S(1)}, bf16[16,64,128]{2,1,0:T(8,128)(2,1)S(1)}, u32[]{:S(2)}, u32[]{:S(2)}) collective-permute-start(bf16[16,64,128]{2,1,0:T(8,128)(2,1)S(1)} %constant_dynamic-slice_fusion.15), channel_id=1, source_target_pairs={{0,16},{4,20},{8,24},{12,28},{16,0},{20,4},{24,8},{28,12},{1,17},{... | collective-permute-start | bytes 786440 | tf_op jit(solution)/shard_map/ppermute | solution.py:124
  67.6 8.8 %collective-permute-start.9 = (bf16[16,64,128]{2,1,0:T(8,128)(2,1)S(1)}, bf16[16,64,128]{2,1,0:T(8,128)(2,1)S(1)}, u32[]{:S(2)}, u32[]{:S(2)}) collective-permute-start(bf16[16,64,128]{2,1,0:T(8,128)(2,1)S(1)} %constant_dynamic-slice_fusion.13), channel_id=1, source_target_pairs={{0,8},{4,12},{8,0},{12,4},{16,24},{20,28},{24,16},{28,20},{1,9},{5... | collective-permute-start | bytes 786440 | tf_op jit(solution)/shard_map/ppermute | solution.py:124
  75.6 8.0 %collective-permute-start.6 = (bf16[16,64,128]{2,1,0:T(8,128)(2,1)S(1)}, bf16[16,64,128]{2,1,0:T(8,128)(2,1)S(1)}, u32[]{:S(2)}, u32[]{:S(2)}) collective-permute-start(bf16[16,64,128]{2,1,0:T(8,128)(2,1)S(1)} %add_convert_fusion.11), channel_id=1, source_target_pairs={{0,16},{4,20},{8,24},{12,28},{16,0},{20,4},{24,8},{28,12},{1,17},{... | collective-permute-start | bytes 786440 | tf_op jit(solution)/shard_map/ppermute | solution.py:124
  76.3 11.5 %collective-permute-start.3 = (bf16[64,64,128]{2,1,0:T(8,128)(2,1)S(1)}, bf16[64,64,128]{2,1,0:T(8,128)(2,1)S(1)}, u32[]{:S(2)}, u32[]{:S(2)}) collective-permute-start(bf16[64,64,128]{2,1,0:T(8,128)(2,1)S(1)} %constant_dynamic-slice_fusion.17), channel_id=1, source_target_pairs={{0,4},{4,0},{8,12},{12,8},{16,20},{20,16},{24,28},{28,24},{1,5},{5... | collective-permute-start | bytes 3145736 | tf_op jit(solution)/shard_map/ppermute | solution.py:124
  76.5 8.8 %collective-permute-start.10 = (bf16[16,64,128]{2,1,0:T(8,128)(2,1)S(1)}, bf16[16,64,128]{2,1,0:T(8,128)(2,1)S(1)}, u32[]{:S(2)}, u32[]{:S(2)}) collective-permute-start(bf16[16,64,128]{2,1,0:T(8,128)(2,1)S(1)} %add_convert_fusion.10), channel_id=1, source_target_pairs={{0,8},{4,12},{8,0},{12,4},{16,24},{20,28},{24,16},{28,20},{1,9},{5... | collective-permute-start | bytes 786440 | tf_op jit(solution)/shard_map/ppermute | solution.py:124
  83.7 12.7 %collective-permute-start.7 = (bf16[32,64,128]{2,1,0:T(8,128)(2,1)S(1)}, bf16[32,64,128]{2,1,0:T(8,128)(2,1)S(1)}, u32[]{:S(2)}, u32[]{:S(2)}) collective-permute-start(bf16[32,64,128]{2,1,0:T(8,128)(2,1)S(1)} %pad_maximum_fusion.7), channel_id=1, source_target_pairs={{0,8},{4,12},{8,0},{12,4},{16,24},{20,28},{24,16},{28,20},{1,9},{5... | collective-permute-start | bytes 1572872 | tf_op jit(solution)/shard_map/ppermute | solution.py:124
  85.3 13.6 %collective-permute-start.11 = (bf16[32,64,128]{2,1,0:T(8,128)(2,1)S(1)}, bf16[32,64,128]{2,1,0:T(8,128)(2,1)S(1)}, u32[]{:S(2)}, u32[]{:S(2)}) collective-permute-start(bf16[32,64,128]{2,1,0:T(8,128)(2,1)S(1)} %pad_maximum_fusion.8), channel_id=1, source_target_pairs={{0,16},{4,20},{8,24},{12,28},{16,0},{20,4},{24,8},{28,12},{1,17},{... | collective-permute-start | bytes 1572872 | tf_op jit(solution)/shard_map/ppermute | solution.py:124
  99.1 2.9 collective-permute-start.13
  99.2 4.3 %collective-permute-start.12 = (bf16[64,64,128]{2,1,0:T(8,128)(2,1)S(1)}, bf16[64,64,128]{2,1,0:T(8,128)(2,1)}, u32[]{:S(2)}, u32[]{:S(2)}) collective-permute-start(bf16[64,64,128]{2,1,0:T(8,128)(2,1)S(1)} %pad_maximum_fusion.3), channel_id=1, source_target_pairs={{0,4},{4,0},{8,12},{12,8},{16,20},{20,16},{24,28},{28,24},{1,5},{5... | collective-permute-start | bytes 3145736 | tf_op jit(solution)/shard_map/ppermute | solution.py:124
  107.1 19.8 %copy-start.11 = (bf16[64,64,128]{2,1,0:T(8,128)(2,1)S(1)}, bf16[64,64,128]{2,1,0:T(8,128)(2,1)}, u32[]{:S(2)}) copy-start(bf16[64,64,128]{2,1,0:T(8,128)(2,1)} %add_convert_fusion) | copy-start | bytes 3145732
  127.0 14.0 %collective-permute-start.19 = (bf16[32,64,128]{2,1,0:T(8,128)(2,1)S(1)}, bf16[32,64,128]{2,1,0:T(8,128)(2,1)S(1)}, u32[]{:S(2)}, u32[]{:S(2)}) collective-permute-start(bf16[32,64,128]{2,1,0:T(8,128)(2,1)S(1)} %constant_dynamic-slice_fusion.10), channel_id=1, source_target_pairs={{0,16},{4,20},{8,24},{12,28},{16,0},{20,4},{24,8},{28,12},{1,17},{... | collective-permute-start | bytes 1572872 | tf_op jit(solution)/shard_map/ppermute | solution.py:124
  128.6 13.7 %collective-permute-start.14 = (bf16[32,64,128]{2,1,0:T(8,128)(2,1)S(1)}, bf16[32,64,128]{2,1,0:T(8,128)(2,1)S(1)}, u32[]{:S(2)}, u32[]{:S(2)}) collective-permute-start(bf16[32,64,128]{2,1,0:T(8,128)(2,1)S(1)} %constant_dynamic-slice_fusion.12), channel_id=1, source_target_pairs={{0,8},{4,12},{8,0},{12,4},{16,24},{20,28},{24,16},{28,20},{1,9},{5... | collective-permute-start | bytes 1572872 | tf_op jit(solution)/shard_map/ppermute | solution.py:124
  141.2 7.6 %collective-permute-start.20 = (bf16[16,64,128]{2,1,0:T(8,128)(2,1)S(1)}, bf16[16,64,128]{2,1,0:T(8,128)(2,1)S(1)}, u32[]{:S(2)}, u32[]{:S(2)}) collective-permute-start(bf16[16,64,128]{2,1,0:T(8,128)(2,1)S(1)} %constant_dynamic-slice_fusion.9), channel_id=1, source_target_pairs={{0,8},{4,12},{8,0},{12,4},{16,24},{20,28},{24,16},{28,20},{1,9},{5... | collective-permute-start | bytes 786440 | tf_op jit(solution)/shard_map/ppermute | solution.py:124
  142.6 7.5 %collective-permute-start.15 = (bf16[16,64,128]{2,1,0:T(8,128)(2,1)S(1)}, bf16[16,64,128]{2,1,0:T(8,128)(2,1)S(1)}, u32[]{:S(2)}, u32[]{:S(2)}) collective-permute-start(bf16[16,64,128]{2,1,0:T(8,128)(2,1)S(1)} %constant_dynamic-slice_fusion.11), channel_id=1, source_target_pairs={{0,16},{4,20},{8,24},{12,28},{16,0},{20,4},{24,8},{28,12},{1,17},{... | collective-permute-start | bytes 786440 | tf_op jit(solution)/shard_map/ppermute | solution.py:124
  149.6 6.9 %collective-permute-start.21 = (bf16[16,64,128]{2,1,0:T(8,128)(2,1)}, bf16[16,64,128]{2,1,0:T(8,128)(2,1)}, u32[]{:S(2)}, u32[]{:S(2)}) collective-permute-start(bf16[16,64,128]{2,1,0:T(8,128)(2,1)} %add_convert_fusion.8), channel_id=1, source_target_pairs={{0,8},{4,12},{8,0},{12,4},{16,24},{20,28},{24,16},{28,20},{1,9},{5... | collective-permute-start | bytes 786440 | tf_op jit(solution)/shard_map/ppermute | solution.py:124
  150.2 9.7 %copy-start = (bf16[64,101,256]{2,1,0:T(8,128)(2,1)S(1)}, bf16[64,101,256]{2,1,0:T(8,128)(2,1)}, u32[]{:S(2)}) copy-start(bf16[64,101,256]{2,1,0:T(8,128)(2,1)} %shard_map.111) | copy-start | bytes 9928708
  150.2 9.0 %collective-permute-start.16 = (bf16[16,64,128]{2,1,0:T(8,128)(2,1)S(1)}, bf16[16,64,128]{2,1,0:T(8,128)(2,1)S(1)}, u32[]{:S(2)}, u32[]{:S(2)}) collective-permute-start(bf16[16,64,128]{2,1,0:T(8,128)(2,1)S(1)} %add_convert_fusion.9), channel_id=1, source_target_pairs={{0,16},{4,20},{8,24},{12,28},{16,0},{20,4},{24,8},{28,12},{1,17},{... | collective-permute-start | bytes 786440 | tf_op jit(solution)/shard_map/ppermute | solution.py:124
  157.6 11.4 %collective-permute-start.22 = (bf16[32,64,128]{2,1,0:T(8,128)(2,1)S(1)}, bf16[32,64,128]{2,1,0:T(8,128)(2,1)S(1)}, u32[]{:S(2)}, u32[]{:S(2)}) collective-permute-start(bf16[32,64,128]{2,1,0:T(8,128)(2,1)S(1)} %pad_maximum_fusion.10), channel_id=1, source_target_pairs={{0,16},{4,20},{8,24},{12,28},{16,0},{20,4},{24,8},{28,12},{1,17},{... | collective-permute-start | bytes 1572872 | tf_op jit(solution)/shard_map/ppermute | solution.py:124
  159.3 11.1 %collective-permute-start.17 = (bf16[32,64,128]{2,1,0:T(8,128)(2,1)S(1)}, bf16[32,64,128]{2,1,0:T(8,128)(2,1)S(1)}, u32[]{:S(2)}, u32[]{:S(2)}) collective-permute-start(bf16[32,64,128]{2,1,0:T(8,128)(2,1)S(1)} %pad_maximum_fusion.9), channel_id=1, source_target_pairs={{0,8},{4,12},{8,0},{12,4},{16,24},{20,28},{24,16},{28,20},{1,9},{5... | collective-permute-start | bytes 1572872 | tf_op jit(solution)/shard_map/ppermute | solution.py:124
  161.2 12.3 %collective-permute-start.26 = (bf16[16,101,256]{2,0,1:T(8,128)(2,1)}, bf16[16,101,256]{2,0,1:T(8,128)(2,1)}, u32[]{:S(2)}, u32[]{:S(2)}) collective-permute-start(bf16[16,101,256]{2,0,1:T(8,128)(2,1)} %bitcast.56), channel_id=1, source_target_pairs={{3,2},{7,6},{11,10},{15,14},{19,18},{23,22},{27,26},{31,30}} | collective-permute-start | bytes 2482184 | tf_op jit(solution)/shard_map/ppermute | solution.py:180
  163.8 19.4 %collective-permute-start.24 = (bf16[16,101,256]{2,0,1:T(8,128)(2,1)}, bf16[16,101,256]{2,0,1:T(8,128)(2,1)}, u32[]{:S(2)}, u32[]{:S(2)}) collective-permute-start(bf16[16,101,256]{2,0,1:T(8,128)(2,1)} %bitcast.57), channel_id=1, source_target_pairs={{0,1},{4,5},{8,9},{12,13},{16,17},{20,21},{24,25},{28,29}} | collective-permute-start | bytes 2482184 | tf_op jit(solution)/shard_map/ppermute | solution.py:179
  170.2 18.3 %collective-permute-start.23 = (bf16[64,64,128]{2,1,0:T(8,128)(2,1)}, bf16[64,64,128]{2,1,0:T(8,128)(2,1)}, u32[]{:S(2)}, u32[]{:S(2)}) collective-permute-start(bf16[64,64,128]{2,1,0:T(8,128)(2,1)} %pad_maximum_fusion.6), channel_id=1, source_target_pairs={{0,4},{4,0},{8,12},{12,8},{16,20},{20,16},{24,28},{28,24},{1,5},{5... | collective-permute-start | bytes 3145736 | tf_op jit(solution)/shard_map/ppermute | solution.py:124
  170.5 1.9 copy-start.9
  172.4 17.5 %collective-permute-start.18 = (bf16[64,64,128]{2,1,0:T(8,128)(2,1)}, bf16[64,64,128]{2,1,0:T(8,128)(2,1)}, u32[]{:S(2)}, u32[]{:S(2)}) collective-permute-start(bf16[64,64,128]{2,1,0:T(8,128)(2,1)} %pad_maximum_fusion.5), channel_id=1, source_target_pairs={{0,4},{4,0},{8,12},{12,8},{16,20},{20,16},{24,28},{28,24},{1,5},{5... | collective-permute-start | bytes 3145736 | tf_op jit(solution)/shard_map/ppermute | solution.py:124
  173.4 11.7 %copy-start.1 = (bf16[4,16,101,256]{3,1,2,0:T(8,128)(2,1)}, bf16[4,16,101,256]{3,1,2,0:T(8,128)(2,1)S(1)}, u32[]{:S(2)}) copy-start(bf16[4,16,101,256]{3,1,2,0:T(8,128)(2,1)S(1)} %copy.13) | copy-start | bytes 9928708
  173.4 15.1 %copy-start.4 = (bf16[32,64,128]{2,1,0:T(8,128)(2,1)S(1)}, bf16[32,64,128]{2,1,0:T(8,128)(2,1)}, u32[]{:S(2)}) copy-start(bf16[32,64,128]{2,1,0:T(8,128)(2,1)} %copy-done.3) | copy-start | bytes 1572868
  173.4 15.1 %copy-start.6 = (bf16[32,64,128]{2,1,0:T(8,128)(2,1)S(1)}, bf16[32,64,128]{2,1,0:T(8,128)(2,1)}, u32[]{:S(2)}) copy-start(bf16[32,64,128]{2,1,0:T(8,128)(2,1)} %copy-done.5) | copy-start | bytes 1572868
  185.1 18.2 %collective-permute-start.25 = (bf16[16,101,256]{2,0,1:T(8,128)(2,1)S(1)}, bf16[16,101,256]{2,0,1:T(8,128)(2,1)S(1)}, u32[]{:S(2)}, u32[]{:S(2)}) collective-permute-start(bf16[16,101,256]{2,0,1:T(8,128)(2,1)S(1)} %get-tuple-element.47), channel_id=1, source_target_pairs={{0,1},{1,2},{4,5},{5,6},{8,9},{9,10},{12,13},{13,14},{16,17},{17,1... | collective-permute-start | bytes 2482184 | tf_op jit(solution)/shard_map/ppermute | solution.py:179
  187.0 2.9 copy-start.8
  187.0 2.9 copy-start.10
  187.0 18.3 %collective-permute-start.27 = (bf16[16,101,256]{2,0,1:T(8,128)(2,1)S(1)}, bf16[16,101,256]{2,0,1:T(8,128)(2,1)S(1)}, u32[]{:S(2)}, u32[]{:S(2)}) collective-permute-start(bf16[16,101,256]{2,0,1:T(8,128)(2,1)S(1)} %get-tuple-element.46), channel_id=1, source_target_pairs={{3,2},{2,1},{7,6},{6,5},{11,10},{10,9},{15,14},{14,13},{19,18},{18... | collective-permute-start | bytes 2482184 | tf_op jit(solution)/shard_map/ppermute | solution.py:180
  228.7 2.2 collective-permute-start.33
  229.6 18.3 %collective-permute-start.30 = (bf16[16,101,256]{2,0,1:T(8,128)(2,1)S(1)}, bf16[16,101,256]{2,0,1:T(8,128)(2,1)S(1)}, u32[]{:S(2)}, u32[]{:S(2)}) collective-permute-start(bf16[16,101,256]{2,0,1:T(8,128)(2,1)S(1)} %bitcast.66), channel_id=1, source_target_pairs={{0,1},{4,5},{8,9},{12,13},{16,17},{20,21},{24,25},{28,29}} | collective-permute-start | bytes 2482184 | tf_op jit(solution)/shard_map/ppermute | solution.py:179
  230.9 20.0 %copy-start.2 = (bf16[4,16,101,256]{3,1,2,0:T(8,128)(2,1)S(1)}, bf16[4,16,101,256]{3,1,2,0:T(8,128)(2,1)}, u32[]{:S(2)}) copy-start(bf16[4,16,101,256]{3,1,2,0:T(8,128)(2,1)} %copy-done.1) | copy-start | bytes 9928708
  231.2 36.8 %collective-permute-start.34 = (bf16[16,101,256]{2,0,1:T(8,128)(2,1)S(1)}, bf16[16,101,256]{2,0,1:T(8,128)(2,1)S(1)}, u32[]{:S(2)}, u32[]{:S(2)}) collective-permute-start(bf16[16,101,256]{2,0,1:T(8,128)(2,1)S(1)} %fusion), channel_id=1, source_target_pairs={{3,2},{2,1},{7,6},{6,5},{11,10},{10,9},{15,14},{14,13},{19,18},{18... | collective-permute-start | bytes 2482184 | tf_op jit(solution)/shard_map/ppermute | solution.py:180
  248.2 23.3 %collective-permute-start.31 = (bf16[16,101,256]{2,0,1:T(8,128)(2,1)S(1)}, bf16[16,101,256]{2,0,1:T(8,128)(2,1)S(1)}, u32[]{:S(2)}, u32[]{:S(2)}) collective-permute-start(bf16[16,101,256]{2,0,1:T(8,128)(2,1)S(1)} %fusion.2), channel_id=1, source_target_pairs={{0,1},{1,2},{4,5},{5,6},{8,9},{9,10},{12,13},{13,14},{16,17},{17,1... | collective-permute-start | bytes 2482184 | tf_op jit(solution)/shard_map/ppermute | solution.py:179
  251.4 34.3 %collective-permute-start.29 = (bf16[16,101,256]{2,0,1:T(8,128)(2,1)S(1)}, bf16[16,101,256]{2,0,1:T(8,128)(2,1)S(1)}, u32[]{:S(2)}, u32[]{:S(2)}) collective-permute-start(bf16[16,101,256]{2,0,1:T(8,128)(2,1)S(1)} %get-tuple-element.45), channel_id=1, source_target_pairs={{3,2},{2,1},{1,0},{7,6},{6,5},{5,4},{11,10},{10,9},{9,8},{15,14},{... | collective-permute-start | bytes 2482184 | tf_op jit(solution)/shard_map/ppermute | solution.py:180
  254.6 34.6 %collective-permute-start.28 = (bf16[16,101,256]{2,0,1:T(8,128)(2,1)S(1)}, bf16[16,101,256]{2,0,1:T(8,128)(2,1)S(1)}, u32[]{:S(2)}, u32[]{:S(2)}) collective-permute-start(bf16[16,101,256]{2,0,1:T(8,128)(2,1)S(1)} %get-tuple-element.44), channel_id=1, source_target_pairs={{0,1},{1,2},{2,3},{4,5},{5,6},{6,7},{8,9},{9,10},{10,11},{12,13},{... | collective-permute-start | bytes 2482184 | tf_op jit(solution)/shard_map/ppermute | solution.py:179
  268.2 27.7 %collective-permute-start.35 = (bf16[16,101,256]{2,0,1:T(8,128)(2,1)S(1)}, bf16[16,101,256]{2,0,1:T(8,128)(2,1)S(1)}, u32[]{:S(2)}, u32[]{:S(2)}) collective-permute-start(bf16[16,101,256]{2,0,1:T(8,128)(2,1)S(1)} %fusion.1), channel_id=1, source_target_pairs={{3,2},{2,1},{1,0},{7,6},{6,5},{5,4},{11,10},{10,9},{9,8},{15,14},{... | collective-permute-start | bytes 2482184 | tf_op jit(solution)/shard_map/ppermute | solution.py:180
  271.7 28.4 %collective-permute-start.32 = (bf16[16,101,256]{2,0,1:T(8,128)(2,1)S(1)}, bf16[16,101,256]{2,0,1:T(8,128)(2,1)S(1)}, u32[]{:S(2)}, u32[]{:S(2)}) collective-permute-start(bf16[16,101,256]{2,0,1:T(8,128)(2,1)S(1)} %fusion.3), channel_id=1, source_target_pairs={{0,1},{1,2},{2,3},{4,5},{5,6},{6,7},{8,9},{9,10},{10,11},{12,13},{... | collective-permute-start | bytes 2482184 | tf_op jit(solution)/shard_map/ppermute | solution.py:179
  (3 other events, 3.7 us)
